TPU v7x, 256 devices: a whole 4x4x8 slice. The times are simulated.
256 devices in a mesh: grp: 32 (over z, x), box: 8 (over y, core).
Axes of the slice: x: 4, y: 4, z: 8, core: 2. Of those that a mesh axis runs over, the one named last changes fastest.
Arguments:
- source_term: float32 [53, 32, 16, 256], P(None, 'grp', 'box'), may hold values from -24 to 24
- diffusion: float32 [53], replicated, may hold values from 0.1 to 2
- stoich: float32 [53, 325], replicated, may hold values from -0.3125 to 0.3125
- orders: float32 [325, 53], replicated, may hold values from -0.875 to 0.875
- rates: float32 [325, 32, 16, 256], P(None, 'grp', 'box'), may hold values from 0.1 to 1
- precond: bfloat16 [53, 53, 32, 16, 256], P(None, None, 'grp', 'box'), may hold values from -1 to 1
- coarse_field: float32 [53, 32, 2048], P(None, 'grp', 'box'), may hold values from -6 to 6
- neighbours: int32 [32, 4], replicated, may hold values from -1 to 31, as said below
- ghost_list: int32 [32, 8, 160], P(None, 'box'), may hold values from -1 to 8191, as said below
- average_list: int32 [32, 8], P(None, 'box'), may hold values from 0 to 127, as said below
Outputs:
- correction: float32 [53, 32, 16, 256], P(None, 'grp', 'box')
- coarse_update: float32 [53, 32, 2048], P(None, 'grp', 'box')
Inputs may be any that keep to these rules, and one draw needn't show every extreme that they name: Column g sits at one position of a grid 4 columns wide and 8 rows tall, each position taken once; neighbours[g, 0] and neighbours[g, 1] are the columns before and after it in its grid row, neighbours[g, 2] and neighbours[g, 3] the ones in the grid rows below and above, -1 at the grid's edge. The relation is symmetric: neighbours[neighbours[g, f], f xor 1] = g. `ghost_list`: an entry is -1 exactly where its face meets another fine sub-box: the lower x face for b > 0, the upper x face for b < 7, side face f where neighbours[g, f] >= 0. Every other entry is o * 256 + c, coarse cell c of the patch of column o at the same box index. `average_list`: entry o * 4 + j names block j of the patch of column o at the same box index; at each box index the 32 entries are distinct.
All inputs are finite; a program needn't handle non-finite values.
Results may differ from a plain program's by a relative error of at most 0.0007.
Values sent between devices are 32-bit elements; how exact they have to be, the bound alone decides.
No kernel may reach another device: no remote copies, remote signals or barrier semaphores. Data moves between devices by JAX's collectives and lax.ppermute only.
A program may use at most 64 MiB of HBM per device.

v0:
```python
import jax
import jax.numpy as jnp
from jax import lax
from jax.sharding import PartitionSpec as P

FS = 16
ITERS = 4


EXACT = lax.Precision.HIGHEST


def extended_2(cells, sides, width):
    for axis, dim in sides:
        count = lax.axis_size(axis)
        ends = count - 1
        head = lax.slice_in_dim(cells, 0, width, axis=dim)
        tail = lax.slice_in_dim(cells, cells.shape[dim] - width, cells.shape[dim], axis=dim)
        cells = jnp.concatenate(
            [
                lax.ppermute(tail, axis, [(i, (i + 1) % count) for i in range(ends)]),
                cells,
                lax.ppermute(head, axis, [((i + 1) % count, i) for i in range(ends)]),
            ],
            axis=dim,
        )
    return cells


def face_planes(core, side):
    return (core[..., :side], core[..., -side:], core[..., 0::side], core[..., side - 1 :: side])


def neighbour_sum(core, x_lower, x_upper, sides, side):
    padded = jnp.concatenate([x_lower[..., None, :], core, x_upper[..., None, :]], axis=-2)
    total = padded[..., :-2, :] + padded[..., 2:, :]
    total = total + jnp.concatenate([core[..., side:], sides[1]], axis=-1)
    total = total + jnp.concatenate([sides[0], core[..., :-side]], axis=-1)
    column = jnp.arange(core.shape[-1]) % side
    blank = jnp.zeros(core.shape[:-1] + (1,), core.dtype)
    ahead = jnp.concatenate([core[..., 1:], blank], axis=-1)
    behind = jnp.concatenate([blank, core[..., :-1]], axis=-1)
    total = total + jnp.where(column == side - 1, jnp.repeat(sides[3], side, axis=-1), ahead)
    total = total + jnp.where(column == 0, jnp.repeat(sides[2], side, axis=-1), behind)
    return total


def least_squares(columns, beta):
    count = len(columns)
    target = [beta] + [jnp.zeros_like(beta)] * count
    rotations = []
    upper = []
    for j in range(count):
        entries = list(columns[j])
        for i in range(j):
            cosine_part, sine_part = rotations[i]
            first = cosine_part * entries[i] + sine_part * entries[i + 1]
            second = cosine_part * entries[i + 1] - sine_part * entries[i]
            entries[i] = first
            entries[i + 1] = second
        radius = jnp.sqrt(entries[j] * entries[j] + entries[j + 1] * entries[j + 1])
        cosine_part = entries[j] / radius
        sine_part = entries[j + 1] / radius
        rotations.append((cosine_part, sine_part))
        entries[j] = radius
        target[j + 1] = -sine_part * target[j]
        target[j] = cosine_part * target[j]
        upper.append(entries[: j + 1])
    result = [None] * count
    for j in reversed(range(count)):
        running = target[j]
        for k in range(j + 1, count):
            running = running - upper[k][j] * result[k]
        result[j] = running / upper[j][j]
    return result


def on_device(
    source_term,
    diffusion,
    stoich,
    orders,
    rates,
    precond,
    coarse_field,
    neighbours,
    ghost_list,
    average_list,
):
    species = source_term.shape[0]
    slab = source_term.shape[2]
    face = source_term.shape[3]
    side = FS
    half = side // 2
    group_index = lax.axis_index("grp")
    field_shape = (species, slab, face)
    diffuse = diffusion[:, None, None]
    inverse = precond.reshape(species, species, slab, face)
    reaction = rates.reshape(rates.shape[0], slab * face)
    links = lax.dynamic_index_in_dim(neighbours, group_index, 0, keepdims=False)
    linked = links >= 0
    partner = jnp.maximum(links, 0)

    def global_norm(field):
        return jnp.sqrt(lax.psum(jnp.sum(field * field), ("grp", "box")))

    own_list = lax.dynamic_index_in_dim(ghost_list[:, 0, :], group_index, 0, keepdims=False)
    patch = coarse_field[:, 0, :]
    patch_size = patch.shape[1]
    every_patch = lax.all_gather(coarse_field, "grp", axis=1, tiled=True).reshape(species, -1)
    values = jnp.take(every_patch, jnp.maximum(own_list, 0), axis=1)
    values = jnp.where(own_list[None, :] >= 0, values, 0.0)
    face_ids = jnp.arange(face)
    x_index = face_ids // side // 2 * half + face_ids % side // 2
    side_ids = jnp.arange(slab * side)
    side_index = (side_ids // side // 2 * half + side_ids % side // 2).reshape(slab, side)
    x_slots = half * half
    side_slots = slab // 2 * half
    lower_x = values[:, :x_slots][:, x_index]
    upper_x = values[:, x_slots : 2 * x_slots][:, x_index]
    sides = tuple(
        (
            values[:, 2 * x_slots + f * side_slots : 2 * x_slots + (f + 1) * side_slots][
                :, side_index
            ]
            for f in range(4)
        )
    )
    boundary = diffuse * neighbour_sum(
        jnp.zeros(field_shape, jnp.float32), lower_x, upper_x, sides, side
    )
    right = source_term.reshape(field_shape) + boundary
    beta = global_norm(right)
    basis = [right / beta]
    directions = []
    columns = []
    for j in range(ITERS):
        direction = jnp.einsum(
            "ijxc,jxc->ixc", inverse, basis[j], preferred_element_type=jnp.float32, precision=EXACT
        )
        directions.append(direction)
        extended = extended_2(direction, (("box", 1),), 1)
        planes = jnp.stack(face_planes(direction, side))
        every = lax.all_gather(planes[None], "grp", axis=0, tiled=True)
        picked = every[partner, jnp.array([1, 0, 3, 2])]
        picked = jnp.where(linked[:, None, None, None], picked, 0.0)
        beside_all = neighbour_sum(
            direction,
            extended[:, 0],
            extended[:, -1],
            (picked[0], picked[1], picked[2], picked[3]),
            side,
        )
        progress = jnp.dot(orders, direction.reshape(species, -1), precision=EXACT)
        chemistry = jnp.dot(stoich, reaction * progress, precision=EXACT).reshape(field_shape)
        image = direction + diffuse * (6.0 * direction - beside_all) - chemistry
        local = jnp.stack([jnp.sum(basis[i] * image) for i in range(j + 1)])
        summed = lax.psum(local, ("grp", "box"))
        heights = [summed[i] for i in range(j + 1)]
        for i in range(j + 1):
            image = image - heights[i] * basis[i]
        length = global_norm(image)
        columns.append(heights + [length])
        if j + 1 < ITERS:
            basis.append(image / length)
    weights = least_squares(columns, beta)
    correction = sum((weights[j] * directions[j] for j in range(ITERS)))
    cells = slab * face
    cell_ids = jnp.arange(cells)
    plane = cell_ids // face
    within = cell_ids % face
    block = slab // 2 * half * half
    target = plane // 2 * (half * half) + within // side // 2 * half + within % side // 2
    averaging = (target[:, None] == jnp.arange(block)[None, :]).astype(jnp.float32)
    averaged = jnp.dot(correction.reshape(species, cells), averaging, precision=EXACT) * 0.125
    every_average = lax.all_gather(averaged[:, None, :], "grp", axis=1, tiled=True)
    slot_count = patch_size // block
    wanted = group_index * slot_count + jnp.arange(slot_count)
    select = (average_list[None, :, 0] == wanted[:, None]).astype(jnp.float32)
    blocks = jnp.einsum("jp,spk->sjk", select, every_average, precision=EXACT)
    covered = jnp.sum(select, axis=1) > 0
    updated = jnp.where(covered[None, :, None], blocks, patch.reshape(species, slot_count, block))
    return (correction.reshape(species, 1, slab, face), updated.reshape(species, 1, patch_size))


def solution(mesh):
    placed = (
        P(None, "grp", "box", None),
        P(),
        P(),
        P(),
        P(None, "grp", "box", None),
        P(None, None, "grp", "box", None),
        P(None, "grp", "box"),
        P(),
        P(None, "box", None),
        P(None, "box"),
    )
    return jax.shard_map(
        on_device,
        mesh=mesh,
        in_specs=placed,
        out_specs=(P(None, "grp", "box", None), P(None, "grp", "box")),
        check_vma=False,
    )
```

profile of v0, /device:TPU:2, one launch (start us, length us, event | category | flops | bytes accessed | tf_op | source)
XLA Modules:
  0.0 1165.8 jit_solution(8963964011460617496)
XLA Ops:
  7.3 1.5 copy.150
  8.9 1.0 copy.149
  10.0 11.9 %copy.160 = bf16[53,53,2,256]{0,1,3,2:T(8,128)(2,1)} copy(bf16[53,53,2,256]{3,2,1,0:T(2,128)(2,1)} %bitcast.310) | data formatting | bytes 5752832 | tf_op jit(solution)/shard_map/reshape | solution.py:98
  22.2 0.7 reduce.4
  24.9 65.7 %all-gather.8.cloned.1.call-done = f32[53,32,256]{2,0,1:T(8,128)} async-done(((f32[53,1,256]{2,0,1:T(8,128)}), f32[53,32,256]{2,0,1:T(8,128)}) %all-gather.8.cloned.1.call-update) | async-done | bytes 1736720 | tf_op jit(solution)/shard_map/all_gather | solution.py:110
  90.6 3.9 copy.151
  94.6 2.9 gather_fusion
  99.9 0.7 gather_fusion.1
  100.6 0.7 gather_fusion.2
  101.3 0.8 multiply_reduce_fusion.14
  102.1 74.1 %psum.63 = f32[]{:T(128)} all-reduce(f32[]{:T(128)} %get-tuple-element.30), channel_id=1, replica_groups=mesh['grp'=32,'box'=8] {'grp','box'}, use_global_device_ids=true, to_apply=%region_1.2 | all-reduce | flops 1 | bytes 8 | tf_op jit(solution)/shard_map/psum | solution.py:105
  177.0 8.5 fusion.96
  185.5 0.8 fusion.90
  186.3 0.8 fusion.89
  187.2 0.7 fusion.88
  187.9 50.0 %all-gather = f32[128,53,2,16]{1,3,2,0:T(8,128)S(1)} all-gather(f32[4,53,2,16]{1,3,2,0:T(8,128)S(1)} %pad_maximum_fusion.8), channel_id=2, replica_groups=mesh['grp'=32,'box'=8] {'grp'}, dimensions={0}, use_global_device_ids=true | all-gather | bytes 895488 | tf_op jit(solution)/shard_map/all_gather | solution.py:144
  237.9 1.9 collective-permute-start
  239.8 1.3 collective-permute-start.1
  241.8 0.7 fusion.3
  243.4 2.1 multiply_reduce_fusion.13
  245.5 77.4 %psum.64 = f32[]{:T(128)} all-reduce(f32[]{:T(128)} %get-tuple-element.28), channel_id=1, replica_groups=mesh['grp'=32,'box'=8] {'grp','box'}, use_global_device_ids=true, to_apply=%region_3.4 | all-reduce | flops 1 | bytes 8 | tf_op jit(solution)/shard_map/psum | solution.py:158
  322.9 1.4 multiply_reduce_fusion.12
  324.3 1.6 reshape_squeeze.3
  325.9 74.2 %psum.65 = f32[]{:T(128)} all-reduce(f32[]{:T(128)} %multiply_reduce_fusion.12), channel_id=1, replica_groups=mesh['grp'=32,'box'=8] {'grp','box'}, use_global_device_ids=true, to_apply=%region_5.6 | all-reduce | flops 1 | bytes 8 | tf_op jit(solution)/shard_map/psum | solution.py:105
  401.6 8.4 fusion.97
  410.9 54.3 %all-gather.1 = f32[128,53,2,16]{1,3,2,0:T(8,128)} all-gather(f32[4,53,2,16]{1,3,2,0:T(8,128)S(1)} %pad_maximum_fusion.9), channel_id=3, replica_groups=mesh['grp'=32,'box'=8] {'grp'}, dimensions={0}, use_global_device_ids=true | all-gather | bytes 895488 | tf_op jit(solution)/shard_map/all_gather | solution.py:144
  465.2 2.1 gather_fusion.8
  467.4 0.7 fusion.2
  468.8 1.9 collective-permute-start.2
  470.7 1.3 collective-permute-start.3
  474.4 1.9 multiply_reduce_fusion.11
  476.3 1.4 pad_maximum_fusion.12
  477.7 77.4 %psum.66 = f32[2]{0:T(128)S(1)} all-reduce(f32[2]{0:T(128)S(1)} %pad_maximum_fusion.12), channel_id=1, replica_groups=mesh['grp'=32,'box'=8] {'grp','box'}, use_global_device_ids=true, to_apply=%region_8.9 | all-reduce | flops 2 | bytes 16 | tf_op jit(solution)/shard_map/psum | solution.py:158
  555.8 2.0 multiply_reduce_fusion.9
  557.8 73.9 %psum.67 = f32[]{:T(128)} all-reduce(f32[]{:T(128)} %get-tuple-element.25), channel_id=1, replica_groups=mesh['grp'=32,'box'=8] {'grp','box'}, use_global_device_ids=true, to_apply=%region_10.11 | all-reduce | flops 1 | bytes 8 | tf_op jit(solution)/shard_map/psum | solution.py:105
  632.4 8.4 fusion.98
  640.9 0.8 fusion.83
  642.5 54.6 %all-gather.2 = f32[128,53,2,16]{1,3,2,0:T(8,128)} all-gather(f32[4,53,2,16]{1,3,2,0:T(8,128)S(1)} %pad_maximum_fusion.10), channel_id=4, replica_groups=mesh['grp'=32,'box'=8] {'grp'}, dimensions={0}, use_global_device_ids=true | all-gather | bytes 895488 | tf_op jit(solution)/shard_map/all_gather | solution.py:144
  697.1 2.1 gather_fusion.9
  699.3 0.7 fusion.1
  700.7 1.9 collective-permute-start.4
  702.7 1.3 collective-permute-start.5
  706.8 2.3 multiply_reduce_fusion.8
  709.1 2.0 pad_maximum_fusion.13
  711.1 76.8 %psum.68 = f32[3]{0:T(128)S(1)} all-reduce(f32[3]{0:T(128)S(1)} %pad_maximum_fusion.13), channel_id=1, replica_groups=mesh['grp'=32,'box'=8] {'grp','box'}, use_global_device_ids=true, to_apply=%region_14.15 | all-reduce | flops 3 | bytes 24 | tf_op jit(solution)/shard_map/psum | solution.py:158
  788.6 2.6 multiply_reduce_fusion.5
  791.2 73.9 %psum.69 = f32[]{:T(128)} all-reduce(f32[]{:T(128)} %get-tuple-element.22), channel_id=1, replica_groups=mesh['grp'=32,'box'=8] {'grp','box'}, use_global_device_ids=true, to_apply=%region_16.17 | all-reduce | flops 1 | bytes 8 | tf_op jit(solution)/shard_map/psum | solution.py:105
  865.9 8.4 fusion.99
  874.4 0.8 fusion.81
  875.2 0.8 fusion.80
  876.0 0.7 fusion.79
  876.8 54.4 %all-gather.3 = f32[128,53,2,16]{1,3,2,0:T(8,128)} all-gather(f32[4,53,2,16]{1,3,2,0:T(8,128)S(1)} %pad_maximum_fusion.11), channel_id=5, replica_groups=mesh['grp'=32,'box'=8] {'grp'}, dimensions={0}, use_global_device_ids=true | all-gather | bytes 895488 | tf_op jit(solution)/shard_map/all_gather | solution.py:144
  931.2 2.1 gather_fusion.10
  933.4 0.7 fusion
  934.8 1.3 collective-permute-start.6
  936.1 1.3 collective-permute-start.7
  942.2 2.3 multiply_reduce_fusion.4
  944.5 2.6 pad_maximum_fusion.14
  947.0 76.2 %psum.70 = f32[4]{0:T(128)S(1)} all-reduce(f32[4]{0:T(128)S(1)} %pad_maximum_fusion.14), channel_id=1, replica_groups=mesh['grp'=32,'box'=8] {'grp','box'}, use_global_device_ids=true, to_apply=%region_21.22 | all-reduce | flops 4 | bytes 32 | tf_op jit(solution)/shard_map/psum | solution.py:158
  1029.0 3.3 multiply_reduce_fusion
  1032.3 74.0 %psum.71 = f32[]{:T(128)} all-reduce(f32[]{:T(128)} %multiply_reduce_fusion), channel_id=1, replica_groups=mesh['grp'=32,'box'=8] {'grp','box'}, use_global_device_ids=true, to_apply=%region_23.24 | all-reduce | flops 1 | bytes 8 | tf_op jit(solution)/shard_map/psum | solution.py:105
  1107.9 48.3 %all-gather.5 = f32[32,64,53]{1,2,0:T(8,128)S(1)} all-gather(f32[1,64,53]{1,2,0:T(8,128)S(1)} %fusion.5), channel_id=6, replica_groups=mesh['grp'=32,'box'=8] {'grp'}, dimensions={0}, use_global_device_ids=true | all-gather | bytes 447744 | tf_op jit(solution)/shard_map/all_gather | solution.py:176
  1157.5 0.7 reshape.722
  1158.2 0.8 copy.157
  (112 shorter events, 15.9 us)
Async XLA Ops:
  7.2 234.6 %copy-start = (f32[325,53]{0,1:T(8,128)S(1)}, f32[325,53]{0,1:T(8,128)}, u32[]{:S(2)}) copy-start(f32[325,53]{0,1:T(8,128)} %param.17) | copy-start | bytes 206704
  7.2 16.8 %copy-start.8 = (s32[1,4]{0,1:T(4,128)S(1)}, s32[1,4]{0,1:T(4,128)}, u32[]{:S(2)}) copy-start(s32[1,4]{0,1:T(4,128)} %constant.321) | copy-start | bytes 52
  7.2 15.0 %copy-start.4 = (f32[53,1,256]{2,1,0:T(1,128)S(1)}, f32[53,1,256]{2,1,0:T(1,128)}, u32[]{:S(2)}) copy-start(f32[53,1,256]{2,1,0:T(1,128)} %param.20) | copy-start | bytes 162820
  7.2 14.7 %copy-start.2 = (f32[325,1,2,256]{3,2,1,0:T(2,128)S(1)}, f32[325,1,2,256]{3,2,1,0:T(2,128)}, u32[]{:S(2)}) copy-start(f32[325,1,2,256]{3,2,1,0:T(2,128)} %param.18) | copy-start | bytes 1996804
  7.2 15.7 %copy-start.7 = (s32[32,4]{0,1:T(4,128)S(1)}, s32[32,4]{0,1:T(4,128)}, u32[]{:S(2)}) copy-start(s32[32,4]{0,1:T(4,128)} %param.21) | copy-start | bytes 1540
  7.2 16.9 %copy-start.9 = (s32[32,1]{0,1:T(1,128)S(1)}, s32[32,1]{0,1:T(1,128)}, u32[]{:S(2)}) copy-start(s32[32,1]{0,1:T(1,128)} %param.23) | copy-start | bytes 388
  7.2 83.4 %all-gather.8.cloned.1.call-start = ((), (), s32[]{:S(2)}) async-start(), calls=%async_computation | async-start | bytes 1892352 | tf_op jit(solution)/shard_map/all_gather | solution.py:110
  21.9 79.4 %copy-start.6 = (f32[53]{0:T(128)S(1)}, f32[53]{0:T(128)}, u32[]{:S(2)}) copy-start(f32[53]{0:T(128)} %param.15) | copy-start | bytes 640
  23.1 76.7 %copy-start.11 = (s32[4]{0:T(128)}, s32[4]{0:T(128)S(1)}, u32[]{:S(2)}) copy-start(s32[4]{0:T(128)S(1)} %iota_add_fusion) | copy-start | bytes 52
  177.0 65.6 %copy-start.1 = (f32[53,325]{1,0:T(8,128)S(1)}, f32[53,325]{1,0:T(8,128)}, u32[]{:S(2)}) copy-start(f32[53,325]{1,0:T(8,128)} %param.16) | copy-start | bytes 206704
  237.9 5.4 collective-permute-start
  239.8 3.6 collective-permute-start.1
  468.8 5.4 collective-permute-start.2
  470.7 3.7 collective-permute-start.3
  700.7 6.1 collective-permute-start.4
  702.7 4.2 collective-permute-start.5
  933.4 223.6 %copy-start.3 = (f32[53,4,64]{2,1,0:T(4,128)S(1)}, f32[53,4,64]{2,1,0:T(4,128)}, u32[]{:S(2)}) copy-start(f32[53,4,64]{2,1,0:T(4,128)} %reshape_squeeze.3) | copy-start | bytes 162820
  933.4 223.6 %copy-start.10 = (s32[32,1]{0,1:T(1,128)S(1)}, s32[32,1]{0,1:T(1,128)}, u32[]{:S(2)}) copy-start(s32[32,1]{0,1:T(1,128)} %param.23) | copy-start | bytes 388
  933.4 223.7 %copy-start.12 = (s32[4]{0:T(128)S(1)}, s32[4]{0:T(128)}, u32[]{:S(2)}) copy-start(s32[4]{0:T(128)} %copy-done.11) | copy-start | bytes 52
  933.4 223.7 %copy-start.13 = (pred[4]{0:T(512)(128)(4,1)S(1)}, pred[4]{0:T(512)(128)(4,1)}, u32[]{:S(2)}) copy-start(pred[4]{0:T(512)(128)(4,1)} %broadcast_compare_fusion.2) | copy-start | bytes 16
  934.8 6.7 collective-permute-start.6
  936.1 5.4 collective-permute-start.7
  941.5 0.6 copy-start.5
Sparse Core Ops, SparseCore 0:
  11.2 79.3 all-gather.7
where the time goes:
time: 1170 us
  blocking collectives  940 us (80%)
  waiting for transfers between devices  66 us (6%)
  local copies, waits for them, and re-layouts  46.8 us (4%)
  matrix products  40 us (3%)
  between operations  32.3 us (3%)
  other arithmetic  28.7 us (2%)
  starting transfers between devices  12.3 us (1%)
    psum x5, blocking collectives, global_norm(): return jnp.sqrt(lax.psum(jnp.sum(field * field), ('grp', 'box')))  370 us
    psum x4, blocking collectives, on_device(): summed = lax.psum(local, ('grp', 'box'))  308 us
    all_gather x4, blocking collectives, on_device(): every = lax.all_gather(planes[None], 'grp', axis=0, tiled=True)  213 us
    all_gather x1, waiting for transfers between devices, on_device(): lax.all_gather(coarse_field, 'grp', axis=1, tiled=True).reshape(species, -1)  65.7 us
    all_gather x1, blocking collectives, on_device(): lax.all_gather(averaged[:, None, :], 'grp', axis=1, tiled=True)  48.3 us
    dot_general x4, matrix products, on_device(): jnp.einsum('ijxc,jxc->ixc', inverse, basis[j], preferred_element_type=jnp...  33.8 us
  transfers between devices with their start and end apart: 9, of which 3 were waited for; matrix products, arithmetic and copies ran while one was open for 2% of the time, Pallas kernels for 0%

commit v1 on v0

v1 whole, which is shorter than its diff:
```python
import functools

import jax
import jax.numpy as jnp
import numpy as np
from jax import lax
from jax.experimental import pallas as pl
from jax.experimental.pallas import tpu as pltpu
from jax.sharding import PartitionSpec as P

FS = 16
ITERS = 4
SHIFT = 1.0
HALF = FS // 2
FACE = FS * FS
PAD = 56
ROWS = 2 * PAD
EXACT = lax.Precision.HIGHEST
VMEM = pl.BlockSpec(memory_space=pltpu.VMEM)
SMEM = pl.BlockSpec(memory_space=pltpu.SMEM)

NN = (((1,), (0,)), ((), ()))
NT = (((1,), (1,)), ((), ()))
TN = (((0,), (0,)), ((), ()))


def mm(a, b, dims=NN):
    return lax.dot_general(a, b, dims, precision=EXACT, preferred_element_type=jnp.float32)


def constants():
    cell = np.arange(FACE)
    y, z = cell // FS, cell % FS
    t = np.arange(FS)
    faces = np.zeros((4 * FS, FACE), np.float32)
    for f, lanes in enumerate((t, FACE - FS + t, t * FS, t * FS + FS - 1)):
        faces[f * FS + t, lanes] = 1.0
    inside = np.zeros((FACE, FACE), np.float32)
    for dy, dz in ((1, 0), (-1, 0), (0, 1), (0, -1)):
        ok = (y + dy >= 0) & (y + dy < FS) & (z + dz >= 0) & (z + dz < FS)
        inside[cell[ok], (y + dy)[ok] * FS + (z + dz)[ok]] = 1.0
    coarse = y // 2 * HALF + z // 2
    upsample = np.zeros((HALF * HALF, FACE), np.float32)
    upsample[coarse, cell] = 1.0
    side = np.zeros((4 * HALF, FACE), np.float32)
    for f in range(4):
        for k in range(FS):
            side[f * HALF + k // 2] += faces[f * FS + k]
    spread = np.zeros((2, 128, FACE), np.float32)
    spread[0, :64] = upsample
    spread[1, 64:96] = side
    halves = np.zeros((2, 128, FACE), np.float32)
    for m in range(4):
        c = np.arange(32)
        halves[0, 32 * m + c, 64 * m + c] = 1.0
        halves[1, 32 * m + c, 64 * m + 32 + c] = 1.0
    return faces, inside, upsample * 0.125, spread, halves


FACES, INSIDE, AVERAGE, SPREAD, HALVES = constants()


def call(kernel, name, shapes, args, specs, scratch=()):
    return pl.pallas_call(
        kernel,
        out_shape=[jax.ShapeDtypeStruct(s, jnp.float32) for s in shapes],
        in_specs=specs,
        out_specs=[VMEM] * len(shapes),
        scratch_shapes=list(scratch),
        compiler_params=pltpu.CompilerParams(vmem_limit_bytes=24 << 20),
        name=name,
    )(*args)


def gather_kernel(patch, entries, out):
    p = patch[...]
    p = jnp.concatenate([p, jnp.zeros((PAD - p.shape[0], FACE), jnp.float32)], axis=0)
    high = p.astype(jnp.bfloat16)
    rest = p - high.astype(jnp.float32)
    mid = rest.astype(jnp.bfloat16)
    low = (rest - mid.astype(jnp.float32)).astype(jnp.bfloat16)
    parts = jnp.concatenate([high, mid, low], axis=0)
    cell = lax.broadcasted_iota(jnp.int32, (FACE, 128), 0)
    for g in range(out.shape[0]):
        hot = (cell == entries[g : g + 1, :]).astype(jnp.float32).astype(jnp.bfloat16)
        got = jnp.dot(parts, hot, preferred_element_type=jnp.float32)
        out[g] = got[:PAD] + got[PAD : 2 * PAD] + got[2 * PAD :]


def mix(a, b, keep, shift):
    return jnp.where(keep, a, b) + pltpu.roll(jnp.where(keep, b, a), shift, 0)


def apply_inverse(inv, rows, u):
    count, depth = inv.shape[0], inv.shape[1]
    full = depth // 8
    for half in range(2):
        lanes = slice(128 * half, 128 * half + 128)
        row = lax.broadcasted_iota(jnp.int32, (8, 128), 0)
        bit2, bit1, bit0 = (row & 4) == 0, (row & 2) == 0, (row & 1) == 0
        w = [rows[half, 8 * k : 8 * k + 8, :] for k in range(full + 1)]
        zero = jnp.zeros((8, 128), jnp.float32)

        def one(i):
            if i >= count:
                return zero
            m = inv[i, :, lanes].astype(jnp.float32)
            total = m[0:8] * w[0]
            for k in range(1, full):
                total = total + m[8 * k : 8 * k + 8] * w[k]
            last = m[8 * full : depth]
            last = jnp.concatenate([last, jnp.zeros((8 - last.shape[0], 128), jnp.float32)], axis=0)
            return total + last * w[full]

        for block in range(PAD // 8):
            a = [one(8 * block + d) for d in range(8)]
            b = [mix(a[d], a[d + 2], bit1, 6) for d in (0, 1, 4, 5)]
            c = [mix(b[d], b[d + 2], bit2, 4) for d in range(2)]
            u[8 * block : 8 * block + 8, lanes] = jnp.where(bit0, c[0], pltpu.roll(c[1], 1, 0))
            u[PAD + 8 * block : PAD + 8 * block + 8, lanes] = jnp.where(
                bit0, pltpu.roll(c[0], 7, 0), c[1]
            )


def interleave(rows, field):
    for half in range(2):
        lanes = slice(128 * half, 128 * half + 128)
        rows.at[half][pl.ds(0, PAD, stride=2), :] = field[:PAD, lanes]
        rows.at[half][pl.ds(1, PAD, stride=2), :] = field[PAD:, lanes]


def separate(rows):
    planes = [
        jnp.concatenate([rows.at[h][pl.ds(x, PAD, stride=2), :] for h in range(2)], axis=1)
        for x in range(2)
    ]
    return jnp.concatenate(planes, axis=0)


def precondition(meta, inv, faces, w, rows, u, slots):
    interleave(rows, w)
    apply_inverse(inv, rows, u)
    planes = mm(faces[...], u[...], NT)
    for f in range(4):
        slots[meta[f], :, 0:ROWS] = planes[FS * f : FS * f + FS]


def first_kernel(meta, received, source, scale, spread, faces, inv, w_out, u, slots, rows):
    values = received[0]
    for g in range(1, received.shape[0]):
        values = values + received[g]
    beside = mm(values, spread[1])
    across = mm(values, spread[0])
    box = jnp.full((1, 1), meta[9], jnp.int32)
    lower = beside + jnp.where(box == 0, across, 0.0)
    upper = beside + jnp.where(box == meta[10], across, 0.0)
    boundary = jnp.concatenate([lower, upper], axis=0)
    species = source.shape[0]
    for half in range(2):
        rows[half, 0:species, :] = source[:, 128 * half : 128 * half + 128]
        rows[half, species:ROWS, :] = jnp.zeros((ROWS - species, 128), jnp.float32)
    right = separate(rows) + scale[:, 3:4] * boundary
    w_out[...] = right
    precondition(meta, inv, faces, right, rows, u, slots)


def operate(meta, received, low, high, u, w, scale, inside, faces, orders, stoich, rates):
    field = u[...]
    ghosts = []
    for f in range(4):
        plane = received[meta[f], :, 0:ROWS]
        ghosts.append(jnp.where(jnp.full((1, 1), meta[11 + f], jnp.int32) > 0, plane, 0.0))
    total = mm(field, inside[...]) + mm(jnp.concatenate(ghosts, axis=0), faces[...], TN)
    total = total + jnp.concatenate([low[...] + field[PAD:], field[:PAD] + high[...]], axis=0)
    both = jnp.concatenate([field[:PAD], field[PAD:]], axis=1)
    progress = mm(orders[...], both) * rates[...]
    chemistry = mm(stoich[...], progress)
    chemistry = jnp.concatenate([chemistry[:, :FACE], chemistry[:, FACE:]], axis=0)
    return scale[:, 0:1] * field - scale[:, 1:2] * total - chemistry - scale[:, 2:3] * w[...]


def step_kernel(meta, received, low, high, u, w, scale, inside, faces, orders, stoich, rates, inv, w_out, u_out, slots, rows):
    image = operate(meta, received, low, high, u, w, scale, inside, faces, orders, stoich, rates)
    w_out[...] = image
    precondition(meta, inv, faces, image, rows, u_out, slots)


def last_kernel(meta, received, low, high, u, w0, w1, w2, w3, scale, inside, faces, orders, stoich, rates, out):
    image = operate(meta, received, low, high, u, w3, scale, inside, faces, orders, stoich, rates)
    w = [w0[...], w1[...], w2[...], w3[...], image]
    lane = lax.broadcasted_iota(jnp.int32, (1, 128), 1)
    line = jnp.zeros((1, 128), jnp.float32)
    k = 0
    for a in range(ITERS + 1):
        for b in range(a + 1):
            part = jnp.sum(w[a] * w[b], axis=0, keepdims=True)
            part = jnp.sum(part, axis=1, keepdims=True)
            line = jnp.where(lane == k, part, line)
            k += 1
    out[...] = jnp.broadcast_to(line, out.shape)


def solve(gram, shift):
    def g(a, b):
        return gram[(max(a, b), min(a, b))]

    n = ITERS
    target = [g(a + 1, 0) + shift * g(a, 0) for a in range(n)]
    normal = {}
    for a in range(n):
        for b in range(a + 1):
            normal[a, b] = (
                g(a + 1, b + 1) + shift * (g(a + 1, b) + g(a, b + 1)) + shift * shift * g(a, b)
            )
    size = [lax.rsqrt(normal[a, a]) for a in range(n)]
    target = [target[a] * size[a] for a in range(n)]
    lower = {}
    inverse = [None] * n
    for a in range(n):
        for b in range(a + 1):
            value = normal[a, b] * size[a] * size[b]
            for c in range(b):
                value = value - lower[a, c] * lower[b, c]
            if a == b:
                inverse[a] = lax.rsqrt(value)
            else:
                lower[a, b] = value * inverse[b]
    half = []
    for a in range(n):
        value = target[a]
        for c in range(a):
            value = value - lower[a, c] * half[c]
        half.append(value * inverse[a])
    result = [None] * n
    for a in reversed(range(n)):
        value = half[a]
        for c in range(a + 1, n):
            value = value - lower[c, a] * result[c]
        result[a] = value * inverse[a]
    return [result[a] * size[a] for a in range(n)]


def finish_kernel(meta, lines, u0, u1, u2, u3, scale, average, correction, slots, rows):
    line = jnp.sum(lines[...], axis=0, keepdims=True)
    gram = {}
    k = 0
    for a in range(ITERS + 1):
        for b in range(a + 1):
            gram[a, b] = line[:, k : k + 1]
            k += 1
    shift = scale[0:1, 2:3]
    weights = solve(gram, shift)
    factor = scale[0:1, 4:5]
    total = jnp.zeros((ROWS, FACE), jnp.float32)
    for weight, u in zip(weights, (u0, u1, u2, u3)):
        total = total + (weight * factor) * u[...]
    interleave(rows, total)
    for half in range(2):
        lanes = slice(128 * half, 128 * half + 128)
        correction[:, lanes] = rows[half, 0 : correction.shape[0], :]
    summed = total[:PAD] + total[PAD:]
    blank = jnp.zeros((64 - PAD, FACE), jnp.float32)
    spread = jnp.concatenate([summed, blank, summed, blank], axis=0)
    mean = mm(average[...], spread, NT)
    lane = lax.broadcasted_iota(jnp.int32, (32, 128), 1)
    slots[meta[4]] = jnp.where(lane < 64, mean[:32], mean[32:])


def update_kernel(meta, received, patch, halves, out):
    blocks = []
    lane = lax.broadcasted_iota(jnp.int32, (1, FACE), 1)
    covered = jnp.zeros((1, FACE), jnp.int32)
    for m in range(4):
        source = meta[5 + m]
        block = received[jnp.maximum(source, 0)]
        blocks.append(jnp.where(jnp.full((1, 1), source, jnp.int32) >= 0, block, 0.0))
        covered = jnp.where(lane // 64 == m, source, covered)
    stacked = jnp.concatenate(blocks, axis=0)
    species = patch.shape[0]
    first = mm(stacked, halves[0], TN)[0:species]
    second = mm(stacked, halves[1], TN)[64 : 64 + species]
    out[...] = jnp.where(covered >= 0, first + second, patch[...])


def on_device(
    source_term,
    diffusion,
    stoich,
    orders,
    rates,
    precond,
    coarse_field,
    neighbours,
    ghost_list,
    average_list,
):
    species, reactions = stoich.shape
    groups = lax.axis_size("grp")
    boxes = lax.axis_size("box")
    me = lax.axis_index("grp")
    box = lax.axis_index("box")
    f32 = jnp.float32

    links = lax.dynamic_index_in_dim(neighbours, me, 0, keepdims=False)
    owned = average_list[:, 0]
    wanted = me * 4 + jnp.arange(4)
    found = jnp.max(
        jnp.where(owned[None, :] == wanted[:, None], jnp.arange(groups)[None, :], -1), axis=1
    )
    home = lax.dynamic_index_in_dim(owned, me, 0, keepdims=True) // 4
    meta = jnp.concatenate(
        [
            jnp.where(links >= 0, links, me),
            home,
            found,
            jnp.stack([box, jnp.asarray(boxes - 1, box.dtype)]),
            (links >= 0).astype(jnp.int32),
            jnp.zeros((1,), jnp.int32),
        ]
    ).astype(jnp.int32)

    wide = 1.0 + 12.0 * jnp.max(diffusion)
    wide = wide + jnp.sqrt(jnp.sum(stoich * stoich)) * jnp.sqrt(jnp.sum(orders * orders))
    unit = 32.0 / wide
    column = jnp.pad(diffusion, (0, PAD - species))
    mask = (jnp.arange(PAD) < species).astype(f32)
    scale = jnp.stack(
        [
            unit * (1.0 + 6.0 * column) * mask,
            unit * column,
            jnp.full((PAD,), SHIFT, f32) * unit,
            column,
            jnp.full((PAD,), 1.0, f32) * unit,
        ],
        axis=1,
    )
    scale = jnp.concatenate([scale, scale], axis=0)
    stoich_s = jnp.pad(stoich * unit, ((0, PAD - species), (0, 0)))
    orders_s = jnp.pad(orders, ((0, 0), (0, PAD - species)))
    rates_s = rates.reshape(reactions, 2 * FACE)
    inverse = precond.reshape(species, 2 * species, FACE)
    source = source_term.reshape(2 * species, FACE)
    patch = coarse_field.reshape(species, FACE)

    lists = ghost_list[:, 0, :]
    entries = jnp.concatenate(
        [jnp.where(box == 0, lists[:, :64], lists[:, 64:128]), lists[:, 128:]], axis=1
    )
    entries = jnp.where(entries >= 0, entries - me * FACE, -1)
    entries = jnp.pad(entries, ((0, 0), (0, 128 - entries.shape[1])), constant_values=-1)

    def exchange(slots):
        return lax.all_to_all(slots, "grp", 0, 0, tiled=True)

    (asked,) = call(gather_kernel, "gather", [(groups, PAD, 128)], (patch, entries), [VMEM] * 2)
    received = exchange(asked)
    faces = jnp.asarray(FACES)
    inside = jnp.asarray(INSIDE)
    outs = [(ROWS, FACE), (ROWS, FACE), (groups, FS, 128)]
    rows = [pltpu.VMEM((2, ROWS, 128), f32)]
    w, u, slots = call(
        first_kernel,
        "first",
        outs,
        (meta, received, source, scale, jnp.asarray(SPREAD), faces, inverse),
        [SMEM] + [VMEM] * 6,
        rows,
    )
    basis, directions = [w], [u]
    for j in range(ITERS):
        low = lax.ppermute(u[PAD:], "box", [(i, i + 1) for i in range(boxes - 1)])
        high = lax.ppermute(u[:PAD], "box", [(i + 1, i) for i in range(boxes - 1)])
        received = exchange(slots)
        shared = (scale, inside, faces, orders_s, stoich_s, rates_s)
        if j + 1 < ITERS:
            w, u, slots = call(
                step_kernel,
                "step%d" % j,
                outs,
                (meta, received, low, high, u, w) + shared + (inverse,),
                [SMEM] + [VMEM] * 12,
                rows,
            )
            basis.append(w)
            directions.append(u)
        else:
            (lines,) = call(
                last_kernel,
                "last",
                [(groups * boxes, 128)],
                (meta, received, low, high, u) + tuple(basis) + shared,
                [SMEM] + [VMEM] * 14,
            )
    lines = lax.all_to_all(lines, ("grp", "box"), 0, 0, tiled=True)
    correction, slots = call(
        finish_kernel,
        "finish",
        [(2 * species, FACE), (groups, 32, 128)],
        (meta, lines) + tuple(directions) + (scale, jnp.asarray(AVERAGE)),
        [SMEM] + [VMEM] * 7,
        rows,
    )
    received = exchange(slots)
    (updated,) = call(
        update_kernel,
        "update",
        [(species, FACE)],
        (meta, received, patch, jnp.asarray(HALVES)),
        [SMEM] + [VMEM] * 3,
    )
    return (
        correction.reshape(species, 1, 2, FACE),
        updated.reshape(species, 1, FACE),
    )


def solution(mesh):
    placed = (
        P(None, "grp", "box", None),
        P(),
        P(),
        P(),
        P(None, "grp", "box", None),
        P(None, None, "grp", "box", None),
        P(None, "grp", "box"),
        P(),
        P(None, "box", None),
        P(None, "box"),
    )
    return jax.shard_map(
        on_device,
        mesh=mesh,
        in_specs=placed,
        out_specs=(P(None, "grp", "box", None), P(None, "grp", "box")),
        check_vma=False,
    )
```

time: 1170 us -> 219 us (0.19)
  blocking collectives: 940 us -> 23.2 us
  starting transfers between devices: 12.3 us -> 62.9 us
  matrix products: 40 us -> 0 us
  between operations: 32.3 us -> 5.84 us
  other arithmetic: 28.7 us -> 2.92 us
  waiting for transfers between devices: 66 us -> 44.6 us
  Pallas kernels: 0 us -> 20.6 us
    psum x9 -> x0, blocking collectives: 678 us -> none  [the longest x5 370 us: global_norm(): return jnp.sqrt(lax.psum(jnp.sum(field * field), ('grp', 'box')))]
    all_gather x5 -> x0, blocking collectives: 262 us -> none  [the longest x4 213 us: on_device(): every = lax.all_gather(planes[None], 'grp', axis=0, tiled=True)]
    all_gather x1 -> x0, waiting for transfers between devices: 65.7 us -> none  [on_device(): lax.all_gather(coarse_field, 'grp', axis=1, tiled=True).reshape(species, -1)]
    all_to_all x0 -> x6, starting transfers between devices: none -> 44.2 us  [exchange(): return lax.all_to_all(slots, 'grp', 0, 0, tiled=True)]
    all_to_all x0 -> x6, waiting for transfers between devices: none -> 43.4 us  [exchange(): return lax.all_to_all(slots, 'grp', 0, 0, tiled=True)]
    dot_general x14 -> x0, matrix products: 40 us -> none  [the longest x4 33.8 us: on_device(): jnp.einsum('ijxc,jxc->ixc', inverse, basis[j], preferred_element_type=jnp...]
    unnamed x34 -> x124, local copies, waits for them, and re-layouts: 4.61 us -> 42.2 us
    all_to_all x0 -> x1, blocking collectives: none -> 23.2 us  [on_device(): lines = lax.all_to_all(lines, ('grp', 'box'), 0, 0, tiled=True)]
  transfers between devices with their start and end apart: 9 -> 14, of which waited for: 3 -> 8; matrix products, arithmetic and copies ran while one was open for 2% -> 10% of each run, Pallas kernels for 0% -> 0%
where the time goes in v1:
time: 219 us; the launch traced here: 216 us
  starting transfers between devices  62.9 us (29%)
  local copies, waits for them, and re-layouts  56.4 us (26%)
  waiting for transfers between devices  44.6 us (20%)
  blocking collectives  23.2 us (11%)
  Pallas kernels  20.6 us (9%)
  between operations  5.84 us (3%)
  other arithmetic  2.92 us (1%)
    all_to_all x6, starting transfers between devices, exchange(): return lax.all_to_all(slots, 'grp', 0, 0, tiled=True)  44.2 us
    all_to_all x6, waiting for transfers between devices, exchange(): return lax.all_to_all(slots, 'grp', 0, 0, tiled=True)  43.4 us
    unnamed x124, local copies, waits for them, and re-layouts  42.2 us
    all_to_all x1, blocking collectives, on_device(): lines = lax.all_to_all(lines, ('grp', 'box'), 0, 0, tiled=True)  23.2 us
    pallas_call x8, Pallas kernels, call(): pl.pallas_call(kernel, out_shape=[jax.ShapeDtypeStruct(s, jnp.float32) fo...  20.6 us
    ppermute x4, starting transfers between devices, on_device(): low = lax.ppermute(u[PAD:], 'box', [(i, i + 1) for i in range(boxes - 1)])  13.6 us
    reshape x1, local copies, waits for them, and re-layouts, on_device(): inverse = precond.reshape(species, 2 * species, FACE)  5.91 us
    ppermute x4, starting transfers between devices, on_device(): high = lax.ppermute(u[:PAD], 'box', [(i + 1, i) for i in range(boxes - 1)])  5.14 us
  transfers between devices with their start and end apart: 14, of which 8 were waited for; matrix products, arithmetic and copies ran while one was open for 10% of the time, Pallas kernels for 0%

profile of v1, /device:TPU:2, one launch (start us, length us, event | category | flops | bytes accessed | tf_op | source)
XLA Modules:
  0.0 216.4 jit_solution(5329860615509032843)
XLA Ops:
  1.6 0.8 copy.48
  2.5 1.8 gather.1
  4.3 11.7 %all-to-all-start = ((f32[32,56,128]{2,1,0:T(8,128)}), f32[32,56,128]{2,1,0:T(8,128)}, u32[]{:S(2)}, u32[]{:S(2)}) async-start(f32[32,56,128]{2,1,0:T(8,128)} %gather.1), calls=%async_computation | async-start | bytes 1835008 | tf_op jit(solution)/shard_map/all_to_all | solution.py:353
  23.7 5.9 %reshape.36.inv = bf16[53,106,256]{2,1,0:T(8,128)(2,1)S(1)} reshape(bf16[53,53,1,2,256]{4,3,2,1,0:T(2,128)(2,1)} %param.20) | data formatting | bytes 5752832 | tf_op jit(solution)/shard_map/reshape | solution.py:341
  29.9 11.4 %all-to-all-done.received = f32[32,56,128]{2,1,0:T(8,128)} async-done(((f32[32,56,128]{2,1,0:T(8,128)}), f32[32,56,128]{2,1,0:T(8,128)}, u32[]{:S(2)}, u32[]{:S(2)}) %all-to-all-start) | async-done | bytes 917536 | tf_op jit(solution)/shard_map/all_to_all | solution.py:353
  41.3 0.9 copy-done.38
  42.3 2.4 %first.1 = (f32[112,256]{1,0:T(8,128)S(1)}, f32[112,256]{1,0:T(8,128)S(1)}, f32[32,16,128]{2,1,0:T(8,128)S(1)}) custom-call(s32[16]{0:T(128)S(1)} %concatenate.9.meta, f32[32,56,128]{2,1,0:T(8,128)} %all-to-all-done.received, f32[106,256]{1,0:T(8,128)S(1)} %reshape.35.source, f32[112,5]{1,0:T(8,128)S(1)} %copy.33.scale, f32[2,128,256]{2,1,0:T(8,128)S(1)} %copy-done.38, ...), custom_call_target="tpu_custom_call" | custom-call | tf_op jit(solution)/shard_map/first/pallas_call | solution.py:64
  46.7 5.8 %all-to-all-start.1 = ((f32[32,16,128]{2,1,0:T(8,128)}), f32[32,16,128]{2,1,0:T(8,128)}, u32[]{:S(2)}, u32[]{:S(2)}) async-start(f32[32,16,128]{2,1,0:T(8,128)} %copy-done.39), calls=%async_computation.1 | async-start | bytes 524288 | tf_op jit(solution)/shard_map/all_to_all | solution.py:353
  52.5 1.5 fusion.4
  53.9 1.3 collective-permute-start.1
  55.2 3.6 %collective-permute-start = (f32[56,256]{1,0:T(8,128)}, f32[56,256]{1,0:T(8,128)}, u32[]{:S(2)}, u32[]{:S(2)}) collective-permute-start(f32[56,256]{1,0:T(8,128)} %get-tuple-element.43), channel_id=1, source_target_pairs={{0,1},{1,2},{2,3},{3,4},{4,5},{5,6},{6,7},{8,9},{9,10},{10,11},{11... | collective-permute-start | bytes 172040 | tf_op jit(solution)/shard_map/ppermute | solution.py:371
  59.5 1.7 copy.34
  61.2 1.5 pad.19.stoich
  62.7 0.9 pad.18.orders
  63.7 1.3 pad.24
  65.0 0.9 copy.45
  65.9 1.1 copy-done.1
  67.0 0.9 copy-done.6
  67.9 0.8 copy-done.11
  68.8 0.9 copy-done.16
  69.7 0.9 copy-done.29
  70.6 3.5 %step0.1 = (f32[112,256]{1,0:T(8,128)S(1)}, f32[112,256]{1,0:T(8,128)S(1)}, f32[32,16,128]{2,1,0:T(8,128)S(1)}) custom-call(s32[16]{0:T(128)S(1)} %concatenate.9.meta, f32[32,16,128]{2,1,0:T(8,128)} %all-to-all-done.1.received, f32[56,256]{1,0:T(8,128)} %collective-permute-done.low, f32[56,256]{1,0:T(8,128)} %collective-permute-done.1.high, ...), custom_call_target="tpu_custom_call" | custom-call | tf_op jit(solution)/shard_map/step0/pallas_call | solution.py:64
  76.0 9.8 %all-to-all-start.2 = ((f32[32,16,128]{2,1,0:T(8,128)}), f32[32,16,128]{2,1,0:T(8,128)}, u32[]{:S(2)}, u32[]{:S(2)}) async-start(f32[32,16,128]{2,1,0:T(8,128)} %copy-done.41), calls=%async_computation.2 | async-start | bytes 524288 | tf_op jit(solution)/shard_map/all_to_all | solution.py:353
  85.9 0.9 fusion.3
  86.7 1.3 collective-permute-start.3
  88.0 3.0 %collective-permute-start.2 = (f32[56,256]{1,0:T(8,128)S(1)}, f32[56,256]{1,0:T(8,128)S(1)}, u32[]{:S(2)}, u32[]{:S(2)}) collective-permute-start(f32[56,256]{1,0:T(8,128)S(1)} %get-tuple-element.41), channel_id=1, source_target_pairs={{0,1},{1,2},{2,3},{3,4},{4,5},{5,6},{6,7},{8,9},{9,10},{10,11},{11... | collective-permute-start | bytes 172040 | tf_op jit(solution)/shard_map/ppermute | solution.py:371
  92.6 5.3 %all-to-all-done.2.received = f32[32,16,128]{2,1,0:T(8,128)} async-done(((f32[32,16,128]{2,1,0:T(8,128)}), f32[32,16,128]{2,1,0:T(8,128)}, u32[]{:S(2)}, u32[]{:S(2)}) %all-to-all-start.2) | async-done | bytes 262176 | tf_op jit(solution)/shard_map/all_to_all | solution.py:353
  97.9 1.1 copy-done.2
  99.0 0.9 copy-done.7
  99.9 0.8 copy-done.12
  100.7 0.9 copy-done.19
  101.6 0.9 copy-done.32
  104.2 3.4 %step1.1 = (f32[112,256]{1,0:T(8,128)S(1)}, f32[112,256]{1,0:T(8,128)S(1)}, f32[32,16,128]{2,1,0:T(8,128)S(1)}) custom-call(s32[16]{0:T(128)S(1)} %concatenate.9.meta, f32[32,16,128]{2,1,0:T(8,128)} %all-to-all-done.2.received, f32[56,256]{1,0:T(8,128)S(1)} %copy-done.53, f32[56,256]{1,0:T(8,128)S(1)} %copy-done.49, f32[112,256]{1,0:T(8,128)S(1)} %copy-done.19, ...), custom_call_target="tpu_custom_call" | custom-call | tf_op jit(solution)/shard_map/step1/pallas_call | solution.py:64
  109.6 6.2 %all-to-all-start.3 = ((f32[32,16,128]{2,1,0:T(8,128)}), f32[32,16,128]{2,1,0:T(8,128)}, u32[]{:S(2)}, u32[]{:S(2)}) async-start(f32[32,16,128]{2,1,0:T(8,128)} %copy-done.42), calls=%async_computation.3 | async-start | bytes 524288 | tf_op jit(solution)/shard_map/all_to_all | solution.py:353
  115.8 0.9 fusion.2
  116.7 1.3 collective-permute-start.5
  118.0 3.2 %collective-permute-start.4 = (f32[56,256]{1,0:T(8,128)S(1)}, f32[56,256]{1,0:T(8,128)S(1)}, u32[]{:S(2)}, u32[]{:S(2)}) collective-permute-start(f32[56,256]{1,0:T(8,128)S(1)} %get-tuple-element.39), channel_id=1, source_target_pairs={{0,1},{1,2},{2,3},{3,4},{4,5},{5,6},{6,7},{8,9},{9,10},{10,11},{11... | collective-permute-start | bytes 172040 | tf_op jit(solution)/shard_map/ppermute | solution.py:371
  122.5 4.6 %all-to-all-done.3.received = f32[32,16,128]{2,1,0:T(8,128)} async-done(((f32[32,16,128]{2,1,0:T(8,128)}), f32[32,16,128]{2,1,0:T(8,128)}, u32[]{:S(2)}, u32[]{:S(2)}) %all-to-all-start.3) | async-done | bytes 262176 | tf_op jit(solution)/shard_map/all_to_all | solution.py:353
  127.2 1.1 copy-done.3
  128.3 0.9 copy-done.8
  129.2 0.8 copy-done.13
  130.0 0.9 copy-done.22
  130.9 0.9 copy-done.35
  133.4 3.4 %step2.1 = (f32[112,256]{1,0:T(8,128)S(1)}, f32[112,256]{1,0:T(8,128)S(1)}, f32[32,16,128]{2,1,0:T(8,128)S(1)}) custom-call(s32[16]{0:T(128)S(1)} %concatenate.9.meta, f32[32,16,128]{2,1,0:T(8,128)} %all-to-all-done.3.received, f32[56,256]{1,0:T(8,128)S(1)} %copy-done.51, f32[56,256]{1,0:T(8,128)S(1)} %copy-done.47, f32[112,256]{1,0:T(8,128)S(1)} %copy-done.22, ...), custom_call_target="tpu_custom_call" | custom-call | tf_op jit(solution)/shard_map/step2/pallas_call | solution.py:64
  138.9 5.7 %all-to-all-start.4 = ((f32[32,16,128]{2,1,0:T(8,128)}), f32[32,16,128]{2,1,0:T(8,128)S(1)}, u32[]{:S(2)}, u32[]{:S(2)}) async-start(f32[32,16,128]{2,1,0:T(8,128)} %copy-done.40), calls=%async_computation.4 | async-start | bytes 524288 | tf_op jit(solution)/shard_map/all_to_all | solution.py:353
  144.6 0.9 fusion.1
  145.5 1.3 collective-permute-start.7
  146.8 3.7 %collective-permute-start.6 = (f32[56,256]{1,0:T(8,128)S(1)}, f32[56,256]{1,0:T(8,128)S(1)}, u32[]{:S(2)}, u32[]{:S(2)}) collective-permute-start(f32[56,256]{1,0:T(8,128)S(1)} %get-tuple-element.37), channel_id=1, source_target_pairs={{0,1},{1,2},{2,3},{3,4},{4,5},{5,6},{6,7},{8,9},{9,10},{10,11},{11... | collective-permute-start | bytes 172040 | tf_op jit(solution)/shard_map/ppermute | solution.py:371
  150.4 0.9 collective-permute-done.6.low
  151.3 5.4 %all-to-all-done.4.received = f32[32,16,128]{2,1,0:T(8,128)S(1)} async-done(((f32[32,16,128]{2,1,0:T(8,128)}), f32[32,16,128]{2,1,0:T(8,128)S(1)}, u32[]{:S(2)}, u32[]{:S(2)}) %all-to-all-start.4) | async-done | bytes 262176 | tf_op jit(solution)/shard_map/all_to_all | solution.py:353
  156.7 1.1 copy-done.4
  157.8 0.9 copy-done.9
  158.7 0.8 copy-done.14
  159.5 0.9 copy-done.25
  160.4 0.9 copy-done.30
  161.3 0.9 copy-done.33
  162.2 0.9 copy-done.36
  163.1 0.9 copy-done.44
  164.0 2.2 %last.1 = f32[256,128]{1,0:T(8,128)S(1)} custom-call(s32[16]{0:T(128)S(1)} %concatenate.9.meta, f32[32,16,128]{2,1,0:T(8,128)S(1)} %all-to-all-done.4.received, f32[56,256]{1,0:T(8,128)S(1)} %collective-permute-done.6.low, f32[56,256]{1,0:T(8,128)S(1)} %collective-permute-done.7.high, f32[112,256]{1,0:T(8,128)S(1)} %copy-done.25, f32[112,256]{1,0:T(8,128)S(1)} %copy-done.30, ...), custom_call_target="tpu_custom_call" | custom-call | tf_op jit(solution)/shard_map/last/pallas_call | solution.py:64
  166.3 23.2 %all_to_all.41 = f32[256,1,128]{2,1,0:T(1,128)S(1)} all-to-all(f32[256,1,128]{2,1,0:T(1,128)S(1)} %bitcast.30), channel_id=1, replica_groups=mesh['grp'=32,'box'=8] {'grp','box'}, dimensions={0} | all-to-all | bytes 262144 | tf_op jit(solution)/shard_map/all_to_all | solution.py:394
  189.5 2.9 %finish.1 = (f32[106,256]{1,0:T(8,128)S(1)}, f32[32,32,128]{2,1,0:T(8,128)}) custom-call(s32[16]{0:T(128)S(1)} %concatenate.9.meta, f32[256,128]{1,0:T(8,128)S(1)} %bitcast.29, f32[112,256]{1,0:T(8,128)S(1)} %copy-done.17, f32[112,256]{1,0:T(8,128)S(1)} %copy-done.20, f32[112,256]{1,0:T(8,128)S(1)} %copy-done.23, f32[112,256]{1,0:T(8,128)S(1)} %copy-done.25, ...), custom_call_target="tpu_custom_call" | custom-call | tf_op jit(solution)/shard_map/finish/pallas_call | solution.py:64
  192.4 5.0 %all-to-all-start.6 = ((f32[32,32,128]{2,1,0:T(8,128)}), f32[32,32,128]{2,1,0:T(8,128)S(1)}, u32[]{:S(2)}, u32[]{:S(2)}) async-start(f32[32,32,128]{2,1,0:T(8,128)} %get-tuple-element.29), calls=%async_computation.6 | async-start | bytes 1048576 | tf_op jit(solution)/shard_map/all_to_all | solution.py:353
  198.1 16.6 %all-to-all-done.6.received = f32[32,32,128]{2,1,0:T(8,128)S(1)} async-done(((f32[32,32,128]{2,1,0:T(8,128)}), f32[32,32,128]{2,1,0:T(8,128)S(1)}, u32[]{:S(2)}, u32[]{:S(2)}) %all-to-all-start.6) | async-done | bytes 524320 | tf_op jit(solution)/shard_map/all_to_all | solution.py:353
  214.8 1.0 update.1
  (126 shorter events, 20.4 us)
Async XLA Ops:
  0.6 21.2 %copy-start = (s32[32,4]{0,1:T(4,128)S(1)}, s32[32,4]{0,1:T(4,128)}, u32[]{:S(2)}) copy-start(s32[32,4]{0,1:T(4,128)} %param.22) | copy-start | bytes 1540
  0.6 15.4 %copy-start.58 = (s32[32,1]{0,1:T(1,128)S(1)}, s32[32,1]{0,1:T(1,128)}, u32[]{:S(2)}) copy-start(s32[32,1]{0,1:T(1,128)} %param.24) | copy-start | bytes 388
  0.7 18.5 %copy-start.55 = (f32[325,53]{0,1:T(8,128)S(1)}, f32[325,53]{0,1:T(8,128)}, u32[]{:S(2)}) copy-start(f32[325,53]{0,1:T(8,128)} %param.18) | copy-start | bytes 206704
  0.7 19.9 %copy-start.54 = (f32[53,325]{1,0:T(8,128)S(1)}, f32[53,325]{1,0:T(8,128)}, u32[]{:S(2)}) copy-start(f32[53,325]{1,0:T(8,128)} %param.17) | copy-start | bytes 206704
  0.7 21.4 %copy-start.57 = (f32[53]{0:T(128)S(1)}, f32[53]{0:T(128)}, u32[]{:S(2)}) copy-start(f32[53]{0:T(128)} %param.16) | copy-start | bytes 640
  0.7 22.9 %copy-start.56 = (f32[53,1,2,256]{3,2,1,0:T(2,128)S(1)}, f32[53,1,2,256]{3,2,1,0:T(2,128)}, u32[]{:S(2)}) copy-start(f32[53,1,2,256]{3,2,1,0:T(2,128)} %param.15) | copy-start | bytes 325636
  2.4 21.0 %copy-start.26 = (f32[53,1,256]{2,0,1:T(8,128)}, f32[53,1,256]{2,0,1:T(8,128)S(1)}, u32[]{:S(2)}) copy-start(f32[53,1,256]{2,0,1:T(8,128)S(1)} %copy.48) | copy-start | bytes 162820
  4.3 37.0 %all-to-all-start = ((f32[32,56,128]{2,1,0:T(8,128)}), f32[32,56,128]{2,1,0:T(8,128)}, u32[]{:S(2)}, u32[]{:S(2)}) async-start(f32[32,56,128]{2,1,0:T(8,128)} %gather.1), calls=%async_computation | async-start | bytes 1835008 | tf_op jit(solution)/shard_map/all_to_all | solution.py:353
  23.6 17.7 %copy-start.10 = (f32[64,256]{1,0:T(8,128)S(1)}, f32[64,256]{1,0:T(8,128)}, u32[]{:S(2)}) copy-start(f32[64,256]{1,0:T(8,128)} %constant.82.clone.faces) | copy-start | bytes 196612
  41.3 1.0 copy-start.38
  45.3 0.7 copy-start.28
  46.0 0.7 copy-start.39
  46.7 19.2 %copy-start.5 = (f32[256,256]{1,0:T(8,128)S(1)}, f32[256,256]{1,0:T(8,128)}, u32[]{:S(2)}) copy-start(f32[256,256]{1,0:T(8,128)} %constant.83.clone.inside) | copy-start | bytes 786436
  46.7 19.2 %all-to-all-start.1 = ((f32[32,16,128]{2,1,0:T(8,128)}), f32[32,16,128]{2,1,0:T(8,128)}, u32[]{:S(2)}, u32[]{:S(2)}) async-start(f32[32,16,128]{2,1,0:T(8,128)} %copy-done.39), calls=%async_computation.1 | async-start | bytes 524288 | tf_op jit(solution)/shard_map/all_to_all | solution.py:353
  53.9 12.0 %collective-permute-start.1 = (f32[56,256]{1,0:T(8,128)}, f32[56,256]{1,0:T(8,128)}, u32[]{:S(2)}, u32[]{:S(2)}) collective-permute-start(f32[56,256]{1,0:T(8,128)} %get-tuple-element.42), channel_id=1, source_target_pairs={{1,0},{2,1},{3,2},{4,3},{5,4},{6,5},{7,6},{9,8},{10,9},{11,10},{12... | collective-permute-start | bytes 172040 | tf_op jit(solution)/shard_map/ppermute | solution.py:372
  55.2 10.7 %collective-permute-start = (f32[56,256]{1,0:T(8,128)}, f32[56,256]{1,0:T(8,128)}, u32[]{:S(2)}, u32[]{:S(2)}) collective-permute-start(f32[56,256]{1,0:T(8,128)} %get-tuple-element.43), channel_id=1, source_target_pairs={{0,1},{1,2},{2,3},{3,4},{4,5},{5,6},{6,7},{8,9},{9,10},{10,11},{11... | collective-permute-start | bytes 172040 | tf_op jit(solution)/shard_map/ppermute | solution.py:371
  65.9 1.1 copy-start.1
  67.0 0.9 copy-start.6
  67.9 0.8 copy-start.11
  68.8 0.9 copy-start.16
  69.7 0.9 copy-start.29
  75.3 0.7 copy-start.41
  76.0 21.9 %all-to-all-start.2 = ((f32[32,16,128]{2,1,0:T(8,128)}), f32[32,16,128]{2,1,0:T(8,128)}, u32[]{:S(2)}, u32[]{:S(2)}) async-start(f32[32,16,128]{2,1,0:T(8,128)} %copy-done.41), calls=%async_computation.2 | async-start | bytes 524288 | tf_op jit(solution)/shard_map/all_to_all | solution.py:353
  86.7 4.3 %collective-permute-start.3 = (f32[56,256]{1,0:T(8,128)S(1)}, f32[56,256]{1,0:T(8,128)S(1)}, u32[]{:S(2)}, u32[]{:S(2)}) collective-permute-start(f32[56,256]{1,0:T(8,128)S(1)} %get-tuple-element.40), channel_id=1, source_target_pairs={{1,0},{2,1},{3,2},{4,3},{5,4},{6,5},{7,6},{9,8},{10,9},{11,10},{12... | collective-permute-start | bytes 172040 | tf_op jit(solution)/shard_map/ppermute | solution.py:372
  88.0 3.9 %collective-permute-start.2 = (f32[56,256]{1,0:T(8,128)S(1)}, f32[56,256]{1,0:T(8,128)S(1)}, u32[]{:S(2)}, u32[]{:S(2)}) collective-permute-start(f32[56,256]{1,0:T(8,128)S(1)} %get-tuple-element.41), channel_id=1, source_target_pairs={{0,1},{1,2},{2,3},{3,4},{4,5},{5,6},{6,7},{8,9},{9,10},{10,11},{11... | collective-permute-start | bytes 172040 | tf_op jit(solution)/shard_map/ppermute | solution.py:371
  97.9 1.1 copy-start.2
  99.0 0.9 copy-start.7
  99.9 0.8 copy-start.12
  100.7 0.9 copy-start.19
  101.6 0.9 copy-start.32
  102.5 0.8 copy-start.49
  103.3 0.8 copy-start.53
  108.2 0.7 copy-start.34
  108.9 0.7 copy-start.42
  109.6 17.6 %all-to-all-start.3 = ((f32[32,16,128]{2,1,0:T(8,128)}), f32[32,16,128]{2,1,0:T(8,128)}, u32[]{:S(2)}, u32[]{:S(2)}) async-start(f32[32,16,128]{2,1,0:T(8,128)} %copy-done.42), calls=%async_computation.3 | async-start | bytes 524288 | tf_op jit(solution)/shard_map/all_to_all | solution.py:353
  116.7 4.5 %collective-permute-start.5 = (f32[56,256]{1,0:T(8,128)S(1)}, f32[56,256]{1,0:T(8,128)S(1)}, u32[]{:S(2)}, u32[]{:S(2)}) collective-permute-start(f32[56,256]{1,0:T(8,128)S(1)} %get-tuple-element.38), channel_id=1, source_target_pairs={{1,0},{2,1},{3,2},{4,3},{5,4},{6,5},{7,6},{9,8},{10,9},{11,10},{12... | collective-permute-start | bytes 172040 | tf_op jit(solution)/shard_map/ppermute | solution.py:372
  118.0 3.9 %collective-permute-start.4 = (f32[56,256]{1,0:T(8,128)S(1)}, f32[56,256]{1,0:T(8,128)S(1)}, u32[]{:S(2)}, u32[]{:S(2)}) collective-permute-start(f32[56,256]{1,0:T(8,128)S(1)} %get-tuple-element.39), channel_id=1, source_target_pairs={{0,1},{1,2},{2,3},{3,4},{4,5},{5,6},{6,7},{8,9},{9,10},{10,11},{11... | collective-permute-start | bytes 172040 | tf_op jit(solution)/shard_map/ppermute | solution.py:371
  127.2 1.1 copy-start.3
  128.3 0.9 copy-start.8
  129.2 0.8 copy-start.13
  130.0 0.9 copy-start.22
  130.9 0.9 copy-start.35
  131.8 0.8 copy-start.47
  132.6 0.8 copy-start.51
  136.8 0.7 copy-start.24
  137.5 0.7 copy-start.40
  138.9 50.6 %copy-start.17 = (f32[112,256]{1,0:T(8,128)S(1)}, f32[112,256]{1,0:T(8,128)}, u32[]{:S(2)}) copy-start(f32[112,256]{1,0:T(8,128)} %copy-done.15) | copy-start | bytes 344068
  138.9 50.6 %copy-start.20 = (f32[112,256]{1,0:T(8,128)S(1)}, f32[112,256]{1,0:T(8,128)}, u32[]{:S(2)}) copy-start(f32[112,256]{1,0:T(8,128)} %copy-done.18) | copy-start | bytes 344068
  138.9 50.6 %copy-start.23 = (f32[112,256]{1,0:T(8,128)S(1)}, f32[112,256]{1,0:T(8,128)}, u32[]{:S(2)}) copy-start(f32[112,256]{1,0:T(8,128)} %copy-done.21) | copy-start | bytes 344068
  138.9 50.6 %copy-start.45 = (f32[64,256]{1,0:T(8,128)S(1)}, f32[64,256]{1,0:T(8,128)}, u32[]{:S(2)}) copy-start(f32[64,256]{1,0:T(8,128)} %constant.85.clone.average) | copy-start | bytes 196612
  138.9 75.9 %copy-start.27 = (f32[53,1,256]{2,0,1:T(8,128)S(1)}, f32[53,1,256]{2,0,1:T(8,128)}, u32[]{:S(2)}) copy-start(f32[53,1,256]{2,0,1:T(8,128)} %copy-done.26) | copy-start | bytes 162820
  138.9 75.9 %copy-start.37 = (f32[2,128,256]{2,1,0:T(8,128)S(1)}, f32[2,128,256]{2,1,0:T(8,128)}, u32[]{:S(2)}) copy-start(f32[2,128,256]{2,1,0:T(8,128)} %constant.86.clone.halves) | copy-start | bytes 786436
  138.9 17.8 %all-to-all-start.4 = ((f32[32,16,128]{2,1,0:T(8,128)}), f32[32,16,128]{2,1,0:T(8,128)S(1)}, u32[]{:S(2)}, u32[]{:S(2)}) async-start(f32[32,16,128]{2,1,0:T(8,128)} %copy-done.40), calls=%async_computation.4 | async-start | bytes 524288 | tf_op jit(solution)/shard_map/all_to_all | solution.py:353
  145.5 5.0 %collective-permute-start.7 = (f32[56,256]{1,0:T(8,128)S(1)}, f32[56,256]{1,0:T(8,128)S(1)}, u32[]{:S(2)}, u32[]{:S(2)}) collective-permute-start(f32[56,256]{1,0:T(8,128)S(1)} %get-tuple-element.36), channel_id=1, source_target_pairs={{1,0},{2,1},{3,2},{4,3},{5,4},{6,5},{7,6},{9,8},{10,9},{11,10},{12... | collective-permute-start | bytes 172040 | tf_op jit(solution)/shard_map/ppermute | solution.py:372
  146.8 4.5 %collective-permute-start.6 = (f32[56,256]{1,0:T(8,128)S(1)}, f32[56,256]{1,0:T(8,128)S(1)}, u32[]{:S(2)}, u32[]{:S(2)}) collective-permute-start(f32[56,256]{1,0:T(8,128)S(1)} %get-tuple-element.37), channel_id=1, source_target_pairs={{0,1},{1,2},{2,3},{3,4},{4,5},{5,6},{6,7},{8,9},{9,10},{10,11},{11... | collective-permute-start | bytes 172040 | tf_op jit(solution)/shard_map/ppermute | solution.py:371
  156.7 1.1 copy-start.4
  157.8 0.9 copy-start.9
  158.7 0.8 copy-start.14
  159.5 0.9 copy-start.25
  160.4 0.9 copy-start.30
  161.3 0.9 copy-start.33
  162.2 0.9 copy-start.36
  163.1 0.9 copy-start.44
  192.4 22.4 %all-to-all-start.6 = ((f32[32,32,128]{2,1,0:T(8,128)}), f32[32,32,128]{2,1,0:T(8,128)S(1)}, u32[]{:S(2)}, u32[]{:S(2)}) async-start(f32[32,32,128]{2,1,0:T(8,128)} %get-tuple-element.29), calls=%async_computation.6 | async-start | bytes 1048576 | tf_op jit(solution)/shard_map/all_to_all | solution.py:353
  (9 other events, 5.7 us)

commit v2 on v1

v2 whole, which is shorter than its diff:
```python
import functools

import jax
import jax.numpy as jnp
import numpy as np
from jax import lax
from jax.experimental import pallas as pl
from jax.experimental.pallas import tpu as pltpu
from jax.sharding import PartitionSpec as P

FS = 16
ITERS = 4
SHIFT = 1.0
HALF = FS // 2
FACE = FS * FS
PAD = 56
ROWS = 2 * PAD
SLOT = 40
EXACT = lax.Precision.HIGHEST
VMEM = pl.BlockSpec(memory_space=pltpu.VMEM)
SMEM = pl.BlockSpec(memory_space=pltpu.SMEM)

NN = (((1,), (0,)), ((), ()))
NT = (((1,), (1,)), ((), ()))
TN = (((0,), (0,)), ((), ()))


def mm(a, b, dims=NN):
    return lax.dot_general(a, b, dims, precision=EXACT, preferred_element_type=jnp.float32)


def two(value):
    high = value.astype(jnp.bfloat16)
    return high, (value - high.astype(jnp.float32)).astype(jnp.bfloat16)


def select(a, b):
    parts = jnp.concatenate(two(a), axis=0)
    got = lax.dot_general(parts, b, NN, preferred_element_type=jnp.float32)
    return got[: a.shape[0]] + got[a.shape[0] :]


def constants():
    cell = np.arange(FACE)
    y, z = cell // FS, cell % FS
    t = np.arange(FS)
    faces = np.zeros((4 * FS, FACE), np.float32)
    for f, lanes in enumerate((t, FACE - FS + t, t * FS, t * FS + FS - 1)):
        faces[f * FS + t, lanes] = 1.0
    inside = np.zeros((FACE, FACE), np.float32)
    for dy, dz in ((1, 0), (-1, 0), (0, 1), (0, -1)):
        ok = (y + dy >= 0) & (y + dy < FS) & (z + dz >= 0) & (z + dz < FS)
        inside[cell[ok], (y + dy)[ok] * FS + (z + dz)[ok]] = 1.0
    coarse = y // 2 * HALF + z // 2
    upsample = np.zeros((HALF * HALF, FACE), np.float32)
    upsample[coarse, cell] = 1.0
    halves = np.zeros((128, 2 * FACE), np.float32)
    for m in range(4):
        c = np.arange(32)
        halves[32 * m + c, 64 * m + c] = 1.0
        halves[32 * m + c, FACE + 64 * m + 32 + c] = 1.0
    return faces, inside, upsample * 0.125, halves


FACES, INSIDE, AVERAGE, HALVES = constants()


def call(kernel, name, shapes, args, specs, scratch=(), out_specs=None):
    return pl.pallas_call(
        kernel,
        out_shape=[
            jax.ShapeDtypeStruct(s[:-1], s[-1])
            if not isinstance(s[-1], int)
            else jax.ShapeDtypeStruct(s, jnp.float32)
            for s in shapes
        ],
        in_specs=specs,
        out_specs=out_specs or [VMEM] * len(shapes),
        scratch_shapes=list(scratch),
        compiler_params=pltpu.CompilerParams(vmem_limit_bytes=24 << 20),
        name=name,
    )(*args)


def split(value):
    high = value.astype(jnp.bfloat16)
    rest = value - high.astype(jnp.float32)
    middle = rest.astype(jnp.bfloat16)
    low = (rest - middle.astype(jnp.float32)).astype(jnp.bfloat16)
    return high, middle, low


def gather_kernel(ids, patch, lists, out, hot):
    species = patch.shape[0]
    row = lax.broadcasted_iota(jnp.int32, (species, FACE), 0)
    lane = lax.broadcasted_iota(jnp.int32, (species, FACE), 1)
    place = ((lane == row) | (lane == row + 192)).astype(jnp.float32)
    turned = mm(patch[:, 0, :], place, TN)
    parts = jnp.concatenate(
        [jnp.concatenate(split(turned[:, 128 * h : 128 * h + 128]), axis=1) for h in range(2)],
        axis=0,
    )
    entries = lists[:, 0, :].astype(jnp.float32) - (ids[0] * FACE).astype(jnp.float32)
    across = entries[:, 0:128].T
    beside = entries[:, 128:160].T
    entries = jnp.concatenate(
        [
            jnp.maximum(across[0:64], across[64:128]),
            jnp.maximum(beside[0:8], beside[8:16]),
            jnp.maximum(beside[16:24], beside[24:32]),
        ],
        axis=0,
    )
    cell = lax.broadcasted_iota(jnp.int32, (SLOT, FACE), 1).astype(jnp.float32)
    groups = out.shape[0]
    for g in range(0, groups, 2):
        pair = [
            jnp.concatenate(
                [
                    (cell == entries[SLOT * h : SLOT * h + SLOT, k : k + 1]).astype(jnp.float32)
                    for h in range(2)
                ],
                axis=1,
            )
            for k in (g, g + 1)
        ]
        hot[SLOT * g : SLOT * g + 2 * SLOT, :] = jnp.concatenate(pair, axis=0).astype(jnp.bfloat16)
    step = 8
    for g in range(0, groups, step):
        got = jnp.dot(
            hot[SLOT * g : SLOT * (g + step), :], parts, preferred_element_type=jnp.float32
        )
        got = got[:, 0:128] + got[:, 128:256] + got[:, 256:384]
        for k in range(step):
            out[g + k] = got[SLOT * k : SLOT * k + SLOT]


def prepare_kernel(ids, owned, diffusion, stoich, orders, scale, stoich_out, orders_out, sources):
    me = ids[0]
    found = [jnp.int32(-1)] * 4
    for g in range(owned.shape[1]):
        entry = owned[0, g]
        found = [jnp.where(entry == me * 4 + m, g, found[m]) for m in range(4)]
    for m in range(4):
        sources[m] = found[m]
    d = diffusion[...]
    species = d.shape[0]
    column = jnp.concatenate([d, jnp.zeros((PAD - species, 1), jnp.float32)], axis=0)

    def total(value):
        return jnp.sum(jnp.sum(value, axis=0, keepdims=True), axis=1, keepdims=True)

    wide = 1.0 + 12.0 * jnp.max(column, axis=0, keepdims=True)
    s, o = stoich[...], orders[...]
    wide = wide + jnp.sqrt(total(s * s)) * jnp.sqrt(total(o * o))
    unit = 32.0 / wide
    reactions = s.shape[1]
    high, low = two(jnp.concatenate([s * unit, jnp.zeros((PAD - species, reactions))], axis=0))
    stoich_out[...] = jnp.concatenate([high, low], axis=0)
    o = jnp.concatenate([o, jnp.zeros((PAD - species, reactions))], axis=0).T
    high, low = two(o)
    orders_out[...] = jnp.concatenate([high, high, low], axis=1)
    lane = lax.broadcasted_iota(jnp.int32, (PAD, 128), 1)
    row = lax.broadcasted_iota(jnp.int32, (PAD, 1), 0)
    diagonal = jnp.where(row < species, unit * (1.0 + 6.0 * column), 0.0)
    value = jnp.where(lane == 0, diagonal, 0.0)
    value = jnp.where(lane == 1, unit * column, value)
    value = jnp.where(lane == 2, SHIFT * unit, value)
    value = jnp.where(lane == 3, column, value)
    value = jnp.where(lane == 4, unit, value)
    scale[0:PAD, :] = value
    scale[PAD:, :] = value


def mix(a, b, keep, shift):
    return jnp.where(keep, a, b) + pltpu.roll(jnp.where(keep, b, a), shift, 0)


def apply_inverse(inv, rows, u):
    count, depth = inv.shape[0], inv.shape[1]
    full = depth // 8
    for half in range(2):
        lanes = slice(128 * half, 128 * half + 128)
        row = lax.broadcasted_iota(jnp.int32, (8, 128), 0)
        bit2, bit1, bit0 = (row & 4) == 0, (row & 2) == 0, (row & 1) == 0
        w = [rows[half, 8 * k : 8 * k + 8, :] for k in range(full + 1)]
        zero = jnp.zeros((8, 128), jnp.float32)

        def one(i):
            if i >= count:
                return zero
            m = inv[i, :, lanes].astype(jnp.float32)
            total = m[0:8] * w[0]
            for k in range(1, full):
                total = total + m[8 * k : 8 * k + 8] * w[k]
            last = m[8 * full : depth]
            last = jnp.concatenate([last, jnp.zeros((8 - last.shape[0], 128), jnp.float32)], axis=0)
            return total + last * w[full]

        for block in range(PAD // 8):
            a = [one(8 * block + d) for d in range(8)]
            b = [mix(a[d], a[d + 2], bit1, 6) for d in (0, 1, 4, 5)]
            c = [mix(b[d], b[d + 2], bit2, 4) for d in range(2)]
            u[8 * block : 8 * block + 8, lanes] = jnp.where(bit0, c[0], pltpu.roll(c[1], 1, 0))
            u[PAD + 8 * block : PAD + 8 * block + 8, lanes] = jnp.where(
                bit0, pltpu.roll(c[0], 7, 0), c[1]
            )


def interleave(rows, field):
    for half in range(2):
        lanes = slice(128 * half, 128 * half + 128)
        rows.at[half][pl.ds(0, PAD, stride=2), :] = field[:PAD, lanes]
        rows.at[half][pl.ds(1, PAD, stride=2), :] = field[PAD:, lanes]


def separate(rows):
    planes = [
        jnp.concatenate([rows.at[h][pl.ds(x, PAD, stride=2), :] for h in range(2)], axis=1)
        for x in range(2)
    ]
    return jnp.concatenate(planes, axis=0)


def flag(condition):
    return jnp.full((1, 1), condition, jnp.int32) != 0


def precondition(ids, inv, w, rows, u, near, far):
    interleave(rows, w)
    apply_inverse(inv, rows, u)

    @pl.when(ids[1] % 2 == 0)
    def _():
        near[...] = u[PAD:]
        far[...] = u[:PAD]

    @pl.when(ids[1] % 2 == 1)
    def _():
        near[...] = u[:PAD]
        far[...] = u[PAD:]


def first_kernel(ids, links, received, source, scale, inv, w_out, near, far, u, rows):
    values = received[0]
    for g in range(1, received.shape[0]):
        values = values + received[g]
    me = ids[0]
    row = lax.broadcasted_iota(jnp.int32, (SLOT, FACE), 0)
    cell = lax.broadcasted_iota(jnp.int32, (SLOT, FACE), 1)
    y, z = cell // FS, cell % FS
    coarse = y // 2 * HALF + z // 2
    first = 64 - SLOT
    y_face = jnp.where(links[0, me] < 0, 0, FS - 1)
    z_face = jnp.where(links[2, me] < 0, 0, FS - 1)
    sides = ((y == y_face) & (row == first + z // 2)).astype(jnp.float32)
    sides = sides + ((z == z_face) & (row == first + HALF + y // 2)).astype(jnp.float32)
    faces = [coarse == row, (coarse == row + SLOT) & (row < first)]
    faces = [face.astype(jnp.float32) for face in faces]
    across = mm(values, jnp.concatenate([faces[0], faces[1], sides], axis=1), TN)
    beside = across[64 : 64 + PAD, 2 * FACE :]
    across = across[0:PAD, :FACE] + across[64 : 64 + PAD, FACE : 2 * FACE]
    bottom = flag(ids[1] == 0)
    boundary = jnp.concatenate(
        [beside + jnp.where(bottom, across, 0.0), beside + jnp.where(bottom, 0.0, across)], axis=0
    )
    species = source.shape[0]
    for half in range(2):
        rows[half, 0:species, :] = source[:, 128 * half : 128 * half + 128]
        rows[half, species:ROWS, :] = jnp.zeros((ROWS - species, 128), jnp.float32)
    right = separate(rows) + scale[:, 3:4] * boundary
    w_out[...] = right
    precondition(ids, inv, right, rows, u, near, far)


def dots(vectors, last, line):
    lane = lax.broadcasted_iota(jnp.int32, (1, 128), 1)
    count = len(vectors)
    for b, vector in enumerate(vectors + [last]):
        part = jnp.sum(last * vector, axis=0, keepdims=True)
        part = jnp.sum(part, axis=1, keepdims=True)
        line = jnp.where(lane == count * (count + 1) // 2 + b, part, line)
    return line


def local_kernel(j, ids, links, *refs):
    u, scale, inside, faces, orders, stoich, rates = refs[:7]
    basis = refs[7 : 8 + j]
    part, slots, line_out = refs[-3:]
    line = refs[8 + j][...] if j else jnp.zeros((1, 128), jnp.float32)
    me = ids[0]
    field = u[...]
    lower, upper = field[:PAD], field[PAD:]
    face = faces[...].astype(jnp.bfloat16)
    planes = lax.dot_general(
        jnp.concatenate([face, face], axis=1),
        jnp.concatenate(two(field), axis=1),
        NT,
        preferred_element_type=jnp.float32,
    )
    for f in range(4):
        other = links[f, me]
        slots[jnp.where(other < 0, me, other), :, 0:ROWS] = planes[FS * f : FS * f + FS]
    total = select(field, inside[...].astype(jnp.bfloat16))
    total = total + jnp.concatenate([field[PAD:], field[:PAD]], axis=0)
    both = jnp.concatenate([lower, upper], axis=1)
    high, low = two(both)
    progress = jnp.dot(
        orders[...], jnp.concatenate([high, low, high], axis=0), preferred_element_type=jnp.float32
    )
    high, low = two(progress * rates[...])
    chemistry = jnp.dot(stoich[...], high, preferred_element_type=jnp.float32)
    chemistry = chemistry[:PAD] + chemistry[PAD:]
    chemistry = chemistry + jnp.dot(stoich[:PAD, :], low, preferred_element_type=jnp.float32)
    chemistry = jnp.concatenate([chemistry[:, :FACE], chemistry[:, FACE:]], axis=0)
    w = basis[-1][...]
    part[...] = scale[:, 0:1] * field - scale[:, 1:2] * total - chemistry - scale[:, 2:3] * w
    line_out[...] = dots([ref[...] for ref in basis[:-1]], w, line)


def image_of(ids, links, received, near, far, part, scale, faces):
    me = ids[0]
    even = (ids[1] % 2 == 0).astype(jnp.float32)
    end = jnp.logical_or(ids[1] == 0, ids[1] == ids[2])
    live = jnp.where(end, 0.0, 1.0)
    low = (1.0 - even) * near[...] + (even * live) * far[...]
    high = even * near[...] + ((1.0 - even) * live) * far[...]
    ghosts = []
    for f in range(4):
        other = links[f, me]
        plane = received[jnp.where(other < 0, me, other), :, 0:ROWS]
        ghosts.append(jnp.where(other < 0, 0.0, 1.0) * plane)
    face = faces[...].astype(jnp.bfloat16)
    total = lax.dot_general(
        jnp.concatenate(two(jnp.concatenate(ghosts, axis=0)), axis=0),
        jnp.concatenate([face, face], axis=0),
        TN,
        preferred_element_type=jnp.float32,
    )
    total = total + jnp.concatenate([low, high], axis=0)
    return part[...] - scale[:, 1:2] * total


def combine_kernel(ids, links, received, near_in, far_in, part, scale, faces, inv, w_out, near, far, u, rows):
    image = image_of(ids, links, received, near_in, far_in, part, scale, faces)
    w_out[...] = image
    precondition(ids, inv, image, rows, u, near, far)


def last_kernel(ids, links, received, near, far, part, scale, faces, w0, w1, w2, w3, line, out):
    image = image_of(ids, links, received, near, far, part, scale, faces)
    result = dots([w0[...], w1[...], w2[...], w3[...]], image, line[...])
    out[...] = jnp.broadcast_to(result, out.shape)


def solve(gram, shift):
    def g(a, b):
        return gram[(max(a, b), min(a, b))]

    n = ITERS
    target = [g(a + 1, 0) + shift * g(a, 0) for a in range(n)]
    normal = {}
    for a in range(n):
        for b in range(a + 1):
            normal[a, b] = (
                g(a + 1, b + 1) + shift * (g(a + 1, b) + g(a, b + 1)) + shift * shift * g(a, b)
            )
    size = [lax.rsqrt(normal[a, a]) for a in range(n)]
    target = [target[a] * size[a] for a in range(n)]
    lower = {}
    inverse = [None] * n
    for a in range(n):
        for b in range(a + 1):
            value = normal[a, b] * size[a] * size[b]
            for c in range(b):
                value = value - lower[a, c] * lower[b, c]
            if a == b:
                inverse[a] = lax.rsqrt(value)
            else:
                lower[a, b] = value * inverse[b]
    half = []
    for a in range(n):
        value = target[a]
        for c in range(a):
            value = value - lower[a, c] * half[c]
        half.append(value * inverse[a])
    result = [None] * n
    for a in reversed(range(n)):
        value = half[a]
        for c in range(a + 1, n):
            value = value - lower[c, a] * result[c]
        result[a] = value * inverse[a]
    return [result[a] * size[a] for a in range(n)]


def finish_kernel(ids, owned, lines, *refs):
    fields = refs[:ITERS]
    scale, average, correction, slots, rows = refs[ITERS:]
    line = jnp.sum(lines[...], axis=0, keepdims=True)
    gram = {}
    k = 0
    for a in range(ITERS + 1):
        for b in range(a + 1):
            gram[a, b] = line[:, k : k + 1]
            k += 1
    weights = solve(gram, scale[0:1, 2:3])
    factor = scale[0:1, 4:5]
    total = (weights[0] * factor) * fields[0][...]
    for weight, field in zip(weights[1:], fields[1:]):
        total = total + (weight * factor) * field[...]
    interleave(rows, total)
    for half in range(2):
        lanes = slice(128 * half, 128 * half + 128)
        correction[:, lanes] = rows[half, 0 : correction.shape[0], :]
    summed = total[:PAD] + total[PAD:]
    blank = jnp.zeros((64 - PAD, FACE), jnp.float32)
    spread = jnp.concatenate([summed, blank, summed, blank], axis=0)
    weight = average[...].astype(jnp.bfloat16)
    mean = lax.dot_general(
        jnp.concatenate([weight, weight], axis=1),
        jnp.concatenate(two(spread), axis=1),
        NT,
        preferred_element_type=jnp.float32,
    )
    lane = lax.broadcasted_iota(jnp.int32, (32, 128), 1)
    slots[owned[0, ids[0]] // 4] = jnp.where(lane < 64, mean[:32], mean[32:])


def update_kernel(sources, received, patch, halves, out, stacked):
    lane = lax.broadcasted_iota(jnp.int32, (1, FACE), 1)
    covered = jnp.zeros((1, FACE), jnp.int32)
    for m in range(4):
        source = sources[m]
        here = slice(32 * m, 32 * m + 32)

        @pl.when(source >= 0)
        def _():
            stacked[here, :] = received[source]

        @pl.when(source < 0)
        def _():
            stacked[here, :] = jnp.zeros((32, 128), jnp.float32)

        covered = jnp.where(lane // 64 == m, source, covered)
    species = patch.shape[0]
    half = halves[...].astype(jnp.bfloat16)
    got = lax.dot_general(
        jnp.concatenate(two(stacked[...]), axis=0),
        jnp.concatenate([half, half], axis=0),
        TN,
        preferred_element_type=jnp.float32,
    )
    got = got[0:species, :FACE] + got[64 : 64 + species, FACE:]
    out[:, 0, :] = jnp.where(covered >= 0, got, patch[...])


def on_device(
    source_term,
    diffusion,
    stoich,
    orders,
    rates,
    precond,
    coarse_field,
    neighbours,
    ghost_list,
    average_list,
):
    species, reactions = stoich.shape
    groups = lax.axis_size("grp")
    boxes = lax.axis_size("box")
    me = lax.axis_index("grp")
    box = lax.axis_index("box")
    f32 = jnp.float32
    barrier = lax.optimization_barrier

    ids = jnp.stack([me, box, jnp.asarray(boxes - 1, box.dtype)]).astype(jnp.int32)
    links = neighbours.T
    owned = average_list.T
    even_swap = [(i, i ^ 1) for i in range(boxes)]
    odd_swap = [(i, (i + (1 if i % 2 else -1)) % boxes) for i in range(boxes)]

    def exchange(slots):
        return lax.all_to_all(slots, "grp", 0, 0, tiled=True)

    (asked,) = call(
        gather_kernel, "gather", [(groups, SLOT, 128)], (ids, coarse_field, ghost_list), [SMEM] + [VMEM] * 2,
        [pltpu.VMEM((groups * SLOT, 2 * FACE), jnp.bfloat16)],
    )
    received = exchange(asked)
    scale, stoich_s, orders_s, sources = call(
        prepare_kernel,
        "prepare",
        [(ROWS, 128), (2 * PAD, reactions, jnp.bfloat16), (reactions, 3 * PAD, jnp.bfloat16), (4, jnp.int32)],
        (ids, owned, diffusion.reshape(species, 1), stoich, orders.T),
        [SMEM] * 2 + [VMEM] * 3,
        (),
        [VMEM] * 3 + [SMEM],
    )
    rates_s = rates.reshape(reactions, 2 * FACE)
    inverse = precond.reshape(species, 2 * species, FACE)
    source = source_term.reshape(2 * species, FACE)
    faces = jnp.asarray(FACES)
    inside = jnp.asarray(INSIDE)
    outs = [(ROWS, FACE), (PAD, FACE), (PAD, FACE), (ROWS, FACE)]
    rows = [pltpu.VMEM((2, ROWS, 128), f32)]
    w, near, far, u = call(
        first_kernel,
        "first",
        outs,
        (ids, links, received, source, scale, inverse),
        [SMEM] * 2 + [VMEM] * 4,
        rows,
    )
    basis, directions = [w], [u]
    line = ()
    for j in range(ITERS):
        near_in = lax.ppermute(near, "box", even_swap)
        far_in = lax.ppermute(far, "box", odd_swap)
        part, slots, line = call(
            functools.partial(local_kernel, j),
            "local%d" % j,
            [(ROWS, FACE), (groups, FS, 128), (1, 128)],
            (ids, links, u, scale, inside, faces, orders_s, stoich_s, rates_s)
            + tuple(basis)
            + ((line,) if j else ()),
            [SMEM] * 2 + [VMEM] * (9 + j if j else 8),
        )
        slots, near_in, far_in, part, line = barrier((slots, near_in, far_in, part, line))
        received = exchange(slots)
        received, near_in, far_in, part, line = barrier((received, near_in, far_in, part, line))
        shared = (ids, links, received, near_in, far_in, part, scale, faces)
        if j + 1 < ITERS:
            w, near, far, u = call(
                combine_kernel,
                "combine%d" % j,
                outs,
                shared + (inverse,),
                [SMEM] * 2 + [VMEM] * 7,
                rows,
            )
            basis.append(w)
            directions.append(u)
        else:
            (lines,) = call(
                last_kernel,
                "last",
                [(groups * boxes, 128)],
                shared + tuple(basis) + (line,),
                [SMEM] * 2 + [VMEM] * 11,
            )
    lines = lax.all_to_all(lines, ("grp", "box"), 0, 0, tiled=True)
    correction, slots = call(
        finish_kernel,
        "finish",
        [(2 * species, FACE), (groups, 32, 128)],
        (ids, owned, lines) + tuple(directions) + (scale, jnp.asarray(AVERAGE)),
        [SMEM] * 2 + [VMEM] * 7,
        rows,
    )
    received = exchange(slots)
    (updated,) = call(
        update_kernel,
        "update",
        [(species, 1, FACE)],
        (sources, received, coarse_field.reshape(species, FACE), jnp.asarray(HALVES)),
        [SMEM] + [VMEM] * 3,
        [pltpu.VMEM((128, 128), f32)],
    )
    return correction.reshape(species, 1, 2, FACE), updated


def solution(mesh):
    placed = (
        P(None, "grp", "box", None),
        P(),
        P(),
        P(),
        P(None, "grp", "box", None),
        P(None, None, "grp", "box", None),
        P(None, "grp", "box"),
        P(),
        P(None, "box", None),
        P(None, "box"),
    )
    return jax.shard_map(
        on_device,
        mesh=mesh,
        in_specs=placed,
        out_specs=(P(None, "grp", "box", None), P(None, "grp", "box")),
        check_vma=False,
    )
```

time: 219 us -> 179 us (0.82)
  blocking collectives: 23.2 us -> 83.2 us
  local copies, waits for them, and re-layouts: 56.4 us -> 11.2 us
  starting transfers between devices: 62.9 us -> 32.3 us
  waiting for transfers between devices: 44.6 us -> 28.9 us
  between operations: 5.84 us -> 0.93 us
  other arithmetic: 2.92 us -> 0.08 us
    all_to_all x0 -> x4, blocking collectives: none -> 61.5 us  [exchange(): return lax.all_to_all(slots, 'grp', 0, 0, tiled=True)]
    unnamed x124 -> x29, local copies, waits for them, and re-layouts: 42.2 us -> 3.67 us
    all_to_all x6 -> x2, starting transfers between devices: 44.2 us -> 16.7 us  [exchange(): return lax.all_to_all(slots, 'grp', 0, 0, tiled=True)]
    all_to_all x6 -> x2, waiting for transfers between devices: 43.4 us -> 26.3 us  [exchange(): return lax.all_to_all(slots, 'grp', 0, 0, tiled=True)]
    slice x5 -> x0, local copies, waits for them, and re-layouts: 4.07 us -> none  [the longest x4 4.06 us: on_device(): high = lax.ppermute(u[:PAD], 'box', [(i + 1, i) for i in range(boxes - 1)])]
    ppermute x8, starting transfers between devices: 18.7 us -> 15.6 us  [the longest x4 15.2 us: on_device(): far_in = lax.ppermute(far, 'box', odd_swap)]
    pad x3 -> x0, local copies, waits for them, and re-layouts: 2.47 us -> none  [the longest x1 1.53 us: on_device(): stoich_s = jnp.pad(stoich * unit, ((0, PAD - species), (0, 0)))]
    pallas_call x8 -> x13, Pallas kernels: 20.6 us -> 21.3 us  [call(): pl.pallas_call(kernel, out_shape=[jax.ShapeDtypeStruct(s[:-1], s[-1]) if...]
  transfers between devices with their start and end apart: 14 -> 10, of which waited for: 8 -> 6; matrix products, arithmetic and copies ran while one was open for 10% -> 4% of each run, Pallas kernels for 0% -> 3%
where the time goes in v2:
time: 179 us; the launch traced here: 178 us
  blocking collectives  83.2 us (46%)
  starting transfers between devices  32.3 us (18%)
  waiting for transfers between devices  28.9 us (16%)
  Pallas kernels  21.3 us (12%)
  local copies, waits for them, and re-layouts  11.2 us (6%)
    all_to_all x4, blocking collectives, exchange(): return lax.all_to_all(slots, 'grp', 0, 0, tiled=True)  61.5 us
    all_to_all x2, waiting for transfers between devices, exchange(): return lax.all_to_all(slots, 'grp', 0, 0, tiled=True)  26.3 us
    all_to_all x1, blocking collectives, on_device(): lines = lax.all_to_all(lines, ('grp', 'box'), 0, 0, tiled=True)  21.6 us
    pallas_call x13, Pallas kernels, call(): pl.pallas_call(kernel, out_shape=[jax.ShapeDtypeStruct(s[:-1], s[-1]) if...  21.3 us
    all_to_all x2, starting transfers between devices, exchange(): return lax.all_to_all(slots, 'grp', 0, 0, tiled=True)  16.7 us
    ppermute x4, starting transfers between devices, on_device(): far_in = lax.ppermute(far, 'box', odd_swap)  15.2 us
    reshape x1, local copies, waits for them, and re-layouts, on_device(): inverse = precond.reshape(species, 2 * species, FACE)  5.92 us
    unnamed x29, local copies, waits for them, and re-layouts  3.67 us
  transfers between devices with their start and end apart: 10, of which 6 were waited for; matrix products, arithmetic and copies ran while one was open for 4% of the time, Pallas kernels for 3%

profile of v2, /device:TPU:2, one launch (start us, length us, event | category | flops | bytes accessed | tf_op | source)
XLA Modules:
  0.0 177.8 jit_solution(9256286067199238373)
XLA Ops:
  0.6 0.1 pad_add_fusion.ids
  0.7 0.0 copy-start.3
  0.7 0.8 copy-done.3
  1.5 0.0 copy-start.9
  1.5 0.8 copy-done.9
  2.3 3.0 %gather.1 = f32[32,40,128]{2,1,0:T(8,128)} custom-call(s32[3]{0:T(128)S(1)} %pad_add_fusion.ids, f32[53,1,256]{2,1,0:T(1,128)S(1)} %copy-done.3, s32[32,1,160]{2,1,0:T(1,128)S(1)} %copy-done.9), custom_call_target="tpu_custom_call" | custom-call | tf_op jit(solution)/shard_map/gather/pallas_call | solution.py:69
  5.3 11.7 %all-to-all-start = ((f32[32,40,128]{2,1,0:T(8,128)}), f32[32,40,128]{2,1,0:T(8,128)}, u32[]{:S(2)}, u32[]{:S(2)}) async-start(f32[32,40,128]{2,1,0:T(8,128)} %gather.1), calls=%async_computation | async-start | bytes 1310720 | tf_op jit(solution)/shard_map/all_to_all | solution.py:484
  17.0 0.0 copy-start.12
  17.0 0.8 copy.18.diffusion
  17.8 0.0 copy-start.10
  17.8 5.9 %reshape.26.inv = bf16[53,106,256]{2,1,0:T(8,128)(2,1)S(1)} reshape(bf16[53,53,1,2,256]{4,3,2,1,0:T(2,128)(2,1)} %param.19) | data formatting | bytes 5752832 | tf_op jit(solution)/shard_map/reshape | solution.py:501
  23.7 0.0 copy-done.12
  23.7 0.1 reshape.24.source
  23.8 0.0 copy-done.10
  23.8 0.0 copy-start.6
  23.8 0.9 copy-done.6
  24.7 0.9 copy-done.7
  25.6 1.4 prepare.1
  27.0 9.6 %all-to-all-done.received = f32[32,40,128]{2,1,0:T(8,128)} async-done(((f32[32,40,128]{2,1,0:T(8,128)}), f32[32,40,128]{2,1,0:T(8,128)}, u32[]{:S(2)}, u32[]{:S(2)}) %all-to-all-start) | async-done | bytes 655392 | tf_op jit(solution)/shard_map/all_to_all | solution.py:484
  36.7 0.0 copy-done.5
  36.7 2.6 %first.1 = (f32[112,256]{1,0:T(8,128)S(1)}, f32[56,256]{1,0:T(8,128)S(1)}, f32[56,256]{1,0:T(8,128)S(1)}, f32[112,256]{1,0:T(8,128)S(1)}) custom-call(s32[3]{0:T(128)S(1)} %pad_add_fusion.ids, s32[4,32]{1,0:T(4,128)S(1)} %bitcast.25, f32[32,40,128]{2,1,0:T(8,128)} %all-to-all-done.received, f32[106,256]{1,0:T(8,128)S(1)} %reshape.24.source, ...), custom_call_target="tpu_custom_call" | custom-call | tf_op jit(solution)/shard_map/first/pallas_call | solution.py:69
  39.2 0.1 collective-permute-start
  39.3 3.1 %collective-permute-start.1 = (f32[56,256]{1,0:T(8,128)S(1)}, f32[56,256]{1,0:T(8,128)S(1)}, u32[]{:S(2)}, u32[]{:S(2)}) collective-permute-start(f32[56,256]{1,0:T(8,128)S(1)} %get-tuple-element.83), channel_id=1, source_target_pairs={{0,7},{1,2},{2,1},{3,4},{4,3},{5,6},{6,5},{7,0},{8,15},{9,10},{10,... | collective-permute-start | bytes 172040 | tf_op jit(solution)/shard_map/ppermute | solution.py:519
  42.4 0.0 copy-done.11
  42.5 0.2 pad.3
  42.7 0.0 copy-done
  42.8 0.0 copy-done.1
  42.8 1.1 local0.1
  43.9 0.0 collective-permute-done.near_in
  43.9 0.4 collective-permute-done.1.far_in
  44.3 15.8 %all_to_all.41.received = f32[32,16,128]{2,1,0:T(8,128)S(1)} all-to-all(f32[32,16,128]{2,1,0:T(8,128)S(1)} %get-tuple-element.86), channel_id=1, replica_groups=mesh['grp'=32,'box'=8] {'grp'}, dimensions={0} | all-to-all | bytes 524288 | tf_op jit(solution)/shard_map/all_to_all | solution.py:484
  60.2 1.6 combine0.1
  61.8 0.1 collective-permute-start.2
  61.9 3.5 %collective-permute-start.3 = (f32[56,256]{1,0:T(8,128)S(1)}, f32[56,256]{1,0:T(8,128)S(1)}, u32[]{:S(2)}, u32[]{:S(2)}) collective-permute-start(f32[56,256]{1,0:T(8,128)S(1)} %get-tuple-element.100), channel_id=1, source_target_pairs={{0,7},{1,2},{2,1},{3,4},{4,3},{5,6},{6,5},{7,0},{8,15},{9,10},{10,... | collective-permute-start | bytes 172040 | tf_op jit(solution)/shard_map/ppermute | solution.py:519
  65.4 1.1 local1.1
  66.5 0.0 collective-permute-done.2.near_in
  66.5 0.7 collective-permute-done.3.far_in
  67.2 15.5 %all_to_all.42.received = f32[32,16,128]{2,1,0:T(8,128)S(1)} all-to-all(f32[32,16,128]{2,1,0:T(8,128)S(1)} %get-tuple-element.103), channel_id=1, replica_groups=mesh['grp'=32,'box'=8] {'grp'}, dimensions={0} | all-to-all | bytes 524288 | tf_op jit(solution)/shard_map/all_to_all | solution.py:484
  82.7 1.6 combine1.1
  84.3 0.1 collective-permute-start.4
  84.4 4.1 %collective-permute-start.5 = (f32[56,256]{1,0:T(8,128)S(1)}, f32[56,256]{1,0:T(8,128)S(1)}, u32[]{:S(2)}, u32[]{:S(2)}) collective-permute-start(f32[56,256]{1,0:T(8,128)S(1)} %get-tuple-element.117), channel_id=1, source_target_pairs={{0,7},{1,2},{2,1},{3,4},{4,3},{5,6},{6,5},{7,0},{8,15},{9,10},{10,... | collective-permute-start | bytes 172040 | tf_op jit(solution)/shard_map/ppermute | solution.py:519
  88.5 1.1 local2.1
  89.6 0.0 collective-permute-done.4.near_in
  89.6 0.7 collective-permute-done.5.far_in
  90.4 15.2 %all_to_all.43.received = f32[32,16,128]{2,1,0:T(8,128)S(1)} all-to-all(f32[32,16,128]{2,1,0:T(8,128)S(1)} %get-tuple-element.120), channel_id=1, replica_groups=mesh['grp'=32,'box'=8] {'grp'}, dimensions={0} | all-to-all | bytes 524288 | tf_op jit(solution)/shard_map/all_to_all | solution.py:484
  105.6 1.6 combine2.1
  107.2 0.0 copy-start.4
  107.2 0.0 copy-start.2
  107.2 0.1 collective-permute-start.6
  107.3 4.5 %collective-permute-start.7 = (f32[56,256]{1,0:T(8,128)S(1)}, f32[56,256]{1,0:T(8,128)S(1)}, u32[]{:S(2)}, u32[]{:S(2)}) collective-permute-start(f32[56,256]{1,0:T(8,128)S(1)} %get-tuple-element.134), channel_id=1, source_target_pairs={{0,7},{1,2},{2,1},{3,4},{4,3},{5,6},{6,5},{7,0},{8,15},{9,10},{10,... | collective-permute-start | bytes 172040 | tf_op jit(solution)/shard_map/ppermute | solution.py:519
  111.8 1.1 local3.1
  112.9 0.0 collective-permute-done.6.near
  112.9 0.7 collective-permute-done.7.far
  113.6 15.0 %all_to_all.44.received = f32[32,16,128]{2,1,0:T(8,128)S(1)} all-to-all(f32[32,16,128]{2,1,0:T(8,128)S(1)} %get-tuple-element.137), channel_id=1, replica_groups=mesh['grp'=32,'box'=8] {'grp'}, dimensions={0} | all-to-all | bytes 524288 | tf_op jit(solution)/shard_map/all_to_all | solution.py:484
  128.7 0.9 last.1
  129.6 21.6 %all_to_all.45 = f32[256,1,128]{2,1,0:T(1,128)S(1)} all-to-all(f32[256,1,128]{2,1,0:T(1,128)S(1)} %bitcast.23), channel_id=1, replica_groups=mesh['grp'=32,'box'=8] {'grp','box'}, dimensions={0} | all-to-all | bytes 262144 | tf_op jit(solution)/shard_map/all_to_all | solution.py:552
  151.2 0.0 copy-done.8
  151.2 2.8 %finish.1 = (f32[106,256]{1,0:T(8,128)S(1)}, f32[32,32,128]{2,1,0:T(8,128)}) custom-call(s32[3]{0:T(128)S(1)} %pad_add_fusion.ids, s32[1,32]{1,0:T(1,128)S(1)} %bitcast.36, f32[256,128]{1,0:T(8,128)S(1)} %bitcast.22, f32[112,256]{1,0:T(8,128)S(1)} %get-tuple-element.77.refs_0_, f32[112,256]{1,0:T(8,128)S(1)} %get-tuple-element.95.refs_0_.refs_1_, ...), custom_call_target="tpu_custom_call" | custom-call | tf_op jit(solution)/shard_map/finish/pallas_call | solution.py:69
  154.0 5.0 %all-to-all-start.6 = ((f32[32,32,128]{2,1,0:T(8,128)}), f32[32,32,128]{2,1,0:T(8,128)S(1)}, u32[]{:S(2)}, u32[]{:S(2)}) async-start(f32[32,32,128]{2,1,0:T(8,128)} %get-tuple-element.149), calls=%async_computation.6 | async-start | bytes 1048576 | tf_op jit(solution)/shard_map/all_to_all | solution.py:484
  159.0 0.0 copy-done.4
  159.0 0.7 reshape.28
  159.7 16.6 %all-to-all-done.6.received = f32[32,32,128]{2,1,0:T(8,128)S(1)} async-done(((f32[32,32,128]{2,1,0:T(8,128)}), f32[32,32,128]{2,1,0:T(8,128)S(1)}, u32[]{:S(2)}, u32[]{:S(2)}) %all-to-all-start.6) | async-done | bytes 524320 | tf_op jit(solution)/shard_map/all_to_all | solution.py:484
  176.4 0.0 copy-done.2
  176.4 1.4 update.1
  (8 shorter events, 0.1 us)
Async XLA Ops:
  0.7 0.8 copy-start.3
  1.5 0.8 copy-start.9
  5.3 31.4 %all-to-all-start = ((f32[32,40,128]{2,1,0:T(8,128)}), f32[32,40,128]{2,1,0:T(8,128)}, u32[]{:S(2)}, u32[]{:S(2)}) async-start(f32[32,40,128]{2,1,0:T(8,128)} %gather.1), calls=%async_computation | async-start | bytes 1310720 | tf_op jit(solution)/shard_map/all_to_all | solution.py:484
  17.0 6.7 %copy-start.12 = (f32[53,1,2,256]{3,2,1,0:T(2,128)S(1)}, f32[53,1,2,256]{3,2,1,0:T(2,128)}, u32[]{:S(2)}) copy-start(f32[53,1,2,256]{3,2,1,0:T(2,128)} %param.14) | copy-start | bytes 325636
  17.8 6.0 %copy-start.10 = (s32[32,1]{0,1:T(1,128)S(1)}, s32[32,1]{0,1:T(1,128)}, u32[]{:S(2)}) copy-start(s32[32,1]{0,1:T(1,128)} %param.23) | copy-start | bytes 388
  17.8 18.9 %copy-start.5 = (s32[32,4]{0,1:T(4,128)S(1)}, s32[32,4]{0,1:T(4,128)}, u32[]{:S(2)}) copy-start(s32[32,4]{0,1:T(4,128)} %param.21) | copy-start | bytes 1540
  23.8 0.9 copy-start.6
  24.7 0.9 copy-start.7
  36.7 5.8 %copy-start.11 = (f32[325,1,2,256]{3,2,1,0:T(2,128)S(1)}, f32[325,1,2,256]{3,2,1,0:T(2,128)}, u32[]{:S(2)}) copy-start(f32[325,1,2,256]{3,2,1,0:T(2,128)} %param.18) | copy-start | bytes 1996804
  36.7 6.1 %copy-start = (f32[64,256]{1,0:T(8,128)S(1)}, f32[64,256]{1,0:T(8,128)}, u32[]{:S(2)}) copy-start(f32[64,256]{1,0:T(8,128)} %constant.19.clone.refs_3_.faces) | copy-start | bytes 196612
  36.7 6.1 %copy-start.1 = (f32[256,256]{1,0:T(8,128)S(1)}, f32[256,256]{1,0:T(8,128)}, u32[]{:S(2)}) copy-start(f32[256,256]{1,0:T(8,128)} %constant.20.clone.refs_2_) | copy-start | bytes 786436
  39.2 4.6 %collective-permute-start = (f32[56,256]{1,0:T(8,128)S(1)}, f32[56,256]{1,0:T(8,128)S(1)}, u32[]{:S(2)}, u32[]{:S(2)}) collective-permute-start(f32[56,256]{1,0:T(8,128)S(1)} %get-tuple-element.82), channel_id=1, source_target_pairs={{0,1},{1,0},{2,3},{3,2},{4,5},{5,4},{6,7},{7,6},{8,9},{9,8},{10,11... | collective-permute-start | bytes 172040 | tf_op jit(solution)/shard_map/ppermute | solution.py:518
  39.3 5.0 %collective-permute-start.1 = (f32[56,256]{1,0:T(8,128)S(1)}, f32[56,256]{1,0:T(8,128)S(1)}, u32[]{:S(2)}, u32[]{:S(2)}) collective-permute-start(f32[56,256]{1,0:T(8,128)S(1)} %get-tuple-element.83), channel_id=1, source_target_pairs={{0,7},{1,2},{2,1},{3,4},{4,3},{5,6},{6,5},{7,0},{8,15},{9,10},{10,... | collective-permute-start | bytes 172040 | tf_op jit(solution)/shard_map/ppermute | solution.py:519
  61.8 4.7 %collective-permute-start.2 = (f32[56,256]{1,0:T(8,128)S(1)}, f32[56,256]{1,0:T(8,128)S(1)}, u32[]{:S(2)}, u32[]{:S(2)}) collective-permute-start(f32[56,256]{1,0:T(8,128)S(1)} %get-tuple-element.99), channel_id=1, source_target_pairs={{0,1},{1,0},{2,3},{3,2},{4,5},{5,4},{6,7},{7,6},{8,9},{9,8},{10,11... | collective-permute-start | bytes 172040 | tf_op jit(solution)/shard_map/ppermute | solution.py:518
  61.9 5.4 %collective-permute-start.3 = (f32[56,256]{1,0:T(8,128)S(1)}, f32[56,256]{1,0:T(8,128)S(1)}, u32[]{:S(2)}, u32[]{:S(2)}) collective-permute-start(f32[56,256]{1,0:T(8,128)S(1)} %get-tuple-element.100), channel_id=1, source_target_pairs={{0,7},{1,2},{2,1},{3,4},{4,3},{5,6},{6,5},{7,0},{8,15},{9,10},{10,... | collective-permute-start | bytes 172040 | tf_op jit(solution)/shard_map/ppermute | solution.py:519
  84.3 5.3 %collective-permute-start.4 = (f32[56,256]{1,0:T(8,128)S(1)}, f32[56,256]{1,0:T(8,128)S(1)}, u32[]{:S(2)}, u32[]{:S(2)}) collective-permute-start(f32[56,256]{1,0:T(8,128)S(1)} %get-tuple-element.116), channel_id=1, source_target_pairs={{0,1},{1,0},{2,3},{3,2},{4,5},{5,4},{6,7},{7,6},{8,9},{9,8},{10,11... | collective-permute-start | bytes 172040 | tf_op jit(solution)/shard_map/ppermute | solution.py:518
  84.4 6.0 %collective-permute-start.5 = (f32[56,256]{1,0:T(8,128)S(1)}, f32[56,256]{1,0:T(8,128)S(1)}, u32[]{:S(2)}, u32[]{:S(2)}) collective-permute-start(f32[56,256]{1,0:T(8,128)S(1)} %get-tuple-element.117), channel_id=1, source_target_pairs={{0,7},{1,2},{2,1},{3,4},{4,3},{5,6},{6,5},{7,0},{8,15},{9,10},{10,... | collective-permute-start | bytes 172040 | tf_op jit(solution)/shard_map/ppermute | solution.py:519
  105.6 45.6 %copy-start.8 = (f32[64,256]{1,0:T(8,128)S(1)}, f32[64,256]{1,0:T(8,128)}, u32[]{:S(2)}) copy-start(f32[64,256]{1,0:T(8,128)} %constant.21.clone.refs_5_) | copy-start | bytes 196612
  107.2 51.8 %copy-start.4 = (f32[53,1,256]{2,1,0:T(1,128)S(1)}, f32[53,1,256]{2,1,0:T(1,128)}, u32[]{:S(2)}) copy-start(f32[53,1,256]{2,1,0:T(1,128)} %patch.1) | copy-start | bytes 162820
  107.2 69.2 %copy-start.2 = (f32[128,512]{1,0:T(8,128)S(1)}, f32[128,512]{1,0:T(8,128)}, u32[]{:S(2)}) copy-start(f32[128,512]{1,0:T(8,128)} %constant.22.clone.halves) | copy-start | bytes 786436
  107.2 5.7 %collective-permute-start.6 = (f32[56,256]{1,0:T(8,128)S(1)}, f32[56,256]{1,0:T(8,128)S(1)}, u32[]{:S(2)}, u32[]{:S(2)}) collective-permute-start(f32[56,256]{1,0:T(8,128)S(1)} %get-tuple-element.133), channel_id=1, source_target_pairs={{0,1},{1,0},{2,3},{3,2},{4,5},{5,4},{6,7},{7,6},{8,9},{9,8},{10,11... | collective-permute-start | bytes 172040 | tf_op jit(solution)/shard_map/ppermute | solution.py:518
  107.3 6.3 %collective-permute-start.7 = (f32[56,256]{1,0:T(8,128)S(1)}, f32[56,256]{1,0:T(8,128)S(1)}, u32[]{:S(2)}, u32[]{:S(2)}) collective-permute-start(f32[56,256]{1,0:T(8,128)S(1)} %get-tuple-element.134), channel_id=1, source_target_pairs={{0,7},{1,2},{2,1},{3,4},{4,3},{5,6},{6,5},{7,0},{8,15},{9,10},{10,... | collective-permute-start | bytes 172040 | tf_op jit(solution)/shard_map/ppermute | solution.py:519
  154.0 22.4 %all-to-all-start.6 = ((f32[32,32,128]{2,1,0:T(8,128)}), f32[32,32,128]{2,1,0:T(8,128)S(1)}, u32[]{:S(2)}, u32[]{:S(2)}) async-start(f32[32,32,128]{2,1,0:T(8,128)} %get-tuple-element.149), calls=%async_computation.6 | async-start | bytes 1048576 | tf_op jit(solution)/shard_map/all_to_all | solution.py:484

commit v3 on v2

--- a/solution.py
+++ b/solution.py
@@ -16,7 +16,9 @@
 PAD = 56
 ROWS = 2 * PAD
 SLOT = 40
+WHOLE = 66900000
 EXACT = lax.Precision.HIGHEST
+HBM = pl.BlockSpec(memory_space=pltpu.HBM)
 VMEM = pl.BlockSpec(memory_space=pltpu.VMEM)
 SMEM = pl.BlockSpec(memory_space=pltpu.SMEM)
 
@@ -65,7 +67,7 @@
 FACES, INSIDE, AVERAGE, HALVES = constants()
 
 
-def call(kernel, name, shapes, args, specs, scratch=(), out_specs=None):
+def call(kernel, name, shapes, args, specs, scratch=(), out_specs=None, limit=24 << 20):
     return pl.pallas_call(
         kernel,
         out_shape=[
@@ -77,7 +79,7 @@
         in_specs=specs,
         out_specs=out_specs or [VMEM] * len(shapes),
         scratch_shapes=list(scratch),
-        compiler_params=pltpu.CompilerParams(vmem_limit_bytes=24 << 20),
+        compiler_params=pltpu.CompilerParams(vmem_limit_bytes=limit),
         name=name,
     )(*args)
 
@@ -142,7 +144,7 @@
         entry = owned[0, g]
         found = [jnp.where(entry == me * 4 + m, g, found[m]) for m in range(4)]
     for m in range(4):
-        sources[m] = found[m]
+        sources[0, m] = found[m]
     d = diffusion[...]
     species = d.shape[0]
     column = jnp.concatenate([d, jnp.zeros((PAD - species, 1), jnp.float32)], axis=0)
@@ -176,28 +178,40 @@
     return jnp.where(keep, a, b) + pltpu.roll(jnp.where(keep, b, a), shift, 0)
 
 
-def apply_inverse(inv, rows, u):
+def fetch(inverse, inv, arrived):
+    count = inverse.shape[0]
+    copies = []
+    for block in range(PAD // 8):
+        part = pl.ds(8 * block, min(8, count - 8 * block))
+        copies.append(pltpu.make_async_copy(inverse.at[part], inv.at[part], arrived.at[block]))
+    for copy in copies:
+        copy.start()
+    return copies
+
+
+def apply_inverse(copies, inv, rows, u):
     count, depth = inv.shape[0], inv.shape[1]
     full = depth // 8
-    for half in range(2):
-        lanes = slice(128 * half, 128 * half + 128)
-        row = lax.broadcasted_iota(jnp.int32, (8, 128), 0)
-        bit2, bit1, bit0 = (row & 4) == 0, (row & 2) == 0, (row & 1) == 0
-        w = [rows[half, 8 * k : 8 * k + 8, :] for k in range(full + 1)]
-        zero = jnp.zeros((8, 128), jnp.float32)
-
-        def one(i):
-            if i >= count:
-                return zero
-            m = inv[i, :, lanes].astype(jnp.float32)
-            total = m[0:8] * w[0]
-            for k in range(1, full):
-                total = total + m[8 * k : 8 * k + 8] * w[k]
-            last = m[8 * full : depth]
-            last = jnp.concatenate([last, jnp.zeros((8 - last.shape[0], 128), jnp.float32)], axis=0)
-            return total + last * w[full]
-
-        for block in range(PAD // 8):
+    row = lax.broadcasted_iota(jnp.int32, (8, 128), 0)
+    bit2, bit1, bit0 = (row & 4) == 0, (row & 2) == 0, (row & 1) == 0
+    zero = jnp.zeros((8, 128), jnp.float32)
+    for block in range(PAD // 8):
+        copies[block].wait()
+        for half in range(2):
+            lanes = slice(128 * half, 128 * half + 128)
+            w = [rows[half, 8 * k : 8 * k + 8, :] for k in range(full + 1)]
+
+            def one(i):
+                if i >= count:
+                    return zero
+                m = inv[i, :, lanes].astype(jnp.float32)
+                total = m[0:8] * w[0]
+                for k in range(1, full):
+                    total = total + m[8 * k : 8 * k + 8] * w[k]
+                last = m[8 * full : depth]
+                last = jnp.concatenate([last, zero[last.shape[0] :]], axis=0)
+                return total + last * w[full]
+
             a = [one(8 * block + d) for d in range(8)]
             b = [mix(a[d], a[d + 2], bit1, 6) for d in (0, 1, 4, 5)]
             c = [mix(b[d], b[d + 2], bit2, 4) for d in range(2)]
@@ -222,85 +236,120 @@
     return jnp.concatenate(planes, axis=0)
 
 
-def flag(condition):
-    return jnp.full((1, 1), condition, jnp.int32) != 0
-
-
-def precondition(ids, inv, w, rows, u, near, far):
-    interleave(rows, w)
-    apply_inverse(inv, rows, u)
-
-    @pl.when(ids[1] % 2 == 0)
-    def _():
-        near[...] = u[PAD:]
-        far[...] = u[:PAD]
-
-    @pl.when(ids[1] % 2 == 1)
-    def _():
-        near[...] = u[:PAD]
-        far[...] = u[PAD:]
-
-
-def first_kernel(ids, links, received, source, scale, inv, w_out, near, far, u, rows):
+def start(pairs, semaphores):
+    copies = [
+        pltpu.make_async_copy(source, target, semaphores.at[k])
+        for k, (source, target) in enumerate(pairs)
+    ]
+    for copy in copies:
+        copy.start()
+    return copies
+
+
+def precondition(meta, fetched, inv, image, faces, w_out, near, far, u_out, slots, w, u, planes, rows, sent):
+    w[...] = image
+    copies = [pltpu.make_async_copy(w, w_out, sent.at[0])]
+    copies[0].start()
+    interleave(rows, image)
+    apply_inverse(fetched, inv, rows, u)
+    even = meta[5, 1] % 2
+    lower = pl.multiple_of(even * PAD, 8)
+    upper = pl.multiple_of(PAD - even * PAD, 8)
+    copies.append(pltpu.make_async_copy(u.at[pl.ds(upper, PAD)], near, sent.at[1]))
+    copies.append(pltpu.make_async_copy(u.at[pl.ds(lower, PAD)], far, sent.at[2]))
+    copies.append(pltpu.make_async_copy(u, u_out, sent.at[3]))
+    for copy in copies[1:]:
+        copy.start()
+    face = faces[...].astype(jnp.bfloat16)
+    planes[:, 0:ROWS] = lax.dot_general(
+        jnp.concatenate([face, face], axis=1),
+        jnp.concatenate(two(u[...]), axis=1),
+        NT,
+        preferred_element_type=jnp.float32,
+    )
+    for f in range(4):
+        other = meta[f, meta[5, 0]]
+
+        @pl.when(other >= 0)
+        def _():
+            pltpu.make_async_copy(
+                planes.at[pl.ds(FS * f, FS)], slots.at[jnp.maximum(other, 0)], sent.at[4 + f]
+            ).start()
+
+    for f in range(4):
+        other = meta[f, meta[5, 0]]
+
+        @pl.when(other >= 0)
+        def _():
+            pltpu.make_async_copy(
+                planes.at[pl.ds(FS * f, FS)], slots.at[jnp.maximum(other, 0)], sent.at[4 + f]
+            ).wait()
+
+    for copy in copies:
+        copy.wait()
+
+
+def first_kernel(*refs):
+    outside, inverse, outs, inside = refs[:5], refs[5], refs[6:11], refs[11:16]
+    arrived, inv, blocks, w, u, planes, rows, sent = refs[16:]
+    copies = start(zip(outside, inside), arrived)
+    fetched = fetch(inverse, inv, blocks)
+    for copy in copies:
+        copy.wait()
+    meta, received, source, scale, faces = inside
     values = received[0]
     for g in range(1, received.shape[0]):
         values = values + received[g]
-    me = ids[0]
+    me = meta[5, 0]
     row = lax.broadcasted_iota(jnp.int32, (SLOT, FACE), 0)
     cell = lax.broadcasted_iota(jnp.int32, (SLOT, FACE), 1)
     y, z = cell // FS, cell % FS
     coarse = y // 2 * HALF + z // 2
     first = 64 - SLOT
-    y_face = jnp.where(links[0, me] < 0, 0, FS - 1)
-    z_face = jnp.where(links[2, me] < 0, 0, FS - 1)
+    y_face = jnp.where(meta[0, me] < 0, 0, FS - 1)
+    z_face = jnp.where(meta[2, me] < 0, 0, FS - 1)
     sides = ((y == y_face) & (row == first + z // 2)).astype(jnp.float32)
     sides = sides + ((z == z_face) & (row == first + HALF + y // 2)).astype(jnp.float32)
-    faces = [coarse == row, (coarse == row + SLOT) & (row < first)]
-    faces = [face.astype(jnp.float32) for face in faces]
-    across = mm(values, jnp.concatenate([faces[0], faces[1], sides], axis=1), TN)
+    ends = [coarse == row, (coarse == row + SLOT) & (row < first)]
+    ends = [end.astype(jnp.float32) for end in ends]
+    across = mm(values, jnp.concatenate([ends[0], ends[1], sides], axis=1), TN)
     beside = across[64 : 64 + PAD, 2 * FACE :]
     across = across[0:PAD, :FACE] + across[64 : 64 + PAD, FACE : 2 * FACE]
-    bottom = flag(ids[1] == 0)
-    boundary = jnp.concatenate(
-        [beside + jnp.where(bottom, across, 0.0), beside + jnp.where(bottom, 0.0, across)], axis=0
-    )
+    bottom = jnp.where(meta[5, 1] == 0, 1.0, 0.0)
+    boundary = jnp.concatenate([beside + bottom * across, beside + (1.0 - bottom) * across], axis=0)
     species = source.shape[0]
     for half in range(2):
         rows[half, 0:species, :] = source[:, 128 * half : 128 * half + 128]
         rows[half, species:ROWS, :] = jnp.zeros((ROWS - species, 128), jnp.float32)
     right = separate(rows) + scale[:, 3:4] * boundary
-    w_out[...] = right
-    precondition(ids, inv, right, rows, u, near, far)
-
-
-def dots(vectors, last, line):
-    lane = lax.broadcasted_iota(jnp.int32, (1, 128), 1)
+    precondition(meta, fetched, inv, right, faces, *outs, w, u, planes, rows, sent)
+
+
+def dots(vectors, last):
+    lane = lax.broadcasted_iota(jnp.int32, (8, 128), 1)
+    line = jnp.zeros((8, 128), jnp.float32)
     count = len(vectors)
     for b, vector in enumerate(vectors + [last]):
-        part = jnp.sum(last * vector, axis=0, keepdims=True)
-        part = jnp.sum(part, axis=1, keepdims=True)
-        line = jnp.where(lane == count * (count + 1) // 2 + b, part, line)
+        product = last * vector
+        total = product[0:8]
+        for k in range(8, ROWS, 8):
+            total = total + product[k : k + 8]
+        total = jnp.sum(total[:, :128] + total[:, 128:], axis=0, keepdims=True)
+        total = jnp.sum(total, axis=1, keepdims=True)
+        line = jnp.where(lane == count * (count + 1) // 2 + b, total, line)
     return line
 
 
-def local_kernel(j, ids, links, *refs):
-    u, scale, inside, faces, orders, stoich, rates = refs[:7]
-    basis = refs[7 : 8 + j]
-    part, slots, line_out = refs[-3:]
-    line = refs[8 + j][...] if j else jnp.zeros((1, 128), jnp.float32)
-    me = ids[0]
+def local_kernel(j, *refs):
+    count = 7 + j
+    outside, (part, line), inside_refs = refs[:count], refs[count : count + 2], refs[count + 2 :]
+    result, summed, arrived, sent = inside_refs[count:]
+    copies = start(zip(outside, inside_refs[:count]), arrived)
+    u, w, scale, inside, orders, stoich, rates = inside_refs[:7]
+    for copy in copies:
+        copy.wait()
     field = u[...]
     lower, upper = field[:PAD], field[PAD:]
-    face = faces[...].astype(jnp.bfloat16)
-    planes = lax.dot_general(
-        jnp.concatenate([face, face], axis=1),
-        jnp.concatenate(two(field), axis=1),
-        NT,
-        preferred_element_type=jnp.float32,
-    )
-    for f in range(4):
-        other = links[f, me]
-        slots[jnp.where(other < 0, me, other), :, 0:ROWS] = planes[FS * f : FS * f + FS]
     total = select(field, inside[...].astype(jnp.bfloat16))
     total = total + jnp.concatenate([field[PAD:], field[:PAD]], axis=0)
     both = jnp.concatenate([lower, upper], axis=1)
@@ -313,23 +362,30 @@
     chemistry = chemistry[:PAD] + chemistry[PAD:]
     chemistry = chemistry + jnp.dot(stoich[:PAD, :], low, preferred_element_type=jnp.float32)
     chemistry = jnp.concatenate([chemistry[:, :FACE], chemistry[:, FACE:]], axis=0)
-    w = basis[-1][...]
-    part[...] = scale[:, 0:1] * field - scale[:, 1:2] * total - chemistry - scale[:, 2:3] * w
-    line_out[...] = dots([ref[...] for ref in basis[:-1]], w, line)
-
-
-def image_of(ids, links, received, near, far, part, scale, faces):
-    me = ids[0]
-    even = (ids[1] % 2 == 0).astype(jnp.float32)
-    end = jnp.logical_or(ids[1] == 0, ids[1] == ids[2])
-    live = jnp.where(end, 0.0, 1.0)
-    low = (1.0 - even) * near[...] + (even * live) * far[...]
-    high = even * near[...] + ((1.0 - even) * live) * far[...]
+    result[...] = (
+        scale[:, 0:1] * field - scale[:, 1:2] * total - chemistry - scale[:, 2:3] * w[...]
+    )
+    copies = start([(result, part)], sent)
+    summed[...] = dots([ref[...] for ref in inside_refs[7:count]], w[...])
+    copy = pltpu.make_async_copy(summed, line, sent.at[1])
+    copy.start()
+    copy.wait()
+    copies[0].wait()
+
+
+def image_of(outside, inside, arrived, blocks=None):
+    meta, received, ends, part, scale, faces = inside
+    targets = (meta, received, ends.at[0], ends.at[1], part, scale, faces)
+    copies = start(zip(outside, targets), arrived)
+    fetched = fetch(*blocks) if blocks else None
+    for copy in copies:
+        copy.wait()
+    me, box = meta[5, 0], meta[5, 1]
     ghosts = []
     for f in range(4):
-        other = links[f, me]
-        plane = received[jnp.where(other < 0, me, other), :, 0:ROWS]
-        ghosts.append(jnp.where(other < 0, 0.0, 1.0) * plane)
+        other = meta[f, me]
+        plane = received[jnp.maximum(other, 0), :, 0:ROWS]
+        ghosts.append(jnp.where(jnp.full((FS, ROWS), other, jnp.int32) >= 0, plane, 0.0))
     face = faces[...].astype(jnp.bfloat16)
     total = lax.dot_general(
         jnp.concatenate(two(jnp.concatenate(ghosts, axis=0)), axis=0),
@@ -337,20 +393,33 @@
         TN,
         preferred_element_type=jnp.float32,
     )
+    even = 1 - box % 2
+    low = jnp.where(box == 0, 0.0, 1.0) * ends[even]
+    high = jnp.where(box == meta[5, 2], 0.0, 1.0) * ends[1 - even]
     total = total + jnp.concatenate([low, high], axis=0)
-    return part[...] - scale[:, 1:2] * total
-
-
-def combine_kernel(ids, links, received, near_in, far_in, part, scale, faces, inv, w_out, near, far, u, rows):
-    image = image_of(ids, links, received, near_in, far_in, part, scale, faces)
-    w_out[...] = image
-    precondition(ids, inv, image, rows, u, near, far)
-
-
-def last_kernel(ids, links, received, near, far, part, scale, faces, w0, w1, w2, w3, line, out):
-    image = image_of(ids, links, received, near, far, part, scale, faces)
-    result = dots([w0[...], w1[...], w2[...], w3[...]], image, line[...])
-    out[...] = jnp.broadcast_to(result, out.shape)
+    return part[...] - scale[:, 1:2] * total, fetched
+
+
+def combine_kernel(*refs):
+    outside, inverse, outs, inside = refs[:7], refs[7], refs[8:13], refs[13:19]
+    arrived, inv, blocks, w, u, planes, rows, sent = refs[19:]
+    image, fetched = image_of(outside, inside, arrived, (inverse, inv, blocks))
+    precondition(inside[0], fetched, inv, image, inside[5], *outs, w, u, planes, rows, sent)
+
+
+def last_kernel(*refs):
+    outside, basis, lines, out, inside = refs[:7], refs[7:11], refs[11:15], refs[15], refs[16:22]
+    arrived, held, sums, landed = refs[22:]
+    pairs = [(basis[k], held.at[k]) for k in range(ITERS)]
+    pairs += [(lines[k], sums.at[k]) for k in range(ITERS)]
+    copies = start(pairs, landed)
+    image, _ = image_of(outside, inside, arrived)
+    for copy in copies:
+        copy.wait()
+    line = dots([held[k] for k in range(ITERS)], image)
+    for k in range(ITERS):
+        line = line + sums[k]
+    out[...] = jnp.broadcast_to(line[0:1], out.shape)
 
 
 def solve(gram, shift):
@@ -393,9 +462,15 @@
     return [result[a] * size[a] for a in range(n)]
 
 
-def finish_kernel(ids, owned, lines, *refs):
-    fields = refs[:ITERS]
-    scale, average, correction, slots, rows = refs[ITERS:]
+def finish_kernel(*refs):
+    n = ITERS
+    outside, outs, inside = refs[: n + 4], refs[n + 4 : n + 6], refs[n + 6 : n + 11]
+    arrived, result, mean, rows, sent = refs[n + 11 :]
+    lines, scale, meta, average, fields = inside
+    copies = start(
+        zip(outside, [lines, scale, meta, average] + [fields.at[k] for k in range(n)]), arrived
+    )
+    copies[0].wait()
     line = jnp.sum(lines[...], axis=0, keepdims=True)
     gram = {}
     k = 0
@@ -403,49 +478,57 @@
         for b in range(a + 1):
             gram[a, b] = line[:, k : k + 1]
             k += 1
+    copies[1].wait()
     weights = solve(gram, scale[0:1, 2:3])
     factor = scale[0:1, 4:5]
-    total = (weights[0] * factor) * fields[0][...]
-    for weight, field in zip(weights[1:], fields[1:]):
-        total = total + (weight * factor) * field[...]
-    interleave(rows, total)
-    for half in range(2):
-        lanes = slice(128 * half, 128 * half + 128)
-        correction[:, lanes] = rows[half, 0 : correction.shape[0], :]
+    for copy in copies[2:]:
+        copy.wait()
+    total = (weights[0] * factor) * fields[0]
+    for k in range(1, ITERS):
+        total = total + (weights[k] * factor) * fields[k]
     summed = total[:PAD] + total[PAD:]
     blank = jnp.zeros((64 - PAD, FACE), jnp.float32)
     spread = jnp.concatenate([summed, blank, summed, blank], axis=0)
     weight = average[...].astype(jnp.bfloat16)
-    mean = lax.dot_general(
+    got = lax.dot_general(
         jnp.concatenate([weight, weight], axis=1),
         jnp.concatenate(two(spread), axis=1),
         NT,
         preferred_element_type=jnp.float32,
     )
     lane = lax.broadcasted_iota(jnp.int32, (32, 128), 1)
-    slots[owned[0, ids[0]] // 4] = jnp.where(lane < 64, mean[:32], mean[32:])
-
-
-def update_kernel(sources, received, patch, halves, out, stacked):
+    mean[...] = jnp.where(lane < 64, got[:32], got[32:])
+    home = meta[4, meta[5, 0]] // 4
+    copies = start([(mean, outs[1].at[home])], sent)
+    interleave(rows, total)
+    for half in range(2):
+        lanes = slice(128 * half, 128 * half + 128)
+        result[:, lanes] = rows[half, 0 : result.shape[0], :]
+    copies.append(pltpu.make_async_copy(result, outs[0], sent.at[1]))
+    copies[1].start()
+    for copy in copies:
+        copy.wait()
+
+
+def update_kernel(*refs):
+    outside, out, inside, arrived = refs[:4], refs[4], refs[5:9], refs[9]
+    copies = start(zip(outside, inside), arrived)
+    for copy in copies:
+        copy.wait()
+    sources, received, patch, halves = inside
     lane = lax.broadcasted_iota(jnp.int32, (1, FACE), 1)
     covered = jnp.zeros((1, FACE), jnp.int32)
+    blocks = []
     for m in range(4):
-        source = sources[m]
-        here = slice(32 * m, 32 * m + 32)
-
-        @pl.when(source >= 0)
-        def _():
-            stacked[here, :] = received[source]
-
-        @pl.when(source < 0)
-        def _():
-            stacked[here, :] = jnp.zeros((32, 128), jnp.float32)
-
+        source = sources[0, m]
+        block = received[jnp.maximum(source, 0)]
+        blocks.append(jnp.where(jnp.full((32, 128), source, jnp.int32) >= 0, block, 0.0))
         covered = jnp.where(lane // 64 == m, source, covered)
+    stacked = jnp.concatenate(blocks, axis=0)
     species = patch.shape[0]
     half = halves[...].astype(jnp.bfloat16)
     got = lax.dot_general(
-        jnp.concatenate(two(stacked[...]), axis=0),
+        jnp.concatenate(two(stacked), axis=0),
         jnp.concatenate([half, half], axis=0),
         TN,
         preferred_element_type=jnp.float32,
@@ -472,7 +555,6 @@
     me = lax.axis_index("grp")
     box = lax.axis_index("box")
     f32 = jnp.float32
-    barrier = lax.optimization_barrier
 
     ids = jnp.stack([me, box, jnp.asarray(boxes - 1, box.dtype)]).astype(jnp.int32)
     links = neighbours.T
@@ -480,6 +562,9 @@
     even_swap = [(i, i ^ 1) for i in range(boxes)]
     odd_swap = [(i, (i + (1 if i % 2 else -1)) % boxes) for i in range(boxes)]
 
+    meta = jnp.concatenate([links, owned, jnp.pad(ids, (0, groups - 3))[None]], axis=0)
+    meta = jnp.pad(meta, ((0, 2), (0, 128 - groups)))
+
     def exchange(slots):
         return lax.all_to_all(slots, "grp", 0, 0, tiled=True)
 
@@ -491,7 +576,7 @@
     scale, stoich_s, orders_s, sources = call(
         prepare_kernel,
         "prepare",
-        [(ROWS, 128), (2 * PAD, reactions, jnp.bfloat16), (reactions, 3 * PAD, jnp.bfloat16), (4, jnp.int32)],
+        [(ROWS, 128), (2 * PAD, reactions, jnp.bfloat16), (reactions, 3 * PAD, jnp.bfloat16), (8, 128, jnp.int32)],
         (ids, owned, diffusion.reshape(species, 1), stoich, orders.T),
         [SMEM] * 2 + [VMEM] * 3,
         (),
@@ -502,42 +587,65 @@
     source = source_term.reshape(2 * species, FACE)
     faces = jnp.asarray(FACES)
     inside = jnp.asarray(INSIDE)
-    outs = [(ROWS, FACE), (PAD, FACE), (PAD, FACE), (ROWS, FACE)]
+    outs = [(ROWS, FACE), (PAD, FACE), (PAD, FACE), (ROWS, FACE), (groups, FS, 128)]
+    cells = pltpu.VMEM((ROWS, FACE), f32)
     rows = [pltpu.VMEM((2, ROWS, 128), f32)]
-    w, near, far, u = call(
+    held = [pltpu.VMEM(inverse.shape, inverse.dtype), pltpu.SemaphoreType.DMA((PAD // 8,))]
+    work = [cells, cells, pltpu.VMEM((4 * FS, 128), f32)] + rows + [pltpu.SemaphoreType.DMA((8,))]
+    landing = [
+        pltpu.SMEM(meta.shape, jnp.int32),
+        pltpu.VMEM((groups, FS, 128), f32),
+        pltpu.VMEM((2, PAD, FACE), f32),
+        cells,
+        pltpu.VMEM((ROWS, 128), f32),
+        pltpu.VMEM((4 * FS, FACE), f32),
+        pltpu.SemaphoreType.DMA((7,)),
+    ]
+    w, near, far, u, slots = call(
         first_kernel,
         "first",
         outs,
-        (ids, links, received, source, scale, inverse),
-        [SMEM] * 2 + [VMEM] * 4,
-        rows,
-    )
-    basis, directions = [w], [u]
-    line = ()
+        (meta, received, source, scale, faces, inverse),
+        [HBM] * 6,
+        [pltpu.SMEM(meta.shape, jnp.int32)]
+        + [pltpu.VMEM(x.shape, f32) for x in (received, source, scale, faces)]
+        + [pltpu.SemaphoreType.DMA((5,))]
+        + held
+        + work,
+        [HBM] * 5,
+        WHOLE,
+    )
+    basis, directions, lines = [w], [u], []
     for j in range(ITERS):
+        received = exchange(slots)
         near_in = lax.ppermute(near, "box", even_swap)
         far_in = lax.ppermute(far, "box", odd_swap)
-        part, slots, line = call(
+        operands = (u, w, scale, inside, orders_s, stoich_s, rates_s) + tuple(basis[:-1])
+        count = len(operands)
+        part, line = call(
             functools.partial(local_kernel, j),
             "local%d" % j,
-            [(ROWS, FACE), (groups, FS, 128), (1, 128)],
-            (ids, links, u, scale, inside, faces, orders_s, stoich_s, rates_s)
-            + tuple(basis)
-            + ((line,) if j else ()),
-            [SMEM] * 2 + [VMEM] * (9 + j if j else 8),
+            [(ROWS, FACE), (8, 128)],
+            operands,
+            [HBM] * count,
+            [pltpu.VMEM(x.shape, x.dtype) for x in operands]
+            + [cells, pltpu.VMEM((8, 128), f32)]
+            + [pltpu.SemaphoreType.DMA((count,)), pltpu.SemaphoreType.DMA((2,))],
+            [HBM] * 2,
+            WHOLE,
         )
-        slots, near_in, far_in, part, line = barrier((slots, near_in, far_in, part, line))
-        received = exchange(slots)
-        received, near_in, far_in, part, line = barrier((received, near_in, far_in, part, line))
-        shared = (ids, links, received, near_in, far_in, part, scale, faces)
+        lines.append(line)
+        shared = (meta, received, near_in, far_in, part, scale, faces)
         if j + 1 < ITERS:
-            w, near, far, u = call(
+            w, near, far, u, slots = call(
                 combine_kernel,
                 "combine%d" % j,
                 outs,
                 shared + (inverse,),
-                [SMEM] * 2 + [VMEM] * 7,
-                rows,
+                [HBM] * 8,
+                landing + held + work,
+                [HBM] * 5,
+                WHOLE,
             )
             basis.append(w)
             directions.append(u)
@@ -546,26 +654,42 @@
                 last_kernel,
                 "last",
                 [(groups * boxes, 128)],
-                shared + tuple(basis) + (line,),
-                [SMEM] * 2 + [VMEM] * 11,
+                shared + tuple(basis) + tuple(lines),
+                [HBM] * 15,
+                landing
+                + [pltpu.VMEM((ITERS, ROWS, FACE), f32), pltpu.VMEM((ITERS, 8, 128), f32)]
+                + [pltpu.SemaphoreType.DMA((2 * ITERS,))],
+                limit=WHOLE,
             )
     lines = lax.all_to_all(lines, ("grp", "box"), 0, 0, tiled=True)
+    average = jnp.asarray(AVERAGE)
     correction, slots = call(
         finish_kernel,
         "finish",
         [(2 * species, FACE), (groups, 32, 128)],
-        (ids, owned, lines) + tuple(directions) + (scale, jnp.asarray(AVERAGE)),
-        [SMEM] * 2 + [VMEM] * 7,
-        rows,
+        (lines, scale, meta, average) + tuple(directions),
+        [HBM] * (4 + ITERS),
+        [pltpu.VMEM(lines.shape, f32), pltpu.VMEM((ROWS, 128), f32)]
+        + [pltpu.SMEM(meta.shape, jnp.int32), pltpu.VMEM(average.shape, f32)]
+        + [pltpu.VMEM((ITERS, ROWS, FACE), f32), pltpu.SemaphoreType.DMA((ITERS + 4,))]
+        + [pltpu.VMEM((2 * species, FACE), f32), pltpu.VMEM((32, 128), f32)]
+        + rows
+        + [pltpu.SemaphoreType.DMA((2,))],
+        [HBM] * 2,
+        WHOLE,
     )
     received = exchange(slots)
+    halves = jnp.asarray(HALVES)
     (updated,) = call(
         update_kernel,
         "update",
         [(species, 1, FACE)],
-        (sources, received, coarse_field.reshape(species, FACE), jnp.asarray(HALVES)),
-        [SMEM] + [VMEM] * 3,
-        [pltpu.VMEM((128, 128), f32)],
+        (sources, received, coarse_field.reshape(species, FACE), halves),
+        [HBM] * 4,
+        [pltpu.SMEM((8, 128), jnp.int32), pltpu.VMEM(received.shape, f32)]
+        + [pltpu.VMEM((species, FACE), f32), pltpu.VMEM(halves.shape, f32)]
+        + [pltpu.SemaphoreType.DMA((4,))],
+        limit=WHOLE,
     )
     return correction.reshape(species, 1, 2, FACE), updated
 

time: 179 us -> 172 us (0.961)
  blocking collectives: 83.2 us -> 20.9 us
  starting transfers between devices: 32.3 us -> 53 us
  Pallas kernels: 21.3 us -> 38 us
  waiting for transfers between devices: 28.9 us -> 40.2 us
  local copies, waits for them, and re-layouts: 11.2 us -> 17.7 us
    all_to_all x4 -> x0, blocking collectives: 61.5 us -> none  [exchange(): return lax.all_to_all(slots, 'grp', 0, 0, tiled=True)]
    all_to_all x2 -> x6, starting transfers between devices: 16.7 us -> 44.1 us  [exchange(): return lax.all_to_all(slots, 'grp', 0, 0, tiled=True)]
    pallas_call x13, Pallas kernels: 21.3 us -> 38 us  [call(): pl.pallas_call(kernel, out_shape=[jax.ShapeDtypeStruct(s[:-1], s[-1]) if...]
    all_to_all x2 -> x6, waiting for transfers between devices: 26.3 us -> 38.1 us  [exchange(): return lax.all_to_all(slots, 'grp', 0, 0, tiled=True)]
    ppermute x4, starting transfers between devices: 15.2 us -> 8.36 us  [on_device(): far_in = lax.ppermute(far, 'box', odd_swap)]
    unnamed x29 -> x41, local copies, waits for them, and re-layouts: 3.67 us -> 6.96 us
  transfers between devices with their start and end apart: 10 -> 14, of which waited for: 6 -> 9; matrix products, arithmetic and copies ran while one was open for 4% -> 8% of each run, Pallas kernels for 3% -> 7%
where the time goes in v3:
time: 172 us; the launch traced here: 171 us
  starting transfers between devices  53 us (31%)
  waiting for transfers between devices  40.2 us (23%)
  Pallas kernels  38 us (22%)
  blocking collectives  20.9 us (12%)
  local copies, waits for them, and re-layouts  17.7 us (10%)
    all_to_all x6, starting transfers between devices, exchange(): return lax.all_to_all(slots, 'grp', 0, 0, tiled=True)  44.1 us
    all_to_all x6, waiting for transfers between devices, exchange(): return lax.all_to_all(slots, 'grp', 0, 0, tiled=True)  38.1 us
    pallas_call x13, Pallas kernels, call(): pl.pallas_call(kernel, out_shape=[jax.ShapeDtypeStruct(s[:-1], s[-1]) if...  38 us
    all_to_all x1, blocking collectives, on_device(): lines = lax.all_to_all(lines, ('grp', 'box'), 0, 0, tiled=True)  20.9 us
    ppermute x4, starting transfers between devices, on_device(): far_in = lax.ppermute(far, 'box', odd_swap)  8.36 us
    reshape x1, local copies, waits for them, and re-layouts, on_device(): inverse = precond.reshape(species, 2 * species, FACE)  7.05 us
    unnamed x41, local copies, waits for them, and re-layouts  6.96 us
  transfers between devices with their start and end apart: 14, of which 9 were waited for; matrix products, arithmetic and copies ran while one was open for 8% of the time, Pallas kernels for 7%

profile of v3, /device:TPU:2, one launch (start us, length us, event | category | flops | bytes accessed | tf_op | source)
XLA Modules:
  0.0 171.1 jit_solution(15357255642101660343)
XLA Ops:
  0.6 0.1 pad_add_fusion.1.ids
  0.7 0.8 copy-done.3
  1.5 0.8 copy-done.7
  2.3 3.0 %gather.1 = f32[32,40,128]{2,1,0:T(8,128)} custom-call(s32[3]{0:T(128)S(1)} %pad_add_fusion.1.ids, f32[53,1,256]{2,1,0:T(1,128)S(1)} %copy-done.3, s32[32,1,160]{2,1,0:T(1,128)S(1)} %copy-done.7), custom_call_target="tpu_custom_call" | custom-call | tf_op jit(solution)/shard_map/gather/pallas_call | solution.py:71
  5.3 11.7 %all-to-all-start = ((f32[32,40,128]{2,1,0:T(8,128)}), f32[32,40,128]{2,1,0:T(8,128)}, u32[]{:S(2)}, u32[]{:S(2)}) async-start(f32[32,40,128]{2,1,0:T(8,128)} %gather.1), calls=%async_computation | async-start | bytes 1310720 | tf_op jit(solution)/shard_map/all_to_all | solution.py:569
  16.9 0.0 copy-start.10
  17.0 0.8 copy.18.diffusion
  17.8 0.0 copy-start.5
  17.8 0.0 copy-start.6
  17.8 7.0 %reshape.26.refs_5_.refs_7_ = bf16[53,106,256]{2,1,0:T(8,128)(2,1)} reshape(bf16[53,53,1,2,256]{4,3,2,1,0:T(2,128)(2,1)} %param.19) | data formatting | bytes 5752832 | tf_op jit(solution)/shard_map/reshape | solution.py:586
  24.8 0.7 reshape.24.refs_2_
  25.6 0.6 pad.9.refs_0_.refs_2_
  26.2 1.5 prepare.1
  27.7 0.0 copy-start
  27.7 0.6 copy-done
  28.3 0.7 copy-done.1
  28.9 0.6 copy-done.2
  29.6 0.6 copy-done.8
  30.2 6.5 %all-to-all-done.refs_1_ = f32[32,40,128]{2,1,0:T(8,128)} async-done(((f32[32,40,128]{2,1,0:T(8,128)}), f32[32,40,128]{2,1,0:T(8,128)}, u32[]{:S(2)}, u32[]{:S(2)}) %all-to-all-start) | async-done | bytes 655392 | tf_op jit(solution)/shard_map/all_to_all | solution.py:569
  36.6 4.2 %first.1 = (f32[112,256]{1,0:T(8,128)}, f32[56,256]{1,0:T(8,128)}, f32[56,256]{1,0:T(8,128)}, f32[112,256]{1,0:T(8,128)}, f32[32,16,128]{2,1,0:T(8,128)}) custom-call(s32[8,128]{1,0:T(8,128)} %pad.9.refs_0_.refs_2_, f32[32,40,128]{2,1,0:T(8,128)} %all-to-all-done.refs_1_, f32[106,256]{1,0:T(8,128)} %reshape.24.refs_2_, f32[112,128]{1,0:T(8,128)} %copy-done, ...), custom_call_target="tpu_custom_call" | custom-call | tf_op jit(solution)/shard_map/first/pallas_call | solution.py:71
  40.8 5.7 %all-to-all-start.1 = ((f32[32,16,128]{2,1,0:T(8,128)}), f32[32,16,128]{2,1,0:T(8,128)}, u32[]{:S(2)}, u32[]{:S(2)}) async-start(f32[32,16,128]{2,1,0:T(8,128)} %get-tuple-element.37), calls=%async_computation.1 | async-start | bytes 524288 | tf_op jit(solution)/shard_map/all_to_all | solution.py:569
  46.5 0.1 collective-permute-start
  46.6 3.1 %collective-permute-start.1 = (f32[56,256]{1,0:T(8,128)}, f32[56,256]{1,0:T(8,128)S(1)}, u32[]{:S(2)}, u32[]{:S(2)}) collective-permute-start(f32[56,256]{1,0:T(8,128)} %get-tuple-element.39), channel_id=1, source_target_pairs={{0,7},{1,2},{2,1},{3,4},{4,3},{5,6},{6,5},{7,0},{8,15},{9,10},{10,... | collective-permute-start | bytes 172040 | tf_op jit(solution)/shard_map/ppermute | solution.py:622
  49.7 1.3 pad.16
  51.0 0.9 copy.22
  51.9 2.6 %local0.1 = (f32[112,256]{1,0:T(8,128)}, f32[8,128]{1,0:T(8,128)}) custom-call(f32[112,256]{1,0:T(8,128)} %get-tuple-element.40.refs_0_.refs_4_, f32[112,256]{1,0:T(8,128)} %get-tuple-element.41.refs_1_.refs_7_, f32[112,128]{1,0:T(8,128)} %copy-done, f32[256,256]{1,0:T(8,128)} %constant.22.clone.refs_3_, bf16[325,168]{1,0:T(8,128)(2,1)} %copy-done.1, ...), custom_call_target="tpu_custom_call" | custom-call | tf_op jit(solution)/shard_map/local0/pallas_call | solution.py:71
  54.6 0.0 collective-permute-done.refs_2_
  54.6 0.0 collective-permute-done.1.refs_3_
  54.6 0.0 copy-start.12
  54.6 2.1 %all-to-all-done.1.refs_1_ = f32[32,16,128]{2,1,0:T(8,128)} async-done(((f32[32,16,128]{2,1,0:T(8,128)}), f32[32,16,128]{2,1,0:T(8,128)}, u32[]{:S(2)}, u32[]{:S(2)}) %all-to-all-start.1) | async-done | bytes 262176 | tf_op jit(solution)/shard_map/all_to_all | solution.py:569
  56.8 3.7 %combine0.1 = (f32[112,256]{1,0:T(8,128)}, f32[56,256]{1,0:T(8,128)}, f32[56,256]{1,0:T(8,128)}, f32[112,256]{1,0:T(8,128)}, f32[32,16,128]{2,1,0:T(8,128)}) custom-call(s32[8,128]{1,0:T(8,128)} %pad.9.refs_0_.refs_2_, f32[32,16,128]{2,1,0:T(8,128)} %all-to-all-done.1.refs_1_, f32[56,256]{1,0:T(8,128)} %copy-done.11, f32[56,256]{1,0:T(8,128)} %copy-done.12, ...), custom_call_target="tpu_custom_call" | custom-call | tf_op jit(solution)/shard_map/combine0/pallas_call | solution.py:71
  60.5 8.3 %all-to-all-start.2 = ((f32[32,16,128]{2,1,0:T(8,128)}), f32[32,16,128]{2,1,0:T(8,128)}, u32[]{:S(2)}, u32[]{:S(2)}) async-start(f32[32,16,128]{2,1,0:T(8,128)} %get-tuple-element.45), calls=%async_computation.2 | async-start | bytes 524288 | tf_op jit(solution)/shard_map/all_to_all | solution.py:569
  68.8 0.1 collective-permute-start.2
  68.9 1.2 collective-permute-start.3
  70.1 2.6 %local1.1 = (f32[112,256]{1,0:T(8,128)}, f32[8,128]{1,0:T(8,128)}) custom-call(f32[112,256]{1,0:T(8,128)} %get-tuple-element.48.refs_0_.refs_5_, f32[112,256]{1,0:T(8,128)} %get-tuple-element.49.refs_1_.refs_8_, f32[112,128]{1,0:T(8,128)} %copy-done, f32[256,256]{1,0:T(8,128)} %constant.22.clone.refs_3_, bf16[325,168]{1,0:T(8,128)(2,1)} %copy-done.1, ...), custom_call_target="tpu_custom_call" | custom-call | tf_op jit(solution)/shard_map/local1/pallas_call | solution.py:71
  72.8 0.0 collective-permute-done.2.refs_2_
  72.8 1.3 collective-permute-done.3.refs_3_
  74.0 4.9 %all-to-all-done.2.refs_1_ = f32[32,16,128]{2,1,0:T(8,128)} async-done(((f32[32,16,128]{2,1,0:T(8,128)}), f32[32,16,128]{2,1,0:T(8,128)}, u32[]{:S(2)}, u32[]{:S(2)}) %all-to-all-start.2) | async-done | bytes 262176 | tf_op jit(solution)/shard_map/all_to_all | solution.py:569
  78.9 3.7 %combine1.1 = (f32[112,256]{1,0:T(8,128)}, f32[56,256]{1,0:T(8,128)}, f32[56,256]{1,0:T(8,128)}, f32[112,256]{1,0:T(8,128)}, f32[32,16,128]{2,1,0:T(8,128)}) custom-call(s32[8,128]{1,0:T(8,128)} %pad.9.refs_0_.refs_2_, f32[32,16,128]{2,1,0:T(8,128)} %all-to-all-done.2.refs_1_, f32[56,256]{1,0:T(8,128)} %copy-done.14, f32[56,256]{1,0:T(8,128)} %copy-done.16, ...), custom_call_target="tpu_custom_call" | custom-call | tf_op jit(solution)/shard_map/combine1/pallas_call | solution.py:71
  82.7 6.4 %all-to-all-start.3 = ((f32[32,16,128]{2,1,0:T(8,128)}), f32[32,16,128]{2,1,0:T(8,128)}, u32[]{:S(2)}, u32[]{:S(2)}) async-start(f32[32,16,128]{2,1,0:T(8,128)} %get-tuple-element.51), calls=%async_computation.3 | async-start | bytes 524288 | tf_op jit(solution)/shard_map/all_to_all | solution.py:569
  89.1 0.3 collective-permute-start.4
  89.3 1.8 %collective-permute-start.5 = (f32[56,256]{1,0:T(8,128)}, f32[56,256]{1,0:T(8,128)S(1)}, u32[]{:S(2)}, u32[]{:S(2)}) collective-permute-start(f32[56,256]{1,0:T(8,128)} %get-tuple-element.53), channel_id=1, source_target_pairs={{0,7},{1,2},{2,1},{3,4},{4,3},{5,6},{6,5},{7,0},{8,15},{9,10},{10,... | collective-permute-start | bytes 172040 | tf_op jit(solution)/shard_map/ppermute | solution.py:622
  91.2 2.7 %local2.1 = (f32[112,256]{1,0:T(8,128)}, f32[8,128]{1,0:T(8,128)}) custom-call(f32[112,256]{1,0:T(8,128)} %get-tuple-element.54.refs_0_.refs_6_, f32[112,256]{1,0:T(8,128)} %get-tuple-element.55.refs_1_.refs_9_, f32[112,128]{1,0:T(8,128)} %copy-done, f32[256,256]{1,0:T(8,128)} %constant.22.clone.refs_3_, bf16[325,168]{1,0:T(8,128)(2,1)} %copy-done.1, ...), custom_call_target="tpu_custom_call" | custom-call | tf_op jit(solution)/shard_map/local2/pallas_call | solution.py:71
  93.9 0.0 collective-permute-done.4.refs_2_
  93.9 0.6 collective-permute-done.5.refs_3_
  94.5 4.8 %all-to-all-done.3.refs_1_ = f32[32,16,128]{2,1,0:T(8,128)} async-done(((f32[32,16,128]{2,1,0:T(8,128)}), f32[32,16,128]{2,1,0:T(8,128)}, u32[]{:S(2)}, u32[]{:S(2)}) %all-to-all-start.3) | async-done | bytes 262176 | tf_op jit(solution)/shard_map/all_to_all | solution.py:569
  99.3 3.7 %combine2.1 = (f32[112,256]{1,0:T(8,128)}, f32[56,256]{1,0:T(8,128)}, f32[56,256]{1,0:T(8,128)}, f32[112,256]{1,0:T(8,128)}, f32[32,16,128]{2,1,0:T(8,128)}) custom-call(s32[8,128]{1,0:T(8,128)} %pad.9.refs_0_.refs_2_, f32[32,16,128]{2,1,0:T(8,128)} %all-to-all-done.3.refs_1_, f32[56,256]{1,0:T(8,128)} %copy-done.13, f32[56,256]{1,0:T(8,128)} %copy-done.15, ...), custom_call_target="tpu_custom_call" | custom-call | tf_op jit(solution)/shard_map/combine2/pallas_call | solution.py:71
  103.0 0.0 copy-start.4
  103.0 6.5 %all-to-all-start.4 = ((f32[32,16,128]{2,1,0:T(8,128)}), f32[32,16,128]{2,1,0:T(8,128)}, u32[]{:S(2)}, u32[]{:S(2)}) async-start(f32[32,16,128]{2,1,0:T(8,128)} %get-tuple-element.57), calls=%async_computation.4 | async-start | bytes 524288 | tf_op jit(solution)/shard_map/all_to_all | solution.py:569
  109.6 0.1 collective-permute-start.6
  109.7 2.2 %collective-permute-start.7 = (f32[56,256]{1,0:T(8,128)}, f32[56,256]{1,0:T(8,128)}, u32[]{:S(2)}, u32[]{:S(2)}) collective-permute-start(f32[56,256]{1,0:T(8,128)} %get-tuple-element.59), channel_id=1, source_target_pairs={{0,7},{1,2},{2,1},{3,4},{4,3},{5,6},{6,5},{7,0},{8,15},{9,10},{10,... | collective-permute-start | bytes 172040 | tf_op jit(solution)/shard_map/ppermute | solution.py:622
  111.9 2.7 %local3.1 = (f32[112,256]{1,0:T(8,128)}, f32[8,128]{1,0:T(8,128)}) custom-call(f32[112,256]{1,0:T(8,128)} %get-tuple-element.60.refs_0_.refs_7_, f32[112,256]{1,0:T(8,128)} %get-tuple-element.61.refs_1_.refs_10_, f32[112,128]{1,0:T(8,128)} %copy-done, f32[256,256]{1,0:T(8,128)} %constant.22.clone.refs_3_, bf16[325,168]{1,0:T(8,128)(2,1)} %copy-done.1, ...), custom_call_target="tpu_custom_call" | custom-call | tf_op jit(solution)/shard_map/local3/pallas_call | solution.py:71
  114.6 0.0 collective-permute-done.6.refs_2_
  114.6 0.0 copy-start.17
  114.6 0.2 collective-permute-done.7.refs_3_
  114.9 5.0 %all-to-all-done.4.refs_1_ = f32[32,16,128]{2,1,0:T(8,128)} async-done(((f32[32,16,128]{2,1,0:T(8,128)}), f32[32,16,128]{2,1,0:T(8,128)}, u32[]{:S(2)}, u32[]{:S(2)}) %all-to-all-start.4) | async-done | bytes 262176 | tf_op jit(solution)/shard_map/all_to_all | solution.py:569
  119.9 2.4 %last.1 = f32[256,128]{1,0:T(8,128)} custom-call(s32[8,128]{1,0:T(8,128)} %pad.9.refs_0_.refs_2_, f32[32,16,128]{2,1,0:T(8,128)} %all-to-all-done.4.refs_1_, f32[56,256]{1,0:T(8,128)} %copy-done.17, f32[56,256]{1,0:T(8,128)} %collective-permute-done.7.refs_3_, f32[112,256]{1,0:T(8,128)} %get-tuple-element.62.refs_4_, f32[112,128]{1,0:T(8,128)} %copy-done, ...), custom_call_target="tpu_custom_call" | custom-call | tf_op jit(solution)/shard_map/last/pallas_call | solution.py:71
  122.3 20.9 %all_to_all.41 = f32[256,1,128]{2,1,0:T(1,128)} all-to-all(f32[256,1,128]{2,1,0:T(1,128)} %bitcast.29), channel_id=1, replica_groups=mesh['grp'=32,'box'=8] {'grp','box'}, dimensions={0} | all-to-all | bytes 262144 | tf_op jit(solution)/shard_map/all_to_all | solution.py:664
  143.3 3.2 %finish.1 = (f32[106,256]{1,0:T(8,128)}, f32[32,32,128]{2,1,0:T(8,128)}) custom-call(f32[256,128]{1,0:T(8,128)} %bitcast.30, f32[112,128]{1,0:T(8,128)} %copy-done, s32[8,128]{1,0:T(8,128)} %pad.9.refs_0_.refs_2_, f32[64,256]{1,0:T(8,128)} %constant.23.clone.refs_3_, f32[112,256]{1,0:T(8,128)} %get-tuple-element.40.refs_0_.refs_4_, ...), custom_call_target="tpu_custom_call" | custom-call | tf_op jit(solution)/shard_map/finish/pallas_call | solution.py:71
  146.4 5.5 %all-to-all-start.6 = ((f32[32,32,128]{2,1,0:T(8,128)}), f32[32,32,128]{2,1,0:T(8,128)}, u32[]{:S(2)}, u32[]{:S(2)}) async-start(f32[32,32,128]{2,1,0:T(8,128)} %get-tuple-element.69), calls=%async_computation.6 | async-start | bytes 1048576 | tf_op jit(solution)/shard_map/all_to_all | solution.py:569
  151.9 0.6 copy.24
  152.6 1.6 reshape.28
  154.2 14.8 %all-to-all-done.6.refs_1_ = f32[32,32,128]{2,1,0:T(8,128)} async-done(((f32[32,32,128]{2,1,0:T(8,128)}), f32[32,32,128]{2,1,0:T(8,128)}, u32[]{:S(2)}, u32[]{:S(2)}) %all-to-all-start.6) | async-done | bytes 524320 | tf_op jit(solution)/shard_map/all_to_all | solution.py:569
  168.9 2.0 %update.1 = f32[53,1,256]{2,1,0:T(1,128)} custom-call(s32[8,128]{1,0:T(8,128)} %copy-done.8, f32[32,32,128]{2,1,0:T(8,128)} %all-to-all-done.6.refs_1_, f32[53,256]{1,0:T(8,128)} %bitcast.31, f32[128,512]{1,0:T(8,128)} %constant.24.clone.refs_3_), custom_call_target="tpu_custom_call" | custom-call | tf_op jit(solution)/shard_map/update/pallas_call | solution.py:71
  (27 shorter events, 0.1 us)
Async XLA Ops:
  0.7 0.8 copy-start.3
  1.5 0.8 copy-start.7
  5.3 31.4 %all-to-all-start = ((f32[32,40,128]{2,1,0:T(8,128)}), f32[32,40,128]{2,1,0:T(8,128)}, u32[]{:S(2)}, u32[]{:S(2)}) async-start(f32[32,40,128]{2,1,0:T(8,128)} %gather.1), calls=%async_computation | async-start | bytes 1310720 | tf_op jit(solution)/shard_map/all_to_all | solution.py:569
  16.9 7.9 %copy-start.10 = (f32[53,1,2,256]{3,2,1,0:T(2,128)S(1)}, f32[53,1,2,256]{3,2,1,0:T(2,128)}, u32[]{:S(2)}) copy-start(f32[53,1,2,256]{3,2,1,0:T(2,128)} %param.14) | copy-start | bytes 325636
  17.7 7.8 %copy-start.9 = (s32[32,1]{0,1:T(1,128)S(1)}, s32[32,1]{0,1:T(1,128)}, u32[]{:S(2)}) copy-start(s32[32,1]{0,1:T(1,128)} %param.23) | copy-start | bytes 388
  17.7 7.8 %copy-start.18 = (s32[32,4]{0,1:T(4,128)S(1)}, s32[32,4]{0,1:T(4,128)}, u32[]{:S(2)}) copy-start(s32[32,4]{0,1:T(4,128)} %param.21) | copy-start | bytes 1540
  17.8 8.4 %copy-start.5 = (f32[53,325]{1,0:T(8,128)S(1)}, f32[53,325]{1,0:T(8,128)}, u32[]{:S(2)}) copy-start(f32[53,325]{1,0:T(8,128)} %stoich.1) | copy-start | bytes 206704
  17.8 8.4 %copy-start.6 = (f32[325,53]{0,1:T(8,128)S(1)}, f32[325,53]{0,1:T(8,128)}, u32[]{:S(2)}) copy-start(f32[325,53]{0,1:T(8,128)} %param.17) | copy-start | bytes 206704
  27.7 0.6 copy-start
  28.3 0.7 copy-start.1
  28.9 0.6 copy-start.2
  29.6 0.6 copy-start.8
  40.8 15.9 %all-to-all-start.1 = ((f32[32,16,128]{2,1,0:T(8,128)}), f32[32,16,128]{2,1,0:T(8,128)}, u32[]{:S(2)}, u32[]{:S(2)}) async-start(f32[32,16,128]{2,1,0:T(8,128)} %get-tuple-element.37), calls=%async_computation.1 | async-start | bytes 524288 | tf_op jit(solution)/shard_map/all_to_all | solution.py:569
  46.5 8.1 %collective-permute-start = (f32[56,256]{1,0:T(8,128)}, f32[56,256]{1,0:T(8,128)S(1)}, u32[]{:S(2)}, u32[]{:S(2)}) collective-permute-start(f32[56,256]{1,0:T(8,128)} %get-tuple-element.38), channel_id=1, source_target_pairs={{0,1},{1,0},{2,3},{3,2},{4,5},{5,4},{6,7},{7,6},{8,9},{9,8},{10,11... | collective-permute-start | bytes 172040 | tf_op jit(solution)/shard_map/ppermute | solution.py:621
  46.6 8.0 %collective-permute-start.1 = (f32[56,256]{1,0:T(8,128)}, f32[56,256]{1,0:T(8,128)S(1)}, u32[]{:S(2)}, u32[]{:S(2)}) collective-permute-start(f32[56,256]{1,0:T(8,128)} %get-tuple-element.39), channel_id=1, source_target_pairs={{0,7},{1,2},{2,1},{3,4},{4,3},{5,6},{6,5},{7,0},{8,15},{9,10},{10,... | collective-permute-start | bytes 172040 | tf_op jit(solution)/shard_map/ppermute | solution.py:622
  54.6 2.2 %copy-start.11 = (f32[56,256]{1,0:T(8,128)}, f32[56,256]{1,0:T(8,128)S(1)}, u32[]{:S(2)}) copy-start(f32[56,256]{1,0:T(8,128)S(1)} %collective-permute-done.refs_2_) | copy-start | bytes 172036
  54.6 2.1 %copy-start.12 = (f32[56,256]{1,0:T(8,128)}, f32[56,256]{1,0:T(8,128)S(1)}, u32[]{:S(2)}) copy-start(f32[56,256]{1,0:T(8,128)S(1)} %collective-permute-done.1.refs_3_) | copy-start | bytes 172036
  60.5 18.4 %all-to-all-start.2 = ((f32[32,16,128]{2,1,0:T(8,128)}), f32[32,16,128]{2,1,0:T(8,128)}, u32[]{:S(2)}, u32[]{:S(2)}) async-start(f32[32,16,128]{2,1,0:T(8,128)} %get-tuple-element.45), calls=%async_computation.2 | async-start | bytes 524288 | tf_op jit(solution)/shard_map/all_to_all | solution.py:569
  68.8 3.9 %collective-permute-start.2 = (f32[56,256]{1,0:T(8,128)}, f32[56,256]{1,0:T(8,128)S(1)}, u32[]{:S(2)}, u32[]{:S(2)}) collective-permute-start(f32[56,256]{1,0:T(8,128)} %get-tuple-element.46), channel_id=1, source_target_pairs={{0,1},{1,0},{2,3},{3,2},{4,5},{5,4},{6,7},{7,6},{8,9},{9,8},{10,11... | collective-permute-start | bytes 172040 | tf_op jit(solution)/shard_map/ppermute | solution.py:621
  68.9 5.1 %collective-permute-start.3 = (f32[56,256]{1,0:T(8,128)}, f32[56,256]{1,0:T(8,128)S(1)}, u32[]{:S(2)}, u32[]{:S(2)}) collective-permute-start(f32[56,256]{1,0:T(8,128)} %get-tuple-element.47), channel_id=1, source_target_pairs={{0,7},{1,2},{2,1},{3,4},{4,3},{5,6},{6,5},{7,0},{8,15},{9,10},{10,... | collective-permute-start | bytes 172040 | tf_op jit(solution)/shard_map/ppermute | solution.py:622
  72.8 6.1 %copy-start.14 = (f32[56,256]{1,0:T(8,128)}, f32[56,256]{1,0:T(8,128)S(1)}, u32[]{:S(2)}) copy-start(f32[56,256]{1,0:T(8,128)S(1)} %collective-permute-done.2.refs_2_) | copy-start | bytes 172036
  74.0 4.9 %copy-start.16 = (f32[56,256]{1,0:T(8,128)}, f32[56,256]{1,0:T(8,128)S(1)}, u32[]{:S(2)}) copy-start(f32[56,256]{1,0:T(8,128)S(1)} %collective-permute-done.3.refs_3_) | copy-start | bytes 172036
  82.7 16.6 %all-to-all-start.3 = ((f32[32,16,128]{2,1,0:T(8,128)}), f32[32,16,128]{2,1,0:T(8,128)}, u32[]{:S(2)}, u32[]{:S(2)}) async-start(f32[32,16,128]{2,1,0:T(8,128)} %get-tuple-element.51), calls=%async_computation.3 | async-start | bytes 524288 | tf_op jit(solution)/shard_map/all_to_all | solution.py:569
  89.1 4.8 %collective-permute-start.4 = (f32[56,256]{1,0:T(8,128)}, f32[56,256]{1,0:T(8,128)S(1)}, u32[]{:S(2)}, u32[]{:S(2)}) collective-permute-start(f32[56,256]{1,0:T(8,128)} %get-tuple-element.52), channel_id=1, source_target_pairs={{0,1},{1,0},{2,3},{3,2},{4,5},{5,4},{6,7},{7,6},{8,9},{9,8},{10,11... | collective-permute-start | bytes 172040 | tf_op jit(solution)/shard_map/ppermute | solution.py:621
  89.3 5.1 %collective-permute-start.5 = (f32[56,256]{1,0:T(8,128)}, f32[56,256]{1,0:T(8,128)S(1)}, u32[]{:S(2)}, u32[]{:S(2)}) collective-permute-start(f32[56,256]{1,0:T(8,128)} %get-tuple-element.53), channel_id=1, source_target_pairs={{0,7},{1,2},{2,1},{3,4},{4,3},{5,6},{6,5},{7,0},{8,15},{9,10},{10,... | collective-permute-start | bytes 172040 | tf_op jit(solution)/shard_map/ppermute | solution.py:622
  93.9 5.4 %copy-start.13 = (f32[56,256]{1,0:T(8,128)}, f32[56,256]{1,0:T(8,128)S(1)}, u32[]{:S(2)}) copy-start(f32[56,256]{1,0:T(8,128)S(1)} %collective-permute-done.4.refs_2_) | copy-start | bytes 172036
  94.5 4.8 %copy-start.15 = (f32[56,256]{1,0:T(8,128)}, f32[56,256]{1,0:T(8,128)S(1)}, u32[]{:S(2)}) copy-start(f32[56,256]{1,0:T(8,128)S(1)} %collective-permute-done.5.refs_3_) | copy-start | bytes 172036
  103.0 48.9 %copy-start.4 = (f32[53,1,256]{2,1,0:T(1,128)S(1)}, f32[53,1,256]{2,1,0:T(1,128)}, u32[]{:S(2)}) copy-start(f32[53,1,256]{2,1,0:T(1,128)} %patch.1) | copy-start | bytes 162820
  103.0 16.9 %all-to-all-start.4 = ((f32[32,16,128]{2,1,0:T(8,128)}), f32[32,16,128]{2,1,0:T(8,128)}, u32[]{:S(2)}, u32[]{:S(2)}) async-start(f32[32,16,128]{2,1,0:T(8,128)} %get-tuple-element.57), calls=%async_computation.4 | async-start | bytes 524288 | tf_op jit(solution)/shard_map/all_to_all | solution.py:569
  109.6 5.1 %collective-permute-start.6 = (f32[56,256]{1,0:T(8,128)}, f32[56,256]{1,0:T(8,128)S(1)}, u32[]{:S(2)}, u32[]{:S(2)}) collective-permute-start(f32[56,256]{1,0:T(8,128)} %get-tuple-element.58), channel_id=1, source_target_pairs={{0,1},{1,0},{2,3},{3,2},{4,5},{5,4},{6,7},{7,6},{8,9},{9,8},{10,11... | collective-permute-start | bytes 172040 | tf_op jit(solution)/shard_map/ppermute | solution.py:621
  109.7 5.2 %collective-permute-start.7 = (f32[56,256]{1,0:T(8,128)}, f32[56,256]{1,0:T(8,128)}, u32[]{:S(2)}, u32[]{:S(2)}) collective-permute-start(f32[56,256]{1,0:T(8,128)} %get-tuple-element.59), channel_id=1, source_target_pairs={{0,7},{1,2},{2,1},{3,4},{4,3},{5,6},{6,5},{7,0},{8,15},{9,10},{10,... | collective-permute-start | bytes 172040 | tf_op jit(solution)/shard_map/ppermute | solution.py:622
  114.6 5.3 %copy-start.17 = (f32[56,256]{1,0:T(8,128)}, f32[56,256]{1,0:T(8,128)S(1)}, u32[]{:S(2)}) copy-start(f32[56,256]{1,0:T(8,128)S(1)} %collective-permute-done.6.refs_2_) | copy-start | bytes 172036
  146.4 22.5 %all-to-all-start.6 = ((f32[32,32,128]{2,1,0:T(8,128)}), f32[32,32,128]{2,1,0:T(8,128)}, u32[]{:S(2)}, u32[]{:S(2)}) async-start(f32[32,32,128]{2,1,0:T(8,128)} %get-tuple-element.69), calls=%async_computation.6 | async-start | bytes 1048576 | tf_op jit(solution)/shard_map/all_to_all | solution.py:569

commit v4 on v3

--- a/solution.py
+++ b/solution.py
@@ -92,7 +92,10 @@
     return high, middle, low
 
 
-def gather_kernel(ids, patch, lists, out, hot):
+def gather_kernel(ids, patch_out, lists_out, out, patch, lists, arrived, hot, slots, sent):
+    copies = start([(patch_out, patch), (lists_out, lists)], arrived)
+    for copy in copies:
+        copy.wait()
     species = patch.shape[0]
     row = lax.broadcasted_iota(jnp.int32, (species, FACE), 0)
     lane = lax.broadcasted_iota(jnp.int32, (species, FACE), 1)
@@ -128,26 +131,31 @@
         ]
         hot[SLOT * g : SLOT * g + 2 * SLOT, :] = jnp.concatenate(pair, axis=0).astype(jnp.bfloat16)
     step = 8
+    copies = []
     for g in range(0, groups, step):
         got = jnp.dot(
             hot[SLOT * g : SLOT * (g + step), :], parts, preferred_element_type=jnp.float32
         )
         got = got[:, 0:128] + got[:, 128:256] + got[:, 256:384]
         for k in range(step):
-            out[g + k] = got[SLOT * k : SLOT * k + SLOT]
+            slots[g + k] = got[SLOT * k : SLOT * k + SLOT]
+        part = pl.ds(g, step)
+        copies.append(pltpu.make_async_copy(slots.at[part], out.at[part], sent.at[g // step]))
+        copies[-1].start()
+    for copy in copies:
+        copy.wait()
 
 
 def prepare_kernel(ids, owned, diffusion, stoich, orders, scale, stoich_out, orders_out, sources):
     me = ids[0]
-    found = [jnp.int32(-1)] * 4
-    for g in range(owned.shape[1]):
-        entry = owned[0, g]
-        found = [jnp.where(entry == me * 4 + m, g, found[m]) for m in range(4)]
+    group = lax.broadcasted_iota(jnp.int32, owned.shape, 1)
     for m in range(4):
-        sources[0, m] = found[m]
+        sources[0, m] = jnp.max(jnp.where(owned[...] == me * 4 + m, group, -1))
     d = diffusion[...]
-    species = d.shape[0]
-    column = jnp.concatenate([d, jnp.zeros((PAD - species, 1), jnp.float32)], axis=0)
+    species = d.shape[1]
+    row = lax.broadcasted_iota(jnp.int32, (PAD, species), 0)
+    lane = lax.broadcasted_iota(jnp.int32, (PAD, species), 1)
+    column = jnp.sum(jnp.where(row == lane, d, 0.0), axis=1, keepdims=True)
 
     def total(value):
         return jnp.sum(jnp.sum(value, axis=0, keepdims=True), axis=1, keepdims=True)
@@ -357,7 +365,8 @@
     progress = jnp.dot(
         orders[...], jnp.concatenate([high, low, high], axis=0), preferred_element_type=jnp.float32
     )
-    high, low = two(progress * rates[...])
+    progress = [progress[:, FACE * x : FACE * x + FACE] * rates[x] for x in range(2)]
+    high, low = two(jnp.concatenate(progress, axis=1))
     chemistry = jnp.dot(stoich[...], high, preferred_element_type=jnp.float32)
     chemistry = chemistry[:PAD] + chemistry[PAD:]
     chemistry = chemistry + jnp.dot(stoich[:PAD, :], low, preferred_element_type=jnp.float32)
@@ -465,7 +474,7 @@
 def finish_kernel(*refs):
     n = ITERS
     outside, outs, inside = refs[: n + 4], refs[n + 4 : n + 6], refs[n + 6 : n + 11]
-    arrived, result, mean, rows, sent = refs[n + 11 :]
+    arrived, result, mean, sent = refs[n + 11 :]
     lines, scale, meta, average, fields = inside
     copies = start(
         zip(outside, [lines, scale, meta, average] + [fields.at[k] for k in range(n)]), arrived
@@ -500,10 +509,9 @@
     mean[...] = jnp.where(lane < 64, got[:32], got[32:])
     home = meta[4, meta[5, 0]] // 4
     copies = start([(mean, outs[1].at[home])], sent)
-    interleave(rows, total)
-    for half in range(2):
-        lanes = slice(128 * half, 128 * half + 128)
-        result[:, lanes] = rows[half, 0 : result.shape[0], :]
+    species = result.shape[0]
+    result[:, 0, :] = total[:species]
+    result[:, 1, :] = total[PAD : PAD + species]
     copies.append(pltpu.make_async_copy(result, outs[0], sent.at[1]))
     copies[1].start()
     for copy in copies:
@@ -534,7 +542,7 @@
         preferred_element_type=jnp.float32,
     )
     got = got[0:species, :FACE] + got[64 : 64 + species, FACE:]
-    out[:, 0, :] = jnp.where(covered >= 0, got, patch[...])
+    out[:, 0, :] = jnp.where(covered >= 0, got, patch[:, 0, :])
 
 
 def on_device(
@@ -569,22 +577,36 @@
         return lax.all_to_all(slots, "grp", 0, 0, tiled=True)
 
     (asked,) = call(
-        gather_kernel, "gather", [(groups, SLOT, 128)], (ids, coarse_field, ghost_list), [SMEM] + [VMEM] * 2,
-        [pltpu.VMEM((groups * SLOT, 2 * FACE), jnp.bfloat16)],
+        gather_kernel,
+        "gather",
+        [(groups, SLOT, 128)],
+        (ids, coarse_field, ghost_list),
+        [SMEM] + [HBM] * 2,
+        [
+            pltpu.VMEM(coarse_field.shape, f32),
+            pltpu.VMEM(ghost_list.shape, jnp.int32),
+            pltpu.SemaphoreType.DMA((2,)),
+            pltpu.VMEM((groups * SLOT, 2 * FACE), jnp.bfloat16),
+            pltpu.VMEM((groups, SLOT, 128), f32),
+            pltpu.SemaphoreType.DMA((groups // 8,)),
+        ],
+        [HBM],
+        WHOLE,
     )
     received = exchange(asked)
     scale, stoich_s, orders_s, sources = call(
         prepare_kernel,
         "prepare",
         [(ROWS, 128), (2 * PAD, reactions, jnp.bfloat16), (reactions, 3 * PAD, jnp.bfloat16), (8, 128, jnp.int32)],
-        (ids, owned, diffusion.reshape(species, 1), stoich, orders.T),
-        [SMEM] * 2 + [VMEM] * 3,
+        (ids, owned, diffusion.reshape(1, species), stoich, orders.T),
+        [SMEM] + [VMEM] * 4,
         (),
         [VMEM] * 3 + [SMEM],
-    )
-    rates_s = rates.reshape(reactions, 2 * FACE)
+        WHOLE,
+    )
+    rates_s = jnp.moveaxis(rates[:, 0], 1, 0)
     inverse = precond.reshape(species, 2 * species, FACE)
-    source = source_term.reshape(2 * species, FACE)
+    source, rates_s = lax.optimization_barrier((source_term.reshape(2 * species, FACE), rates_s))
     faces = jnp.asarray(FACES)
     inside = jnp.asarray(INSIDE)
     outs = [(ROWS, FACE), (PAD, FACE), (PAD, FACE), (ROWS, FACE), (groups, FS, 128)]
@@ -666,28 +688,28 @@
     correction, slots = call(
         finish_kernel,
         "finish",
-        [(2 * species, FACE), (groups, 32, 128)],
+        [(species, 2, FACE), (groups, 32, 128)],
         (lines, scale, meta, average) + tuple(directions),
         [HBM] * (4 + ITERS),
         [pltpu.VMEM(lines.shape, f32), pltpu.VMEM((ROWS, 128), f32)]
         + [pltpu.SMEM(meta.shape, jnp.int32), pltpu.VMEM(average.shape, f32)]
         + [pltpu.VMEM((ITERS, ROWS, FACE), f32), pltpu.SemaphoreType.DMA((ITERS + 4,))]
-        + [pltpu.VMEM((2 * species, FACE), f32), pltpu.VMEM((32, 128), f32)]
-        + rows
+        + [pltpu.VMEM((species, 2, FACE), f32), pltpu.VMEM((32, 128), f32)]
         + [pltpu.SemaphoreType.DMA((2,))],
         [HBM] * 2,
         WHOLE,
     )
     received = exchange(slots)
+    received, correction = lax.optimization_barrier((received, correction))
     halves = jnp.asarray(HALVES)
     (updated,) = call(
         update_kernel,
         "update",
         [(species, 1, FACE)],
-        (sources, received, coarse_field.reshape(species, FACE), halves),
+        (sources, received, coarse_field, halves),
         [HBM] * 4,
         [pltpu.SMEM((8, 128), jnp.int32), pltpu.VMEM(received.shape, f32)]
-        + [pltpu.VMEM((species, FACE), f32), pltpu.VMEM(halves.shape, f32)]
+        + [pltpu.VMEM(coarse_field.shape, f32), pltpu.VMEM(halves.shape, f32)]
         + [pltpu.SemaphoreType.DMA((4,))],
         limit=WHOLE,
     )

time: 172 us -> 172 us (level)
  blocking collectives: 20.9 us -> 45.4 us
  waiting for transfers between devices: 40.2 us -> 22 us
  local copies, waits for them, and re-layouts: 17.7 us -> 11.3 us
  starting transfers between devices: 53 us -> 50.9 us
    all_to_all x0 -> x1, blocking collectives: none -> 22.8 us  [exchange(): return lax.all_to_all(slots, 'grp', 0, 0, tiled=True)]
    all_to_all x6 -> x5, waiting for transfers between devices: 38.1 us -> 22 us  [exchange(): return lax.all_to_all(slots, 'grp', 0, 0, tiled=True)]
    all_to_all x6 -> x5, starting transfers between devices: 44.1 us -> 37 us  [exchange(): return lax.all_to_all(slots, 'grp', 0, 0, tiled=True)]
    ppermute x4, starting transfers between devices: 8.36 us -> 13.6 us  [on_device(): far_in = lax.ppermute(far, 'box', odd_swap)]
    unnamed x41 -> x23, local copies, waits for them, and re-layouts: 6.96 us -> 2.05 us
    ppermute x4, waiting for transfers between devices: 2.06 us -> 0.01 us  [on_device(): far_in = lax.ppermute(far, 'box', odd_swap)]
  transfers between devices with their start and end apart: 14 -> 13, of which waited for: 9 -> 5; matrix products, arithmetic and copies ran while one was open for 8% -> 7% of each run, Pallas kernels for 7% -> 7%
where the time goes in v4:
time: 172 us; the launch traced here: 171 us
  starting transfers between devices  50.9 us (30%)
  blocking collectives  45.4 us (26%)
  Pallas kernels  39.3 us (23%)
  waiting for transfers between devices  22 us (13%)
  local copies, waits for them, and re-layouts  11.3 us (7%)
    pallas_call x13, Pallas kernels, call(): pl.pallas_call(kernel, out_shape=[jax.ShapeDtypeStruct(s[:-1], s[-1]) if...  39.3 us
    all_to_all x5, starting transfers between devices, exchange(): return lax.all_to_all(slots, 'grp', 0, 0, tiled=True)  37 us
    all_to_all x1, blocking collectives, exchange(): return lax.all_to_all(slots, 'grp', 0, 0, tiled=True)  22.8 us
    all_to_all x1, blocking collectives, on_device(): lines = lax.all_to_all(lines, ('grp', 'box'), 0, 0, tiled=True)  22.6 us
    all_to_all x5, waiting for transfers between devices, exchange(): return lax.all_to_all(slots, 'grp', 0, 0, tiled=True)  22 us
    ppermute x4, starting transfers between devices, on_device(): far_in = lax.ppermute(far, 'box', odd_swap)  13.6 us
    reshape x1, local copies, waits for them, and re-layouts, on_device(): inverse = precond.reshape(species, 2 * species, FACE)  7.02 us
  transfers between devices with their start and end apart: 13, of which 5 were waited for; matrix products, arithmetic and copies ran while one was open for 7% of the time, Pallas kernels for 7%

profile of v4, /device:TPU:2, one launch (start us, length us, event | category | flops | bytes accessed | tf_op | source)
XLA Modules:
  0.0 170.6 jit_solution(4994494023744614909)
XLA Ops:
  0.6 0.6 pad_add_fusion.1.ids
  1.2 3.8 %gather.1 = f32[32,40,128]{2,1,0:T(8,128)} custom-call(s32[3]{0:T(128)} %pad_add_fusion.1.ids, f32[53,1,256]{2,1,0:T(1,128)} %refs_2_.1, s32[32,1,160]{2,1,0:T(1,128)} %lists_out.1), custom_call_target="tpu_custom_call" | custom-call | tf_op jit(solution)/shard_map/gather/pallas_call | solution.py:71
  5.0 11.7 %all-to-all-start = ((f32[32,40,128]{2,1,0:T(8,128)}), f32[32,40,128]{2,1,0:T(8,128)}, u32[]{:S(2)}, u32[]{:S(2)}) async-start(f32[32,40,128]{2,1,0:T(8,128)} %gather.1), calls=%async_computation | async-start | bytes 1310720 | tf_op jit(solution)/shard_map/all_to_all | solution.py:577
  16.7 1.6 reshape.18.refs_2_
  18.3 2.0 %copy.22 = f32[325,1,2,256]{3,0,2,1:T(8,128)} copy(f32[325,1,2,256]{3,2,1,0:T(2,128)} %param.18) | data formatting | bytes 1331200 | tf_op args[4]
  20.3 7.0 %reshape.20.refs_5_.refs_7_ = bf16[53,106,256]{2,1,0:T(8,128)(2,1)} reshape(bf16[53,53,1,2,256]{4,3,2,1,0:T(2,128)(2,1)} %param.19) | data formatting | bytes 5752832 | tf_op jit(solution)/shard_map/reshape | solution.py:608
  27.3 0.0 copy-done.8
  27.3 0.0 copy-done.9
  27.3 0.0 copy-done.10
  27.4 0.6 pad.9.refs_0_.refs_2_
  28.0 1.9 %prepare.1 = (f32[112,128]{1,0:T(8,128)}, bf16[112,325]{1,0:T(8,128)(2,1)}, bf16[325,168]{1,0:T(8,128)(2,1)}, s32[8,128]{1,0:T(8,128)}) custom-call(s32[3]{0:T(128)} %pad_add_fusion.1.ids, s32[1,32]{1,0:T(1,128)} %bitcast.27, f32[1,53]{1,0:T(1,128)} %bitcast.30, f32[53,325]{1,0:T(8,128)} %stoich.1, f32[53,325]{1,0:T(8,128)} %bitcast.26), custom_call_target="tpu_custom_call" | custom-call | tf_op jit(solution)/shard_map/prepare/pallas_call | solution.py:71
  29.9 6.5 %all-to-all-done.refs_1_ = f32[32,40,128]{2,1,0:T(8,128)} async-done(((f32[32,40,128]{2,1,0:T(8,128)}), f32[32,40,128]{2,1,0:T(8,128)}, u32[]{:S(2)}, u32[]{:S(2)}) %all-to-all-start) | async-done | bytes 655392 | tf_op jit(solution)/shard_map/all_to_all | solution.py:577
  36.4 4.2 %first.1 = (f32[112,256]{1,0:T(8,128)}, f32[56,256]{1,0:T(8,128)}, f32[56,256]{1,0:T(8,128)}, f32[112,256]{1,0:T(8,128)}, f32[32,16,128]{2,1,0:T(8,128)}) custom-call(s32[8,128]{1,0:T(8,128)} %pad.9.refs_0_.refs_2_, f32[32,40,128]{2,1,0:T(8,128)} %all-to-all-done.refs_1_, f32[106,256]{1,0:T(8,128)} %reshape.18.refs_2_, ...), custom_call_target="tpu_custom_call" | custom-call | tf_op jit(solution)/shard_map/first/pallas_call | solution.py:71
  40.6 5.6 %all-to-all-start.1 = ((f32[32,16,128]{2,1,0:T(8,128)}), f32[32,16,128]{2,1,0:T(8,128)}, u32[]{:S(2)}, u32[]{:S(2)}) async-start(f32[32,16,128]{2,1,0:T(8,128)} %get-tuple-element.42), calls=%async_computation.1 | async-start | bytes 524288 | tf_op jit(solution)/shard_map/all_to_all | solution.py:577
  46.2 0.1 collective-permute-start
  46.3 3.1 %collective-permute-start.1 = (f32[56,256]{1,0:T(8,128)}, f32[56,256]{1,0:T(8,128)S(1)}, u32[]{:S(2)}, u32[]{:S(2)}) collective-permute-start(f32[56,256]{1,0:T(8,128)} %get-tuple-element.44), channel_id=1, source_target_pairs={{0,7},{1,2},{2,1},{3,4},{4,3},{5,6},{6,5},{7,0},{8,15},{9,10},{10,... | collective-permute-start | bytes 172040 | tf_op jit(solution)/shard_map/ppermute | solution.py:644
  49.4 2.6 %local0.1 = (f32[112,256]{1,0:T(8,128)}, f32[8,128]{1,0:T(8,128)}) custom-call(f32[112,256]{1,0:T(8,128)} %get-tuple-element.45.refs_0_.refs_4_, f32[112,256]{1,0:T(8,128)} %get-tuple-element.46.refs_1_.refs_7_, f32[112,128]{1,0:T(8,128)} %get-tuple-element.41.refs_3_.refs_2_.refs_5_.refs_1_, f32[256,256]{1,0:T(8,128)} %constant.22.clone.refs_3_, ...), custom_call_target="tpu_custom_call" | custom-call | tf_op jit(solution)/shard_map/local0/pallas_call | solution.py:71
  52.1 0.0 collective-permute-done.refs_2_
  52.1 0.0 copy-start.1
  52.1 0.0 collective-permute-done.1.refs_3_
  52.1 0.0 copy-start.4
  52.1 4.4 %all-to-all-done.1.refs_1_ = f32[32,16,128]{2,1,0:T(8,128)} async-done(((f32[32,16,128]{2,1,0:T(8,128)}), f32[32,16,128]{2,1,0:T(8,128)}, u32[]{:S(2)}, u32[]{:S(2)}) %all-to-all-start.1) | async-done | bytes 262176 | tf_op jit(solution)/shard_map/all_to_all | solution.py:577
  56.5 0.0 copy-done.1
  56.5 0.0 copy-done.4
  56.5 3.7 %combine0.1 = (f32[112,256]{1,0:T(8,128)}, f32[56,256]{1,0:T(8,128)}, f32[56,256]{1,0:T(8,128)}, f32[112,256]{1,0:T(8,128)}, f32[32,16,128]{2,1,0:T(8,128)}) custom-call(s32[8,128]{1,0:T(8,128)} %pad.9.refs_0_.refs_2_, f32[32,16,128]{2,1,0:T(8,128)} %all-to-all-done.1.refs_1_, f32[56,256]{1,0:T(8,128)} %copy-done.1, f32[56,256]{1,0:T(8,128)} %copy-done.4, ...), custom_call_target="tpu_custom_call" | custom-call | tf_op jit(solution)/shard_map/combine0/pallas_call | solution.py:71
  60.2 6.4 %all-to-all-start.2 = ((f32[32,16,128]{2,1,0:T(8,128)}), f32[32,16,128]{2,1,0:T(8,128)}, u32[]{:S(2)}, u32[]{:S(2)}) async-start(f32[32,16,128]{2,1,0:T(8,128)} %get-tuple-element.51), calls=%async_computation.2 | async-start | bytes 524288 | tf_op jit(solution)/shard_map/all_to_all | solution.py:577
  66.6 0.1 collective-permute-start.2
  66.7 3.1 %collective-permute-start.3 = (f32[56,256]{1,0:T(8,128)}, f32[56,256]{1,0:T(8,128)S(1)}, u32[]{:S(2)}, u32[]{:S(2)}) collective-permute-start(f32[56,256]{1,0:T(8,128)} %get-tuple-element.53), channel_id=1, source_target_pairs={{0,7},{1,2},{2,1},{3,4},{4,3},{5,6},{6,5},{7,0},{8,15},{9,10},{10,... | collective-permute-start | bytes 172040 | tf_op jit(solution)/shard_map/ppermute | solution.py:644
  69.8 2.6 %local1.1 = (f32[112,256]{1,0:T(8,128)}, f32[8,128]{1,0:T(8,128)}) custom-call(f32[112,256]{1,0:T(8,128)} %get-tuple-element.54.refs_0_.refs_5_, f32[112,256]{1,0:T(8,128)} %get-tuple-element.55.refs_1_.refs_8_, f32[112,128]{1,0:T(8,128)} %get-tuple-element.41.refs_3_.refs_2_.refs_5_.refs_1_, f32[256,256]{1,0:T(8,128)} %constant.22.clone.refs_3_, ...), custom_call_target="tpu_custom_call" | custom-call | tf_op jit(solution)/shard_map/local1/pallas_call | solution.py:71
  72.5 0.0 collective-permute-done.2.refs_2_
  72.5 0.0 copy-start.2
  72.5 0.0 collective-permute-done.3.refs_3_
  72.5 0.0 copy-start.5
  72.5 4.1 %all-to-all-done.2.refs_1_ = f32[32,16,128]{2,1,0:T(8,128)} async-done(((f32[32,16,128]{2,1,0:T(8,128)}), f32[32,16,128]{2,1,0:T(8,128)}, u32[]{:S(2)}, u32[]{:S(2)}) %all-to-all-start.2) | async-done | bytes 262176 | tf_op jit(solution)/shard_map/all_to_all | solution.py:577
  76.7 0.0 copy-done.2
  76.7 0.0 copy-done.5
  76.7 3.7 %combine1.1 = (f32[112,256]{1,0:T(8,128)}, f32[56,256]{1,0:T(8,128)}, f32[56,256]{1,0:T(8,128)}, f32[112,256]{1,0:T(8,128)}, f32[32,16,128]{2,1,0:T(8,128)}) custom-call(s32[8,128]{1,0:T(8,128)} %pad.9.refs_0_.refs_2_, f32[32,16,128]{2,1,0:T(8,128)} %all-to-all-done.2.refs_1_, f32[56,256]{1,0:T(8,128)} %copy-done.2, f32[56,256]{1,0:T(8,128)} %copy-done.5, ...), custom_call_target="tpu_custom_call" | custom-call | tf_op jit(solution)/shard_map/combine1/pallas_call | solution.py:71
  80.4 6.5 %all-to-all-start.3 = ((f32[32,16,128]{2,1,0:T(8,128)}), f32[32,16,128]{2,1,0:T(8,128)}, u32[]{:S(2)}, u32[]{:S(2)}) async-start(f32[32,16,128]{2,1,0:T(8,128)} %get-tuple-element.57), calls=%async_computation.3 | async-start | bytes 524288 | tf_op jit(solution)/shard_map/all_to_all | solution.py:577
  86.9 0.1 collective-permute-start.4
  87.0 3.7 %collective-permute-start.5 = (f32[56,256]{1,0:T(8,128)}, f32[56,256]{1,0:T(8,128)S(1)}, u32[]{:S(2)}, u32[]{:S(2)}) collective-permute-start(f32[56,256]{1,0:T(8,128)} %get-tuple-element.59), channel_id=1, source_target_pairs={{0,7},{1,2},{2,1},{3,4},{4,3},{5,6},{6,5},{7,0},{8,15},{9,10},{10,... | collective-permute-start | bytes 172040 | tf_op jit(solution)/shard_map/ppermute | solution.py:644
  90.7 2.7 %local2.1 = (f32[112,256]{1,0:T(8,128)}, f32[8,128]{1,0:T(8,128)}) custom-call(f32[112,256]{1,0:T(8,128)} %get-tuple-element.60.refs_0_.refs_6_, f32[112,256]{1,0:T(8,128)} %get-tuple-element.61.refs_1_.refs_9_, f32[112,128]{1,0:T(8,128)} %get-tuple-element.41.refs_3_.refs_2_.refs_5_.refs_1_, f32[256,256]{1,0:T(8,128)} %constant.22.clone.refs_3_, ...), custom_call_target="tpu_custom_call" | custom-call | tf_op jit(solution)/shard_map/local2/pallas_call | solution.py:71
  93.4 0.0 collective-permute-done.4.refs_2_
  93.4 0.0 copy-start
  93.4 0.0 collective-permute-done.5.refs_3_
  93.4 0.0 copy-start.3
  93.4 3.7 %all-to-all-done.3.refs_1_ = f32[32,16,128]{2,1,0:T(8,128)} async-done(((f32[32,16,128]{2,1,0:T(8,128)}), f32[32,16,128]{2,1,0:T(8,128)}, u32[]{:S(2)}, u32[]{:S(2)}) %all-to-all-start.3) | async-done | bytes 262176 | tf_op jit(solution)/shard_map/all_to_all | solution.py:577
  97.2 0.0 copy-done
  97.2 0.0 copy-done.3
  97.2 3.7 %combine2.1 = (f32[112,256]{1,0:T(8,128)}, f32[56,256]{1,0:T(8,128)}, f32[56,256]{1,0:T(8,128)}, f32[112,256]{1,0:T(8,128)}, f32[32,16,128]{2,1,0:T(8,128)}) custom-call(s32[8,128]{1,0:T(8,128)} %pad.9.refs_0_.refs_2_, f32[32,16,128]{2,1,0:T(8,128)} %all-to-all-done.3.refs_1_, f32[56,256]{1,0:T(8,128)} %copy-done, f32[56,256]{1,0:T(8,128)} %copy-done.3, ...), custom_call_target="tpu_custom_call" | custom-call | tf_op jit(solution)/shard_map/combine2/pallas_call | solution.py:71
  100.9 6.8 %all-to-all-start.4 = ((f32[32,16,128]{2,1,0:T(8,128)}), f32[32,16,128]{2,1,0:T(8,128)}, u32[]{:S(2)}, u32[]{:S(2)}) async-start(f32[32,16,128]{2,1,0:T(8,128)} %get-tuple-element.63), calls=%async_computation.4 | async-start | bytes 524288 | tf_op jit(solution)/shard_map/all_to_all | solution.py:577
  107.7 0.1 collective-permute-start.6
  107.8 3.6 %collective-permute-start.7 = (f32[56,256]{1,0:T(8,128)}, f32[56,256]{1,0:T(8,128)S(1)}, u32[]{:S(2)}, u32[]{:S(2)}) collective-permute-start(f32[56,256]{1,0:T(8,128)} %get-tuple-element.65), channel_id=1, source_target_pairs={{0,7},{1,2},{2,1},{3,4},{4,3},{5,6},{6,5},{7,0},{8,15},{9,10},{10,... | collective-permute-start | bytes 172040 | tf_op jit(solution)/shard_map/ppermute | solution.py:644
  111.5 2.7 %local3.1 = (f32[112,256]{1,0:T(8,128)}, f32[8,128]{1,0:T(8,128)}) custom-call(f32[112,256]{1,0:T(8,128)} %get-tuple-element.66.refs_0_.refs_7_, f32[112,256]{1,0:T(8,128)} %get-tuple-element.67.refs_1_.refs_10_, f32[112,128]{1,0:T(8,128)} %get-tuple-element.41.refs_3_.refs_2_.refs_5_.refs_1_, f32[256,256]{1,0:T(8,128)} %constant.22.clone.refs_3_, ...), custom_call_target="tpu_custom_call" | custom-call | tf_op jit(solution)/shard_map/local3/pallas_call | solution.py:71
  114.2 0.0 collective-permute-done.6.refs_2_
  114.2 0.0 copy-start.6
  114.2 0.0 collective-permute-done.7.refs_3_
  114.2 0.0 copy-start.7
  114.2 3.3 %all-to-all-done.4.refs_1_ = f32[32,16,128]{2,1,0:T(8,128)} async-done(((f32[32,16,128]{2,1,0:T(8,128)}), f32[32,16,128]{2,1,0:T(8,128)}, u32[]{:S(2)}, u32[]{:S(2)}) %all-to-all-start.4) | async-done | bytes 262176 | tf_op jit(solution)/shard_map/all_to_all | solution.py:577
  117.5 0.0 copy-done.7
  117.5 2.4 %last.1 = f32[256,128]{1,0:T(8,128)} custom-call(s32[8,128]{1,0:T(8,128)} %pad.9.refs_0_.refs_2_, f32[32,16,128]{2,1,0:T(8,128)} %all-to-all-done.4.refs_1_, f32[56,256]{1,0:T(8,128)} %copy-done.6, f32[56,256]{1,0:T(8,128)} %copy-done.7, f32[112,256]{1,0:T(8,128)} %get-tuple-element.68.refs_4_, f32[112,128]{1,0:T(8,128)} %get-tuple-element.41.refs_3_.refs_2_.refs_5_.refs_1_, ...), custom_call_target="tpu_custom_call" | custom-call | tf_op jit(solution)/shard_map/last/pallas_call | solution.py:71
  119.9 22.6 %all_to_all.41 = f32[256,1,128]{2,1,0:T(1,128)} all-to-all(f32[256,1,128]{2,1,0:T(1,128)} %bitcast.24), channel_id=1, replica_groups=mesh['grp'=32,'box'=8] {'grp','box'}, dimensions={0} | all-to-all | bytes 262144 | tf_op jit(solution)/shard_map/all_to_all | solution.py:686
  142.5 3.2 %finish.1 = (f32[53,2,256]{2,1,0:T(2,128)}, f32[32,32,128]{2,1,0:T(8,128)}) custom-call(f32[256,128]{1,0:T(8,128)} %bitcast.25, f32[112,128]{1,0:T(8,128)} %get-tuple-element.41.refs_3_.refs_2_.refs_5_.refs_1_, s32[8,128]{1,0:T(8,128)} %pad.9.refs_0_.refs_2_, f32[64,256]{1,0:T(8,128)} %constant.23.clone.refs_3_, ...), custom_call_target="tpu_custom_call" | custom-call | tf_op jit(solution)/shard_map/finish/pallas_call | solution.py:71
  145.7 22.8 %all_to_all.42.refs_1_ = f32[32,32,128]{2,1,0:T(8,128)} all-to-all(f32[32,32,128]{2,1,0:T(8,128)} %get-tuple-element.73), channel_id=1, replica_groups=mesh['grp'=32,'box'=8] {'grp'}, dimensions={0} | all-to-all | bytes 1048576 | tf_op jit(solution)/shard_map/all_to_all | solution.py:577
  168.4 2.0 %update.1 = f32[53,1,256]{2,1,0:T(1,128)} custom-call(s32[8,128]{1,0:T(8,128)} %get-tuple-element.76.refs_0_, f32[32,32,128]{2,1,0:T(8,128)} %all_to_all.42.refs_1_, f32[53,1,256]{2,1,0:T(1,128)} %refs_2_.1, f32[128,512]{1,0:T(8,128)} %constant.24.clone.refs_3_), custom_call_target="tpu_custom_call" | custom-call | tf_op jit(solution)/shard_map/update/pallas_call | solution.py:71
  (6 shorter events, 0.0 us)
Async XLA Ops:
  5.0 31.4 %all-to-all-start = ((f32[32,40,128]{2,1,0:T(8,128)}), f32[32,40,128]{2,1,0:T(8,128)}, u32[]{:S(2)}, u32[]{:S(2)}) async-start(f32[32,40,128]{2,1,0:T(8,128)} %gather.1), calls=%async_computation | async-start | bytes 1310720 | tf_op jit(solution)/shard_map/all_to_all | solution.py:577
  20.3 7.0 %copy-start.8 = (s32[3]{0:T(128)S(1)}, s32[3]{0:T(128)}, u32[]{:S(2)}) copy-start(s32[3]{0:T(128)} %pad_add_fusion.1.ids) | copy-start | bytes 40
  20.3 7.0 %copy-start.9 = (s32[32,1]{0,1:T(1,128)S(1)}, s32[32,1]{0,1:T(1,128)}, u32[]{:S(2)}) copy-start(s32[32,1]{0,1:T(1,128)} %param.23) | copy-start | bytes 388
  20.3 7.0 %copy-start.10 = (s32[32,4]{0,1:T(4,128)S(1)}, s32[32,4]{0,1:T(4,128)}, u32[]{:S(2)}) copy-start(s32[32,4]{0,1:T(4,128)} %param.21) | copy-start | bytes 1540
  40.6 15.9 %all-to-all-start.1 = ((f32[32,16,128]{2,1,0:T(8,128)}), f32[32,16,128]{2,1,0:T(8,128)}, u32[]{:S(2)}, u32[]{:S(2)}) async-start(f32[32,16,128]{2,1,0:T(8,128)} %get-tuple-element.42), calls=%async_computation.1 | async-start | bytes 524288 | tf_op jit(solution)/shard_map/all_to_all | solution.py:577
  46.2 5.9 %collective-permute-start = (f32[56,256]{1,0:T(8,128)}, f32[56,256]{1,0:T(8,128)S(1)}, u32[]{:S(2)}, u32[]{:S(2)}) collective-permute-start(f32[56,256]{1,0:T(8,128)} %get-tuple-element.43), channel_id=1, source_target_pairs={{0,1},{1,0},{2,3},{3,2},{4,5},{5,4},{6,7},{7,6},{8,9},{9,8},{10,11... | collective-permute-start | bytes 172040 | tf_op jit(solution)/shard_map/ppermute | solution.py:643
  46.3 5.8 %collective-permute-start.1 = (f32[56,256]{1,0:T(8,128)}, f32[56,256]{1,0:T(8,128)S(1)}, u32[]{:S(2)}, u32[]{:S(2)}) collective-permute-start(f32[56,256]{1,0:T(8,128)} %get-tuple-element.44), channel_id=1, source_target_pairs={{0,7},{1,2},{2,1},{3,4},{4,3},{5,6},{6,5},{7,0},{8,15},{9,10},{10,... | collective-permute-start | bytes 172040 | tf_op jit(solution)/shard_map/ppermute | solution.py:644
  52.1 4.4 %copy-start.1 = (f32[56,256]{1,0:T(8,128)}, f32[56,256]{1,0:T(8,128)S(1)}, u32[]{:S(2)}) copy-start(f32[56,256]{1,0:T(8,128)S(1)} %collective-permute-done.refs_2_) | copy-start | bytes 172036
  52.1 4.4 %copy-start.4 = (f32[56,256]{1,0:T(8,128)}, f32[56,256]{1,0:T(8,128)S(1)}, u32[]{:S(2)}) copy-start(f32[56,256]{1,0:T(8,128)S(1)} %collective-permute-done.1.refs_3_) | copy-start | bytes 172036
  60.2 16.5 %all-to-all-start.2 = ((f32[32,16,128]{2,1,0:T(8,128)}), f32[32,16,128]{2,1,0:T(8,128)}, u32[]{:S(2)}, u32[]{:S(2)}) async-start(f32[32,16,128]{2,1,0:T(8,128)} %get-tuple-element.51), calls=%async_computation.2 | async-start | bytes 524288 | tf_op jit(solution)/shard_map/all_to_all | solution.py:577
  66.6 5.9 %collective-permute-start.2 = (f32[56,256]{1,0:T(8,128)}, f32[56,256]{1,0:T(8,128)S(1)}, u32[]{:S(2)}, u32[]{:S(2)}) collective-permute-start(f32[56,256]{1,0:T(8,128)} %get-tuple-element.52), channel_id=1, source_target_pairs={{0,1},{1,0},{2,3},{3,2},{4,5},{5,4},{6,7},{7,6},{8,9},{9,8},{10,11... | collective-permute-start | bytes 172040 | tf_op jit(solution)/shard_map/ppermute | solution.py:643
  66.7 5.8 %collective-permute-start.3 = (f32[56,256]{1,0:T(8,128)}, f32[56,256]{1,0:T(8,128)S(1)}, u32[]{:S(2)}, u32[]{:S(2)}) collective-permute-start(f32[56,256]{1,0:T(8,128)} %get-tuple-element.53), channel_id=1, source_target_pairs={{0,7},{1,2},{2,1},{3,4},{4,3},{5,6},{6,5},{7,0},{8,15},{9,10},{10,... | collective-permute-start | bytes 172040 | tf_op jit(solution)/shard_map/ppermute | solution.py:644
  72.5 4.2 %copy-start.2 = (f32[56,256]{1,0:T(8,128)}, f32[56,256]{1,0:T(8,128)S(1)}, u32[]{:S(2)}) copy-start(f32[56,256]{1,0:T(8,128)S(1)} %collective-permute-done.2.refs_2_) | copy-start | bytes 172036
  72.5 4.2 %copy-start.5 = (f32[56,256]{1,0:T(8,128)}, f32[56,256]{1,0:T(8,128)S(1)}, u32[]{:S(2)}) copy-start(f32[56,256]{1,0:T(8,128)S(1)} %collective-permute-done.3.refs_3_) | copy-start | bytes 172036
  80.4 16.8 %all-to-all-start.3 = ((f32[32,16,128]{2,1,0:T(8,128)}), f32[32,16,128]{2,1,0:T(8,128)}, u32[]{:S(2)}, u32[]{:S(2)}) async-start(f32[32,16,128]{2,1,0:T(8,128)} %get-tuple-element.57), calls=%async_computation.3 | async-start | bytes 524288 | tf_op jit(solution)/shard_map/all_to_all | solution.py:577
  86.9 6.5 %collective-permute-start.4 = (f32[56,256]{1,0:T(8,128)}, f32[56,256]{1,0:T(8,128)S(1)}, u32[]{:S(2)}, u32[]{:S(2)}) collective-permute-start(f32[56,256]{1,0:T(8,128)} %get-tuple-element.58), channel_id=1, source_target_pairs={{0,1},{1,0},{2,3},{3,2},{4,5},{5,4},{6,7},{7,6},{8,9},{9,8},{10,11... | collective-permute-start | bytes 172040 | tf_op jit(solution)/shard_map/ppermute | solution.py:643
  87.0 6.4 %collective-permute-start.5 = (f32[56,256]{1,0:T(8,128)}, f32[56,256]{1,0:T(8,128)S(1)}, u32[]{:S(2)}, u32[]{:S(2)}) collective-permute-start(f32[56,256]{1,0:T(8,128)} %get-tuple-element.59), channel_id=1, source_target_pairs={{0,7},{1,2},{2,1},{3,4},{4,3},{5,6},{6,5},{7,0},{8,15},{9,10},{10,... | collective-permute-start | bytes 172040 | tf_op jit(solution)/shard_map/ppermute | solution.py:644
  93.4 3.8 %copy-start = (f32[56,256]{1,0:T(8,128)}, f32[56,256]{1,0:T(8,128)S(1)}, u32[]{:S(2)}) copy-start(f32[56,256]{1,0:T(8,128)S(1)} %collective-permute-done.4.refs_2_) | copy-start | bytes 172036
  93.4 3.8 %copy-start.3 = (f32[56,256]{1,0:T(8,128)}, f32[56,256]{1,0:T(8,128)S(1)}, u32[]{:S(2)}) copy-start(f32[56,256]{1,0:T(8,128)S(1)} %collective-permute-done.5.refs_3_) | copy-start | bytes 172036
  100.9 16.6 %all-to-all-start.4 = ((f32[32,16,128]{2,1,0:T(8,128)}), f32[32,16,128]{2,1,0:T(8,128)}, u32[]{:S(2)}, u32[]{:S(2)}) async-start(f32[32,16,128]{2,1,0:T(8,128)} %get-tuple-element.63), calls=%async_computation.4 | async-start | bytes 524288 | tf_op jit(solution)/shard_map/all_to_all | solution.py:577
  107.7 6.5 %collective-permute-start.6 = (f32[56,256]{1,0:T(8,128)}, f32[56,256]{1,0:T(8,128)S(1)}, u32[]{:S(2)}, u32[]{:S(2)}) collective-permute-start(f32[56,256]{1,0:T(8,128)} %get-tuple-element.64), channel_id=1, source_target_pairs={{0,1},{1,0},{2,3},{3,2},{4,5},{5,4},{6,7},{7,6},{8,9},{9,8},{10,11... | collective-permute-start | bytes 172040 | tf_op jit(solution)/shard_map/ppermute | solution.py:643
  107.8 6.4 %collective-permute-start.7 = (f32[56,256]{1,0:T(8,128)}, f32[56,256]{1,0:T(8,128)S(1)}, u32[]{:S(2)}, u32[]{:S(2)}) collective-permute-start(f32[56,256]{1,0:T(8,128)} %get-tuple-element.65), channel_id=1, source_target_pairs={{0,7},{1,2},{2,1},{3,4},{4,3},{5,6},{6,5},{7,0},{8,15},{9,10},{10,... | collective-permute-start | bytes 172040 | tf_op jit(solution)/shard_map/ppermute | solution.py:644
  114.2 3.3 %copy-start.6 = (f32[56,256]{1,0:T(8,128)}, f32[56,256]{1,0:T(8,128)S(1)}, u32[]{:S(2)}) copy-start(f32[56,256]{1,0:T(8,128)S(1)} %collective-permute-done.6.refs_2_) | copy-start | bytes 172036
  114.2 3.3 %copy-start.7 = (f32[56,256]{1,0:T(8,128)}, f32[56,256]{1,0:T(8,128)S(1)}, u32[]{:S(2)}) copy-start(f32[56,256]{1,0:T(8,128)S(1)} %collective-permute-done.7.refs_3_) | copy-start | bytes 172036

commit v5 on v4

--- a/solution.py
+++ b/solution.py
@@ -369,7 +369,8 @@
     high, low = two(jnp.concatenate(progress, axis=1))
     chemistry = jnp.dot(stoich[...], high, preferred_element_type=jnp.float32)
     chemistry = chemistry[:PAD] + chemistry[PAD:]
-    chemistry = chemistry + jnp.dot(stoich[:PAD, :], low, preferred_element_type=jnp.float32)
+    rest = jnp.dot(stoich[...], low, preferred_element_type=jnp.float32)
+    chemistry = chemistry + rest[:PAD]
     chemistry = jnp.concatenate([chemistry[:, :FACE], chemistry[:, FACE:]], axis=0)
     result[...] = (
         scale[:, 0:1] * field - scale[:, 1:2] * total - chemistry - scale[:, 2:3] * w[...]

time: 172 us -> 172 us (level)
  no operation moved by 1% of the time
where the time goes in v5:
time: 172 us; the launch traced here: 171 us
  starting transfers between devices  51 us (30%)
  blocking collectives  45.3 us (26%)
  Pallas kernels  39.3 us (23%)
  waiting for transfers between devices  22 us (13%)
  local copies, waits for them, and re-layouts  11.3 us (7%)
    pallas_call x13, Pallas kernels, call(): pl.pallas_call(kernel, out_shape=[jax.ShapeDtypeStruct(s[:-1], s[-1]) if...  39.3 us
    all_to_all x5, starting transfers between devices, exchange(): return lax.all_to_all(slots, 'grp', 0, 0, tiled=True)  37 us
    all_to_all x1, blocking collectives, exchange(): return lax.all_to_all(slots, 'grp', 0, 0, tiled=True)  22.8 us
    all_to_all x1, blocking collectives, on_device(): lines = lax.all_to_all(lines, ('grp', 'box'), 0, 0, tiled=True)  22.6 us
    all_to_all x5, waiting for transfers between devices, exchange(): return lax.all_to_all(slots, 'grp', 0, 0, tiled=True)  21.9 us
    ppermute x4, starting transfers between devices, on_device(): far_in = lax.ppermute(far, 'box', odd_swap)  13.6 us
    reshape x1, local copies, waits for them, and re-layouts, on_device(): inverse = precond.reshape(species, 2 * species, FACE)  7.02 us
  transfers between devices with their start and end apart: 13, of which 5 were waited for; matrix products, arithmetic and copies ran while one was open for 7% of the time, Pallas kernels for 7%

profile of v5, /device:TPU:2, one launch (start us, length us, event | category | flops | bytes accessed | tf_op | source)
XLA Modules:
  0.0 170.6 jit_solution(8972530486792918631)
XLA Ops:
  0.6 0.6 pad_add_fusion.1.ids
  1.2 3.8 %gather.1 = f32[32,40,128]{2,1,0:T(8,128)} custom-call(s32[3]{0:T(128)} %pad_add_fusion.1.ids, f32[53,1,256]{2,1,0:T(1,128)} %refs_2_.1, s32[32,1,160]{2,1,0:T(1,128)} %lists_out.1), custom_call_target="tpu_custom_call" | custom-call | tf_op jit(solution)/shard_map/gather/pallas_call | solution.py:71
  5.0 11.7 %all-to-all-start = ((f32[32,40,128]{2,1,0:T(8,128)}), f32[32,40,128]{2,1,0:T(8,128)}, u32[]{:S(2)}, u32[]{:S(2)}) async-start(f32[32,40,128]{2,1,0:T(8,128)} %gather.1), calls=%async_computation | async-start | bytes 1310720 | tf_op jit(solution)/shard_map/all_to_all | solution.py:578
  16.7 1.6 reshape.18.refs_2_
  18.3 2.0 %copy.22 = f32[325,1,2,256]{3,0,2,1:T(8,128)} copy(f32[325,1,2,256]{3,2,1,0:T(2,128)} %param.18) | data formatting | bytes 1331200 | tf_op args[4]
  20.3 7.0 %reshape.20.refs_5_.refs_7_ = bf16[53,106,256]{2,1,0:T(8,128)(2,1)} reshape(bf16[53,53,1,2,256]{4,3,2,1,0:T(2,128)(2,1)} %param.19) | data formatting | bytes 5752832 | tf_op jit(solution)/shard_map/reshape | solution.py:609
  27.3 0.0 copy-done.8
  27.3 0.0 copy-done.9
  27.3 0.0 copy-done.10
  27.4 0.6 pad.9.refs_0_.refs_2_
  28.0 1.9 %prepare.1 = (f32[112,128]{1,0:T(8,128)}, bf16[112,325]{1,0:T(8,128)(2,1)}, bf16[325,168]{1,0:T(8,128)(2,1)}, s32[8,128]{1,0:T(8,128)}) custom-call(s32[3]{0:T(128)} %pad_add_fusion.1.ids, s32[1,32]{1,0:T(1,128)} %bitcast.27, f32[1,53]{1,0:T(1,128)} %bitcast.30, f32[53,325]{1,0:T(8,128)} %stoich.1, f32[53,325]{1,0:T(8,128)} %bitcast.26), custom_call_target="tpu_custom_call" | custom-call | tf_op jit(solution)/shard_map/prepare/pallas_call | solution.py:71
  29.9 6.5 %all-to-all-done.refs_1_ = f32[32,40,128]{2,1,0:T(8,128)} async-done(((f32[32,40,128]{2,1,0:T(8,128)}), f32[32,40,128]{2,1,0:T(8,128)}, u32[]{:S(2)}, u32[]{:S(2)}) %all-to-all-start) | async-done | bytes 655392 | tf_op jit(solution)/shard_map/all_to_all | solution.py:578
  36.4 4.2 %first.1 = (f32[112,256]{1,0:T(8,128)}, f32[56,256]{1,0:T(8,128)}, f32[56,256]{1,0:T(8,128)}, f32[112,256]{1,0:T(8,128)}, f32[32,16,128]{2,1,0:T(8,128)}) custom-call(s32[8,128]{1,0:T(8,128)} %pad.9.refs_0_.refs_2_, f32[32,40,128]{2,1,0:T(8,128)} %all-to-all-done.refs_1_, f32[106,256]{1,0:T(8,128)} %reshape.18.refs_2_, ...), custom_call_target="tpu_custom_call" | custom-call | tf_op jit(solution)/shard_map/first/pallas_call | solution.py:71
  40.6 5.6 %all-to-all-start.1 = ((f32[32,16,128]{2,1,0:T(8,128)}), f32[32,16,128]{2,1,0:T(8,128)}, u32[]{:S(2)}, u32[]{:S(2)}) async-start(f32[32,16,128]{2,1,0:T(8,128)} %get-tuple-element.42), calls=%async_computation.1 | async-start | bytes 524288 | tf_op jit(solution)/shard_map/all_to_all | solution.py:578
  46.2 0.1 collective-permute-start
  46.3 3.1 %collective-permute-start.1 = (f32[56,256]{1,0:T(8,128)}, f32[56,256]{1,0:T(8,128)S(1)}, u32[]{:S(2)}, u32[]{:S(2)}) collective-permute-start(f32[56,256]{1,0:T(8,128)} %get-tuple-element.44), channel_id=1, source_target_pairs={{0,7},{1,2},{2,1},{3,4},{4,3},{5,6},{6,5},{7,0},{8,15},{9,10},{10,... | collective-permute-start | bytes 172040 | tf_op jit(solution)/shard_map/ppermute | solution.py:645
  49.4 2.6 %local0.1 = (f32[112,256]{1,0:T(8,128)}, f32[8,128]{1,0:T(8,128)}) custom-call(f32[112,256]{1,0:T(8,128)} %get-tuple-element.45.refs_0_.refs_4_, f32[112,256]{1,0:T(8,128)} %get-tuple-element.46.refs_1_.refs_7_, f32[112,128]{1,0:T(8,128)} %get-tuple-element.41.refs_3_.refs_2_.refs_5_.refs_1_, f32[256,256]{1,0:T(8,128)} %constant.22.clone.refs_3_, ...), custom_call_target="tpu_custom_call" | custom-call | tf_op jit(solution)/shard_map/local0/pallas_call | solution.py:71
  52.1 0.0 collective-permute-done.refs_2_
  52.1 0.0 copy-start.1
  52.1 0.0 collective-permute-done.1.refs_3_
  52.1 0.0 copy-start.4
  52.1 4.4 %all-to-all-done.1.refs_1_ = f32[32,16,128]{2,1,0:T(8,128)} async-done(((f32[32,16,128]{2,1,0:T(8,128)}), f32[32,16,128]{2,1,0:T(8,128)}, u32[]{:S(2)}, u32[]{:S(2)}) %all-to-all-start.1) | async-done | bytes 262176 | tf_op jit(solution)/shard_map/all_to_all | solution.py:578
  56.5 0.0 copy-done.1
  56.5 0.0 copy-done.4
  56.5 3.7 %combine0.1 = (f32[112,256]{1,0:T(8,128)}, f32[56,256]{1,0:T(8,128)}, f32[56,256]{1,0:T(8,128)}, f32[112,256]{1,0:T(8,128)}, f32[32,16,128]{2,1,0:T(8,128)}) custom-call(s32[8,128]{1,0:T(8,128)} %pad.9.refs_0_.refs_2_, f32[32,16,128]{2,1,0:T(8,128)} %all-to-all-done.1.refs_1_, f32[56,256]{1,0:T(8,128)} %copy-done.1, f32[56,256]{1,0:T(8,128)} %copy-done.4, ...), custom_call_target="tpu_custom_call" | custom-call | tf_op jit(solution)/shard_map/combine0/pallas_call | solution.py:71
  60.2 6.4 %all-to-all-start.2 = ((f32[32,16,128]{2,1,0:T(8,128)}), f32[32,16,128]{2,1,0:T(8,128)}, u32[]{:S(2)}, u32[]{:S(2)}) async-start(f32[32,16,128]{2,1,0:T(8,128)} %get-tuple-element.51), calls=%async_computation.2 | async-start | bytes 524288 | tf_op jit(solution)/shard_map/all_to_all | solution.py:578
  66.6 0.1 collective-permute-start.2
  66.7 3.1 %collective-permute-start.3 = (f32[56,256]{1,0:T(8,128)}, f32[56,256]{1,0:T(8,128)S(1)}, u32[]{:S(2)}, u32[]{:S(2)}) collective-permute-start(f32[56,256]{1,0:T(8,128)} %get-tuple-element.53), channel_id=1, source_target_pairs={{0,7},{1,2},{2,1},{3,4},{4,3},{5,6},{6,5},{7,0},{8,15},{9,10},{10,... | collective-permute-start | bytes 172040 | tf_op jit(solution)/shard_map/ppermute | solution.py:645
  69.8 2.6 %local1.1 = (f32[112,256]{1,0:T(8,128)}, f32[8,128]{1,0:T(8,128)}) custom-call(f32[112,256]{1,0:T(8,128)} %get-tuple-element.54.refs_0_.refs_5_, f32[112,256]{1,0:T(8,128)} %get-tuple-element.55.refs_1_.refs_8_, f32[112,128]{1,0:T(8,128)} %get-tuple-element.41.refs_3_.refs_2_.refs_5_.refs_1_, f32[256,256]{1,0:T(8,128)} %constant.22.clone.refs_3_, ...), custom_call_target="tpu_custom_call" | custom-call | tf_op jit(solution)/shard_map/local1/pallas_call | solution.py:71
  72.5 0.0 collective-permute-done.2.refs_2_
  72.5 0.0 copy-start.2
  72.5 0.0 collective-permute-done.3.refs_3_
  72.5 0.0 copy-start.5
  72.5 4.1 %all-to-all-done.2.refs_1_ = f32[32,16,128]{2,1,0:T(8,128)} async-done(((f32[32,16,128]{2,1,0:T(8,128)}), f32[32,16,128]{2,1,0:T(8,128)}, u32[]{:S(2)}, u32[]{:S(2)}) %all-to-all-start.2) | async-done | bytes 262176 | tf_op jit(solution)/shard_map/all_to_all | solution.py:578
  76.6 0.0 copy-done.2
  76.6 0.0 copy-done.5
  76.7 3.7 %combine1.1 = (f32[112,256]{1,0:T(8,128)}, f32[56,256]{1,0:T(8,128)}, f32[56,256]{1,0:T(8,128)}, f32[112,256]{1,0:T(8,128)}, f32[32,16,128]{2,1,0:T(8,128)}) custom-call(s32[8,128]{1,0:T(8,128)} %pad.9.refs_0_.refs_2_, f32[32,16,128]{2,1,0:T(8,128)} %all-to-all-done.2.refs_1_, f32[56,256]{1,0:T(8,128)} %copy-done.2, f32[56,256]{1,0:T(8,128)} %copy-done.5, ...), custom_call_target="tpu_custom_call" | custom-call | tf_op jit(solution)/shard_map/combine1/pallas_call | solution.py:71
  80.4 6.5 %all-to-all-start.3 = ((f32[32,16,128]{2,1,0:T(8,128)}), f32[32,16,128]{2,1,0:T(8,128)}, u32[]{:S(2)}, u32[]{:S(2)}) async-start(f32[32,16,128]{2,1,0:T(8,128)} %get-tuple-element.57), calls=%async_computation.3 | async-start | bytes 524288 | tf_op jit(solution)/shard_map/all_to_all | solution.py:578
  86.9 0.1 collective-permute-start.4
  87.0 3.7 %collective-permute-start.5 = (f32[56,256]{1,0:T(8,128)}, f32[56,256]{1,0:T(8,128)S(1)}, u32[]{:S(2)}, u32[]{:S(2)}) collective-permute-start(f32[56,256]{1,0:T(8,128)} %get-tuple-element.59), channel_id=1, source_target_pairs={{0,7},{1,2},{2,1},{3,4},{4,3},{5,6},{6,5},{7,0},{8,15},{9,10},{10,... | collective-permute-start | bytes 172040 | tf_op jit(solution)/shard_map/ppermute | solution.py:645
  90.7 2.7 %local2.1 = (f32[112,256]{1,0:T(8,128)}, f32[8,128]{1,0:T(8,128)}) custom-call(f32[112,256]{1,0:T(8,128)} %get-tuple-element.60.refs_0_.refs_6_, f32[112,256]{1,0:T(8,128)} %get-tuple-element.61.refs_1_.refs_9_, f32[112,128]{1,0:T(8,128)} %get-tuple-element.41.refs_3_.refs_2_.refs_5_.refs_1_, f32[256,256]{1,0:T(8,128)} %constant.22.clone.refs_3_, ...), custom_call_target="tpu_custom_call" | custom-call | tf_op jit(solution)/shard_map/local2/pallas_call | solution.py:71
  93.4 0.0 collective-permute-done.4.refs_2_
  93.4 0.0 copy-start
  93.4 0.0 collective-permute-done.5.refs_3_
  93.4 0.0 copy-start.3
  93.4 3.7 %all-to-all-done.3.refs_1_ = f32[32,16,128]{2,1,0:T(8,128)} async-done(((f32[32,16,128]{2,1,0:T(8,128)}), f32[32,16,128]{2,1,0:T(8,128)}, u32[]{:S(2)}, u32[]{:S(2)}) %all-to-all-start.3) | async-done | bytes 262176 | tf_op jit(solution)/shard_map/all_to_all | solution.py:578
  97.2 0.0 copy-done
  97.2 0.0 copy-done.3
  97.2 3.7 %combine2.1 = (f32[112,256]{1,0:T(8,128)}, f32[56,256]{1,0:T(8,128)}, f32[56,256]{1,0:T(8,128)}, f32[112,256]{1,0:T(8,128)}, f32[32,16,128]{2,1,0:T(8,128)}) custom-call(s32[8,128]{1,0:T(8,128)} %pad.9.refs_0_.refs_2_, f32[32,16,128]{2,1,0:T(8,128)} %all-to-all-done.3.refs_1_, f32[56,256]{1,0:T(8,128)} %copy-done, f32[56,256]{1,0:T(8,128)} %copy-done.3, ...), custom_call_target="tpu_custom_call" | custom-call | tf_op jit(solution)/shard_map/combine2/pallas_call | solution.py:71
  100.9 6.8 %all-to-all-start.4 = ((f32[32,16,128]{2,1,0:T(8,128)}), f32[32,16,128]{2,1,0:T(8,128)}, u32[]{:S(2)}, u32[]{:S(2)}) async-start(f32[32,16,128]{2,1,0:T(8,128)} %get-tuple-element.63), calls=%async_computation.4 | async-start | bytes 524288 | tf_op jit(solution)/shard_map/all_to_all | solution.py:578
  107.7 0.1 collective-permute-start.6
  107.8 3.6 %collective-permute-start.7 = (f32[56,256]{1,0:T(8,128)}, f32[56,256]{1,0:T(8,128)S(1)}, u32[]{:S(2)}, u32[]{:S(2)}) collective-permute-start(f32[56,256]{1,0:T(8,128)} %get-tuple-element.65), channel_id=1, source_target_pairs={{0,7},{1,2},{2,1},{3,4},{4,3},{5,6},{6,5},{7,0},{8,15},{9,10},{10,... | collective-permute-start | bytes 172040 | tf_op jit(solution)/shard_map/ppermute | solution.py:645
  111.5 2.7 %local3.1 = (f32[112,256]{1,0:T(8,128)}, f32[8,128]{1,0:T(8,128)}) custom-call(f32[112,256]{1,0:T(8,128)} %get-tuple-element.66.refs_0_.refs_7_, f32[112,256]{1,0:T(8,128)} %get-tuple-element.67.refs_1_.refs_10_, f32[112,128]{1,0:T(8,128)} %get-tuple-element.41.refs_3_.refs_2_.refs_5_.refs_1_, f32[256,256]{1,0:T(8,128)} %constant.22.clone.refs_3_, ...), custom_call_target="tpu_custom_call" | custom-call | tf_op jit(solution)/shard_map/local3/pallas_call | solution.py:71
  114.2 0.0 collective-permute-done.6.refs_2_
  114.2 0.0 copy-start.6
  114.2 0.0 collective-permute-done.7.refs_3_
  114.3 0.0 copy-start.7
  114.3 3.2 %all-to-all-done.4.refs_1_ = f32[32,16,128]{2,1,0:T(8,128)} async-done(((f32[32,16,128]{2,1,0:T(8,128)}), f32[32,16,128]{2,1,0:T(8,128)}, u32[]{:S(2)}, u32[]{:S(2)}) %all-to-all-start.4) | async-done | bytes 262176 | tf_op jit(solution)/shard_map/all_to_all | solution.py:578
  117.5 0.0 copy-done.7
  117.5 2.4 %last.1 = f32[256,128]{1,0:T(8,128)} custom-call(s32[8,128]{1,0:T(8,128)} %pad.9.refs_0_.refs_2_, f32[32,16,128]{2,1,0:T(8,128)} %all-to-all-done.4.refs_1_, f32[56,256]{1,0:T(8,128)} %copy-done.6, f32[56,256]{1,0:T(8,128)} %copy-done.7, f32[112,256]{1,0:T(8,128)} %get-tuple-element.68.refs_4_, f32[112,128]{1,0:T(8,128)} %get-tuple-element.41.refs_3_.refs_2_.refs_5_.refs_1_, ...), custom_call_target="tpu_custom_call" | custom-call | tf_op jit(solution)/shard_map/last/pallas_call | solution.py:71
  119.9 22.6 %all_to_all.41 = f32[256,1,128]{2,1,0:T(1,128)} all-to-all(f32[256,1,128]{2,1,0:T(1,128)} %bitcast.24), channel_id=1, replica_groups=mesh['grp'=32,'box'=8] {'grp','box'}, dimensions={0} | all-to-all | bytes 262144 | tf_op jit(solution)/shard_map/all_to_all | solution.py:687
  142.5 3.2 %finish.1 = (f32[53,2,256]{2,1,0:T(2,128)}, f32[32,32,128]{2,1,0:T(8,128)}) custom-call(f32[256,128]{1,0:T(8,128)} %bitcast.25, f32[112,128]{1,0:T(8,128)} %get-tuple-element.41.refs_3_.refs_2_.refs_5_.refs_1_, s32[8,128]{1,0:T(8,128)} %pad.9.refs_0_.refs_2_, f32[64,256]{1,0:T(8,128)} %constant.23.clone.refs_3_, ...), custom_call_target="tpu_custom_call" | custom-call | tf_op jit(solution)/shard_map/finish/pallas_call | solution.py:71
  145.6 22.8 %all_to_all.42.refs_1_ = f32[32,32,128]{2,1,0:T(8,128)} all-to-all(f32[32,32,128]{2,1,0:T(8,128)} %get-tuple-element.73), channel_id=1, replica_groups=mesh['grp'=32,'box'=8] {'grp'}, dimensions={0} | all-to-all | bytes 1048576 | tf_op jit(solution)/shard_map/all_to_all | solution.py:578
  168.4 2.0 %update.1 = f32[53,1,256]{2,1,0:T(1,128)} custom-call(s32[8,128]{1,0:T(8,128)} %get-tuple-element.76.refs_0_, f32[32,32,128]{2,1,0:T(8,128)} %all_to_all.42.refs_1_, f32[53,1,256]{2,1,0:T(1,128)} %refs_2_.1, f32[128,512]{1,0:T(8,128)} %constant.24.clone.refs_3_), custom_call_target="tpu_custom_call" | custom-call | tf_op jit(solution)/shard_map/update/pallas_call | solution.py:71
  (6 shorter events, 0.0 us)
Async XLA Ops:
  5.0 31.4 %all-to-all-start = ((f32[32,40,128]{2,1,0:T(8,128)}), f32[32,40,128]{2,1,0:T(8,128)}, u32[]{:S(2)}, u32[]{:S(2)}) async-start(f32[32,40,128]{2,1,0:T(8,128)} %gather.1), calls=%async_computation | async-start | bytes 1310720 | tf_op jit(solution)/shard_map/all_to_all | solution.py:578
  20.3 7.0 %copy-start.8 = (s32[3]{0:T(128)S(1)}, s32[3]{0:T(128)}, u32[]{:S(2)}) copy-start(s32[3]{0:T(128)} %pad_add_fusion.1.ids) | copy-start | bytes 40
  20.3 7.0 %copy-start.9 = (s32[32,1]{0,1:T(1,128)S(1)}, s32[32,1]{0,1:T(1,128)}, u32[]{:S(2)}) copy-start(s32[32,1]{0,1:T(1,128)} %param.23) | copy-start | bytes 388
  20.3 7.0 %copy-start.10 = (s32[32,4]{0,1:T(4,128)S(1)}, s32[32,4]{0,1:T(4,128)}, u32[]{:S(2)}) copy-start(s32[32,4]{0,1:T(4,128)} %param.21) | copy-start | bytes 1540
  40.6 15.9 %all-to-all-start.1 = ((f32[32,16,128]{2,1,0:T(8,128)}), f32[32,16,128]{2,1,0:T(8,128)}, u32[]{:S(2)}, u32[]{:S(2)}) async-start(f32[32,16,128]{2,1,0:T(8,128)} %get-tuple-element.42), calls=%async_computation.1 | async-start | bytes 524288 | tf_op jit(solution)/shard_map/all_to_all | solution.py:578
  46.2 5.9 %collective-permute-start = (f32[56,256]{1,0:T(8,128)}, f32[56,256]{1,0:T(8,128)S(1)}, u32[]{:S(2)}, u32[]{:S(2)}) collective-permute-start(f32[56,256]{1,0:T(8,128)} %get-tuple-element.43), channel_id=1, source_target_pairs={{0,1},{1,0},{2,3},{3,2},{4,5},{5,4},{6,7},{7,6},{8,9},{9,8},{10,11... | collective-permute-start | bytes 172040 | tf_op jit(solution)/shard_map/ppermute | solution.py:644
  46.3 5.8 %collective-permute-start.1 = (f32[56,256]{1,0:T(8,128)}, f32[56,256]{1,0:T(8,128)S(1)}, u32[]{:S(2)}, u32[]{:S(2)}) collective-permute-start(f32[56,256]{1,0:T(8,128)} %get-tuple-element.44), channel_id=1, source_target_pairs={{0,7},{1,2},{2,1},{3,4},{4,3},{5,6},{6,5},{7,0},{8,15},{9,10},{10,... | collective-permute-start | bytes 172040 | tf_op jit(solution)/shard_map/ppermute | solution.py:645
  52.1 4.4 %copy-start.1 = (f32[56,256]{1,0:T(8,128)}, f32[56,256]{1,0:T(8,128)S(1)}, u32[]{:S(2)}) copy-start(f32[56,256]{1,0:T(8,128)S(1)} %collective-permute-done.refs_2_) | copy-start | bytes 172036
  52.1 4.4 %copy-start.4 = (f32[56,256]{1,0:T(8,128)}, f32[56,256]{1,0:T(8,128)S(1)}, u32[]{:S(2)}) copy-start(f32[56,256]{1,0:T(8,128)S(1)} %collective-permute-done.1.refs_3_) | copy-start | bytes 172036
  60.2 16.4 %all-to-all-start.2 = ((f32[32,16,128]{2,1,0:T(8,128)}), f32[32,16,128]{2,1,0:T(8,128)}, u32[]{:S(2)}, u32[]{:S(2)}) async-start(f32[32,16,128]{2,1,0:T(8,128)} %get-tuple-element.51), calls=%async_computation.2 | async-start | bytes 524288 | tf_op jit(solution)/shard_map/all_to_all | solution.py:578
  66.6 5.9 %collective-permute-start.2 = (f32[56,256]{1,0:T(8,128)}, f32[56,256]{1,0:T(8,128)S(1)}, u32[]{:S(2)}, u32[]{:S(2)}) collective-permute-start(f32[56,256]{1,0:T(8,128)} %get-tuple-element.52), channel_id=1, source_target_pairs={{0,1},{1,0},{2,3},{3,2},{4,5},{5,4},{6,7},{7,6},{8,9},{9,8},{10,11... | collective-permute-start | bytes 172040 | tf_op jit(solution)/shard_map/ppermute | solution.py:644
  66.7 5.8 %collective-permute-start.3 = (f32[56,256]{1,0:T(8,128)}, f32[56,256]{1,0:T(8,128)S(1)}, u32[]{:S(2)}, u32[]{:S(2)}) collective-permute-start(f32[56,256]{1,0:T(8,128)} %get-tuple-element.53), channel_id=1, source_target_pairs={{0,7},{1,2},{2,1},{3,4},{4,3},{5,6},{6,5},{7,0},{8,15},{9,10},{10,... | collective-permute-start | bytes 172040 | tf_op jit(solution)/shard_map/ppermute | solution.py:645
  72.5 4.1 %copy-start.2 = (f32[56,256]{1,0:T(8,128)}, f32[56,256]{1,0:T(8,128)S(1)}, u32[]{:S(2)}) copy-start(f32[56,256]{1,0:T(8,128)S(1)} %collective-permute-done.2.refs_2_) | copy-start | bytes 172036
  72.5 4.1 %copy-start.5 = (f32[56,256]{1,0:T(8,128)}, f32[56,256]{1,0:T(8,128)S(1)}, u32[]{:S(2)}) copy-start(f32[56,256]{1,0:T(8,128)S(1)} %collective-permute-done.3.refs_3_) | copy-start | bytes 172036
  80.4 16.8 %all-to-all-start.3 = ((f32[32,16,128]{2,1,0:T(8,128)}), f32[32,16,128]{2,1,0:T(8,128)}, u32[]{:S(2)}, u32[]{:S(2)}) async-start(f32[32,16,128]{2,1,0:T(8,128)} %get-tuple-element.57), calls=%async_computation.3 | async-start | bytes 524288 | tf_op jit(solution)/shard_map/all_to_all | solution.py:578
  86.9 6.5 %collective-permute-start.4 = (f32[56,256]{1,0:T(8,128)}, f32[56,256]{1,0:T(8,128)S(1)}, u32[]{:S(2)}, u32[]{:S(2)}) collective-permute-start(f32[56,256]{1,0:T(8,128)} %get-tuple-element.58), channel_id=1, source_target_pairs={{0,1},{1,0},{2,3},{3,2},{4,5},{5,4},{6,7},{7,6},{8,9},{9,8},{10,11... | collective-permute-start | bytes 172040 | tf_op jit(solution)/shard_map/ppermute | solution.py:644
  87.0 6.4 %collective-permute-start.5 = (f32[56,256]{1,0:T(8,128)}, f32[56,256]{1,0:T(8,128)S(1)}, u32[]{:S(2)}, u32[]{:S(2)}) collective-permute-start(f32[56,256]{1,0:T(8,128)} %get-tuple-element.59), channel_id=1, source_target_pairs={{0,7},{1,2},{2,1},{3,4},{4,3},{5,6},{6,5},{7,0},{8,15},{9,10},{10,... | collective-permute-start | bytes 172040 | tf_op jit(solution)/shard_map/ppermute | solution.py:645
  93.4 3.8 %copy-start = (f32[56,256]{1,0:T(8,128)}, f32[56,256]{1,0:T(8,128)S(1)}, u32[]{:S(2)}) copy-start(f32[56,256]{1,0:T(8,128)S(1)} %collective-permute-done.4.refs_2_) | copy-start | bytes 172036
  93.4 3.8 %copy-start.3 = (f32[56,256]{1,0:T(8,128)}, f32[56,256]{1,0:T(8,128)S(1)}, u32[]{:S(2)}) copy-start(f32[56,256]{1,0:T(8,128)S(1)} %collective-permute-done.5.refs_3_) | copy-start | bytes 172036
  100.9 16.6 %all-to-all-start.4 = ((f32[32,16,128]{2,1,0:T(8,128)}), f32[32,16,128]{2,1,0:T(8,128)}, u32[]{:S(2)}, u32[]{:S(2)}) async-start(f32[32,16,128]{2,1,0:T(8,128)} %get-tuple-element.63), calls=%async_computation.4 | async-start | bytes 524288 | tf_op jit(solution)/shard_map/all_to_all | solution.py:578
  107.7 6.5 %collective-permute-start.6 = (f32[56,256]{1,0:T(8,128)}, f32[56,256]{1,0:T(8,128)S(1)}, u32[]{:S(2)}, u32[]{:S(2)}) collective-permute-start(f32[56,256]{1,0:T(8,128)} %get-tuple-element.64), channel_id=1, source_target_pairs={{0,1},{1,0},{2,3},{3,2},{4,5},{5,4},{6,7},{7,6},{8,9},{9,8},{10,11... | collective-permute-start | bytes 172040 | tf_op jit(solution)/shard_map/ppermute | solution.py:644
  107.8 6.4 %collective-permute-start.7 = (f32[56,256]{1,0:T(8,128)}, f32[56,256]{1,0:T(8,128)S(1)}, u32[]{:S(2)}, u32[]{:S(2)}) collective-permute-start(f32[56,256]{1,0:T(8,128)} %get-tuple-element.65), channel_id=1, source_target_pairs={{0,7},{1,2},{2,1},{3,4},{4,3},{5,6},{6,5},{7,0},{8,15},{9,10},{10,... | collective-permute-start | bytes 172040 | tf_op jit(solution)/shard_map/ppermute | solution.py:645
  114.2 3.3 %copy-start.6 = (f32[56,256]{1,0:T(8,128)}, f32[56,256]{1,0:T(8,128)S(1)}, u32[]{:S(2)}) copy-start(f32[56,256]{1,0:T(8,128)S(1)} %collective-permute-done.6.refs_2_) | copy-start | bytes 172036
  114.3 3.3 %copy-start.7 = (f32[56,256]{1,0:T(8,128)}, f32[56,256]{1,0:T(8,128)S(1)}, u32[]{:S(2)}) copy-start(f32[56,256]{1,0:T(8,128)S(1)} %collective-permute-done.7.refs_3_) | copy-start | bytes 172036
